TPU v7x, 32 devices: a whole 2x2x4 slice. The times are simulated.
32 devices in a mesh: groups: 2 (over y), leaf: 4 (over z), sub: 4 (over x, core).
Axes of the slice: x: 2, y: 2, z: 4, core: 2. Of those that a mesh axis runs over, the one named last changes fastest.
Arguments:
- rhs: bfloat16 [32, 65536], P(None, ('groups', 'leaf', 'sub')), parts along dimension 1, may hold values from -6 to 6
- bases: bfloat16 [256, 64, 256], P(('groups', 'leaf', 'sub')), parts along dimension 0, may hold values from -0.375 to 0.375
- near_blocks: bfloat16 [256, 3, 256, 256], P(('groups', 'leaf', 'sub')), parts along dimension 0, may hold values from -0.21875 to 0.21875
- transfer: bfloat16 [12, 2, 64, 64], replicated, may hold values from -0.75 to 0.75
- couple: bfloat16 [12, 4, 64, 64], replicated, may hold values from -0.4375 to 0.4375
- codes: int32 [12, 3, 128], replicated, may hold values from 0 to 4, as said below
Outputs:
- product: bfloat16 [32, 65536], P(None, ('groups', 'leaf', 'sub')), parts along dimension 1
There are 2 independent parts, one for each index of `groups`. A program takes and returns all parts, laid end to end along the dimension named above; an argument that names none is the same for every part. Nothing has to cross between parts.
Inputs may be any that keep to these rules, and one draw needn't show every extreme that they name: For a cluster c of level t (c < 128 / 2**t), codes[t, s, c] in 0 to 3 names the partner c-3, c-2, c+2, c+3 and 4 marks an empty slot; the partners named for one cluster differ; entries of larger c are not read.
All inputs are finite; a program needn't handle non-finite values.
Results may differ from a plain program's by a relative error of at most 0.0044.
Values may be sent and summed in bfloat16 or wider, within the bound.
No kernel may reach another device: no remote copies, remote signals or barrier semaphores. Data moves between devices by JAX's collectives and lax.ppermute only.
A program may use at most 64 MiB of HBM per device.

v0:
```python
import jax
import jax.numpy as jnp
from jax import lax
from jax.sharding import PartitionSpec as P

ROOT_HALF = 0.7071067811865476
OFFSETS = (-3, -2, 2, 3)


def passed_along(x, axis, by):
    devices = lax.axis_size(axis)
    pairs = [(i, i + by) for i in range(devices) if 0 <= i + by < devices]
    return lax.ppermute(x, axis, pairs)


def swapped(block, axis, apart):
    count = lax.axis_size(axis)
    route = []
    for low in range(count):
        high = low | 1 << apart
        if high != low and high < count:
            route += [(low, high), (high, low)]
    return lax.ppermute(block, axis, route)


def with_halo(x, sides, width):
    for axis, dim in sides:
        devices, length = (lax.axis_size(axis), x.shape[dim])
        up = [(i, (i + 1) % devices) for i in range(devices - 1)]
        down = [(j, i) for i, j in up]
        last = lax.slice_in_dim(x, length - width, length, axis=dim)
        leading = lax.slice_in_dim(x, 0, width, axis=dim)
        before = lax.ppermute(last, axis, up)
        after = lax.ppermute(leading, axis, down)
        x = jnp.concatenate([before, x, after], axis=dim)
    return x


def forward_map(coef, matrix):
    return jnp.einsum("crk,kj->crj", coef, matrix, precision=lax.Precision.HIGHEST)


def backward_map(coef, matrix):
    return jnp.einsum("crj,kj->crk", coef, matrix, precision=lax.Precision.HIGHEST)


def merge_pairs(coef, tables, level):
    return (
        forward_map(coef[0::2], tables[level, 0]) + forward_map(coef[1::2], tables[level, 1])
    ) * ROOT_HALF


def split_pairs(coef, tables, level):
    left_part = backward_map(coef, tables[level, 0])
    right_part = backward_map(coef, tables[level, 1])
    return jnp.stack([left_part, right_part], axis=1).reshape((2 * coef.shape[0],) + coef.shape[1:])


def apply_couplings(extended, anchor, count, level_codes, table):
    total = jnp.zeros((count,) + extended.shape[1:], jnp.float32)
    for index, offset in enumerate(OFFSETS):
        window = lax.slice_in_dim(extended, anchor + offset, anchor + offset + count, axis=0)
        weight = jnp.sum((level_codes == index).astype(jnp.float32), axis=0)
        total = total + forward_map(window * weight[:, None, None], table[index])
    return total


def couple_remote(level_coef, level_codes, table, stride):
    count = level_coef.shape[0]
    needed = sorted({(slot + offset) // count for slot in range(count) for offset in OFFSETS} - {0})
    lowest = min(needed + [0])
    highest = max(needed + [0])
    pieces = []
    for step in range(lowest, highest + 1):
        if step == 0:
            pieces.append(level_coef)
        elif step in needed:
            pieces.append(passed_along(level_coef, ("leaf", "sub"), -step * stride))
        else:
            pieces.append(jnp.zeros_like(level_coef))
    extended = jnp.concatenate(pieces, axis=0)
    return apply_couplings(extended, -lowest * count, count, level_codes, table)


def shards(rhs, bases, near_blocks, transfer, couple, codes):
    rhs_count = rhs.shape[0]
    leaf_count, rank_width, leaf_size = bases.shape
    devices = lax.axis_size(("leaf", "sub"))
    position = lax.axis_index(("leaf", "sub"))
    local_bits = leaf_count.bit_length() - 1
    dist_bits = devices.bit_length() - 1
    tables = transfer.astype(jnp.float32)
    links = couple.astype(jnp.float32)
    leaf_rhs = rhs.reshape(rhs_count, leaf_count, leaf_size)
    coef = jnp.einsum("rlm,lkm->lrk", leaf_rhs, bases, preferred_element_type=jnp.float32)
    upward = [coef]
    for level in range(local_bits):
        upward.append(merge_pairs(upward[-1], tables, level))
    fields = []
    for level in range(local_bits):
        count = upward[level].shape[0]
        level_codes = lax.dynamic_slice_in_dim(codes[level], position * count, count, 1)
        fields.append(couple_remote(upward[level], level_codes, links[level], 1))
    own = upward[-1]
    chain = [own]
    for bit in range(dist_bits):
        level = local_bits + bit
        other = swapped(chain[-1], ("leaf", "sub"), bit)
        first = position // 2**bit % 2 == 0
        left_coef = jnp.where(first, chain[-1], other)
        right_coef = jnp.where(first, other, chain[-1])
        chain.append(
            (forward_map(left_coef, tables[level, 0]) + forward_map(right_coef, tables[level, 1]))
            * ROOT_HALF
        )
    couplings = []
    for bit in range(dist_bits + 1):
        level = local_bits + bit
        stride = 2**bit
        if devices // stride >= 4:
            level_codes = lax.dynamic_slice_in_dim(codes[level], position // stride, 1, 1)
            couplings.append(couple_remote(chain[bit], level_codes, links[level], stride))
        else:
            couplings.append(jnp.zeros_like(own))
    state = couplings[dist_bits]
    for bit in reversed(range(dist_bits)):
        level = local_bits + bit
        first = position // 2**bit % 2 == 0
        matrix = jnp.where(first, tables[level, 0], tables[level, 1])
        state = couplings[bit] + backward_map(state, matrix)
    for level in reversed(range(local_bits)):
        state = fields[level] + split_pairs(state, tables, level)
    leaf_coef = state.astype(jnp.bfloat16)
    total = jnp.einsum("lrk,lkm->rlm", leaf_coef, bases, preferred_element_type=jnp.float32)
    widened = with_halo(leaf_rhs, ((("leaf", "sub"), 1),), 1)
    for shift_index in range(3):
        total = total + jnp.einsum(
            "rlm,lnm->rln",
            widened[:, shift_index : shift_index + leaf_count],
            near_blocks[:, shift_index],
            preferred_element_type=jnp.float32,
        )
    return total.reshape(rhs_count, leaf_count * leaf_size).astype(jnp.bfloat16)


def solution(mesh):
    return jax.shard_map(
        shards,
        mesh=mesh,
        in_specs=(
            P(None, ("groups", "leaf", "sub")),
            P(("groups", "leaf", "sub"), None, None),
            P(("groups", "leaf", "sub"), None, None, None),
            P(),
            P(),
            P(),
        ),
        out_specs=P(None, ("groups", "leaf", "sub")),
        check_vma=False,
    )
```

profile of v0, /device:TPU:24, one launch (start us, length us, event | category | flops | bytes accessed | tf_op | source)
XLA Modules:
  0.0 123.6 jit_solution(3711454109395281831)
XLA Ops:
  0.0 0.9 copy-done
  1.0 1.1 fusion.269
  2.0 0.9 fusion.67
  2.9 0.9 fusion.8
  3.8 0.9 fusion.101
  4.7 0.9 fusion.12
  5.6 0.8 fusion.107
  6.4 0.9 fusion.27
  7.3 2.4 %collective-permute-start.11 = (f32[1,32,64]{2,1,0:T(8,128)S(1)}, f32[1,32,64]{2,1,0:T(8,128)S(1)}, u32[]{:S(2)}, u32[]{:S(2)}) collective-permute-start(f32[1,32,64]{2,1,0:T(8,128)S(1)} %fusion.27), channel_id=1, source_target_pairs={{3,0},{4,1},{5,2},{6,3},{7,4},{8,5},{9,6},{10,7},{11,8},{12,9},{13... | collective-permute-start | bytes 24584 | tf_op jit(solution)/shard_map/ppermute | solution.py:13
  9.8 3.3 %collective-permute-start.10 = (f32[1,32,64]{2,1,0:T(8,128)S(1)}, f32[1,32,64]{2,1,0:T(8,128)S(1)}, u32[]{:S(2)}, u32[]{:S(2)}) collective-permute-start(f32[1,32,64]{2,1,0:T(8,128)S(1)} %fusion.27), channel_id=1, source_target_pairs={{2,0},{3,1},{4,2},{5,3},{6,4},{7,5},{8,6},{9,7},{10,8},{11,9},{12,... | collective-permute-start | bytes 24584 | tf_op jit(solution)/shard_map/ppermute | solution.py:13
  13.1 2.6 %collective-permute-start.9 = (f32[1,32,64]{2,1,0:T(8,128)S(1)}, f32[1,32,64]{2,1,0:T(8,128)S(1)}, u32[]{:S(2)}, u32[]{:S(2)}) collective-permute-start(f32[1,32,64]{2,1,0:T(8,128)S(1)} %fusion.27), channel_id=1, source_target_pairs={{0,2},{1,3},{2,4},{3,5},{4,6},{5,7},{6,8},{7,9},{8,10},{9,11},{10,... | collective-permute-start | bytes 24584 | tf_op jit(solution)/shard_map/ppermute | solution.py:13
  15.7 1.9 %collective-permute-start.8 = (f32[1,32,64]{2,1,0:T(8,128)S(1)}, f32[1,32,64]{2,1,0:T(8,128)S(1)}, u32[]{:S(2)}, u32[]{:S(2)}) collective-permute-start(f32[1,32,64]{2,1,0:T(8,128)S(1)} %fusion.27), channel_id=1, source_target_pairs={{0,3},{1,4},{2,5},{3,6},{4,7},{5,8},{6,9},{7,10},{8,11},{9,12},{10... | collective-permute-start | bytes 24584 | tf_op jit(solution)/shard_map/ppermute | solution.py:13
  17.6 1.1 convert_element_type.229
  18.7 0.9 copy.31
  20.0 0.8 fusion.271
  20.8 0.8 convert_reduce_fusion.7
  21.5 0.7 convert_reduce_fusion.3
  22.3 0.8 convert_reduce_fusion.11
  23.3 3.3 %collective-permute-start.6 = (f32[2,32,64]{2,1,0:T(8,128)S(1)}, f32[2,32,64]{2,1,0:T(8,128)S(1)}, u32[]{:S(2)}, u32[]{:S(2)}) collective-permute-start(f32[2,32,64]{2,1,0:T(8,128)S(1)} %fusion.12), channel_id=1, source_target_pairs={{1,0},{2,1},{3,2},{4,3},{5,4},{6,5},{7,6},{8,7},{9,8},{10,9},{11,1... | collective-permute-start | bytes 49160 | tf_op jit(solution)/shard_map/ppermute | solution.py:13
  26.6 0.8 fusion.155
  27.5 3.7 %collective-permute-start.7 = (f32[2,32,64]{2,1,0:T(8,128)S(1)}, f32[2,32,64]{2,1,0:T(8,128)S(1)}, u32[]{:S(2)}, u32[]{:S(2)}) collective-permute-start(f32[2,32,64]{2,1,0:T(8,128)S(1)} %fusion.12), channel_id=1, source_target_pairs={{2,0},{3,1},{4,2},{5,3},{6,4},{7,5},{8,6},{9,7},{10,8},{11,9},{12,... | collective-permute-start | bytes 49160 | tf_op jit(solution)/shard_map/ppermute | solution.py:13
  31.2 0.7 fusion.160
  31.9 1.9 %collective-permute-start.5 = (f32[2,32,64]{2,1,0:T(8,128)S(1)}, f32[2,32,64]{2,1,0:T(8,128)S(1)}, u32[]{:S(2)}, u32[]{:S(2)}) collective-permute-start(f32[2,32,64]{2,1,0:T(8,128)S(1)} %fusion.12), channel_id=1, source_target_pairs={{0,1},{1,2},{2,3},{3,4},{4,5},{5,6},{6,7},{7,8},{8,9},{9,10},{10,1... | collective-permute-start | bytes 49160 | tf_op jit(solution)/shard_map/ppermute | solution.py:13
  33.9 0.8 fusion.163
  34.7 2.2 %collective-permute-start.4 = (f32[2,32,64]{2,1,0:T(8,128)S(1)}, f32[2,32,64]{2,1,0:T(8,128)S(1)}, u32[]{:S(2)}, u32[]{:S(2)}) collective-permute-start(f32[2,32,64]{2,1,0:T(8,128)S(1)} %fusion.12), channel_id=1, source_target_pairs={{0,2},{1,3},{2,4},{3,5},{4,6},{5,7},{6,8},{7,9},{8,10},{9,11},{10,... | collective-permute-start | bytes 49160 | tf_op jit(solution)/shard_map/ppermute | solution.py:13
  36.9 0.7 fusion.166
  37.5 0.9 fusion.22
  38.7 3.5 %collective-permute-done.17 = f32[1,32,64]{2,1,0:T(8,128)S(1)} collective-permute-done((f32[1,32,64]{2,1,0:T(8,128)S(1)}, f32[1,32,64]{2,1,0:T(8,128)S(1)}, u32[]{:S(2)}, u32[]{:S(2)}) %collective-permute-start.17) | collective-permute-done | bytes 8224 | tf_op jit(solution)/shard_map/ppermute | solution.py:23
  42.2 1.9 %collective-permute-start.2 = (f32[4,32,64]{2,1,0:T(8,128)S(1)}, f32[4,32,64]{2,1,0:T(8,128)S(1)}, u32[]{:S(2)}, u32[]{:S(2)}) collective-permute-start(f32[4,32,64]{2,1,0:T(8,128)S(1)} %fusion.8), channel_id=1, source_target_pairs={{0,1},{1,2},{2,3},{3,4},{4,5},{5,6},{6,7},{7,8},{8,9},{9,10},{10,1... | collective-permute-start | bytes 98312 | tf_op jit(solution)/shard_map/ppermute | solution.py:13
  44.1 0.8 fusion.139
  45.0 1.3 %collective-permute-start.14 = (f32[1,32,64]{2,1,0:T(8,128)S(1)}, f32[1,32,64]{2,1,0:T(8,128)S(1)}, u32[]{:S(2)}, u32[]{:S(2)}) collective-permute-start(f32[1,32,64]{2,1,0:T(8,128)S(1)} %fusion.22), channel_id=1, source_target_pairs={{0,4},{1,5},{2,6},{3,7},{4,8},{5,9},{6,10},{7,11},{8,12},{9,13},{1... | collective-permute-start | bytes 24584 | tf_op jit(solution)/shard_map/ppermute | solution.py:13
  46.5 4.8 %collective-permute-done.14 = f32[1,32,64]{2,1,0:T(8,128)S(1)} collective-permute-done((f32[1,32,64]{2,1,0:T(8,128)S(1)}, f32[1,32,64]{2,1,0:T(8,128)S(1)}, u32[]{:S(2)}, u32[]{:S(2)}) %collective-permute-start.14) | collective-permute-done | bytes 8224 | tf_op jit(solution)/shard_map/ppermute | solution.py:13
  51.3 3.8 %collective-permute-start.15 = (f32[1,32,64]{2,1,0:T(8,128)S(1)}, f32[1,32,64]{2,1,0:T(8,128)S(1)}, u32[]{:S(2)}, u32[]{:S(2)}) collective-permute-start(f32[1,32,64]{2,1,0:T(8,128)S(1)} %fusion.22), channel_id=1, source_target_pairs={{4,0},{5,1},{6,2},{7,3},{8,4},{9,5},{10,6},{11,7},{12,8},{13,9},{1... | collective-permute-start | bytes 24584 | tf_op jit(solution)/shard_map/ppermute | solution.py:13
  55.8 0.7 collective-permute-done.15
  56.5 2.9 %collective-permute-start.3 = (f32[4,32,64]{2,1,0:T(8,128)S(1)}, f32[4,32,64]{2,1,0:T(8,128)S(1)}, u32[]{:S(2)}, u32[]{:S(2)}) collective-permute-start(f32[4,32,64]{2,1,0:T(8,128)S(1)} %fusion.8), channel_id=1, source_target_pairs={{1,0},{2,1},{3,2},{4,3},{5,4},{6,5},{7,6},{8,7},{9,8},{10,9},{11,1... | collective-permute-start | bytes 98312 | tf_op jit(solution)/shard_map/ppermute | solution.py:13
  59.4 0.8 fusion.147
  60.2 4.5 %collective-permute-start.16 = (f32[1,32,64]{2,1,0:T(8,128)S(1)}, f32[1,32,64]{2,1,0:T(8,128)S(1)}, u32[]{:S(2)}, u32[]{:S(2)}) collective-permute-start(f32[1,32,64]{2,1,0:T(8,128)S(1)} %fusion.22), channel_id=1, source_target_pairs={{6,0},{7,1},{8,2},{9,3},{10,4},{11,5},{12,6},{13,7},{14,8},{15,9},... | collective-permute-start | bytes 24584 | tf_op jit(solution)/shard_map/ppermute | solution.py:13
  64.9 0.9 fusion.17
  66.1 1.3 %collective-permute-start.19 = (f32[1,32,64]{2,1,0:T(8,128)S(1)}, f32[1,32,64]{2,1,0:T(8,128)S(1)}, u32[]{:S(2)}, u32[]{:S(2)}) collective-permute-start(f32[1,32,64]{2,1,0:T(8,128)S(1)} %fusion.17), channel_id=1, source_target_pairs={{0,8},{1,9},{2,10},{3,11},{4,12},{5,13},{6,14},{7,15},{16,24},{17,... | collective-permute-start | bytes 24584 | tf_op jit(solution)/shard_map/ppermute | solution.py:13
  67.4 0.8 fusion.144
  68.2 4.6 %collective-permute-done.19 = f32[1,32,64]{2,1,0:T(8,128)S(1)} collective-permute-done((f32[1,32,64]{2,1,0:T(8,128)S(1)}, f32[1,32,64]{2,1,0:T(8,128)S(1)}, u32[]{:S(2)}, u32[]{:S(2)}) %collective-permute-start.19) | collective-permute-done | bytes 8224 | tf_op jit(solution)/shard_map/ppermute | solution.py:13
  72.8 1.5 %collective-permute-start.20 = (f32[1,32,64]{2,1,0:T(8,128)S(1)}, f32[1,32,64]{2,1,0:T(8,128)S(1)}, u32[]{:S(2)}, u32[]{:S(2)}) collective-permute-start(f32[1,32,64]{2,1,0:T(8,128)S(1)} %fusion.17), channel_id=1, source_target_pairs={{8,0},{9,1},{10,2},{11,3},{12,4},{13,5},{14,6},{15,7},{24,16},{25,... | collective-permute-start | bytes 24584 | tf_op jit(solution)/shard_map/ppermute | solution.py:13
  74.3 0.7 fusion.134
  75.0 0.7 collective-permute-done.20
  75.7 7.0 %collective-permute-start.21 = (f32[1,32,64]{2,1,0:T(8,128)S(1)}, f32[1,32,64]{2,1,0:T(8,128)S(1)}, u32[]{:S(2)}, u32[]{:S(2)}) collective-permute-start(f32[1,32,64]{2,1,0:T(8,128)S(1)} %fusion.17), channel_id=1, source_target_pairs={{12,0},{13,1},{14,2},{15,3},{28,16},{29,17},{30,18},{31,19}} | collective-permute-start | bytes 24584 | tf_op jit(solution)/shard_map/ppermute | solution.py:13
  82.8 0.7 fusion.131
  83.5 0.7 collective-permute-done.21
  84.2 1.3 %collective-permute-start.18 = (f32[1,32,64]{2,1,0:T(8,128)S(1)}, f32[1,32,64]{2,1,0:T(8,128)S(1)}, u32[]{:S(2)}, u32[]{:S(2)}) collective-permute-start(f32[1,32,64]{2,1,0:T(8,128)S(1)} %fusion.17), channel_id=1, source_target_pairs={{0,12},{1,13},{2,14},{3,15},{16,28},{17,29},{18,30},{19,31}} | collective-permute-start | bytes 24584 | tf_op jit(solution)/shard_map/ppermute | solution.py:13
  86.1 5.5 %collective-permute-done.18 = f32[1,32,64]{2,1,0:T(8,128)S(1)} collective-permute-done((f32[1,32,64]{2,1,0:T(8,128)S(1)}, f32[1,32,64]{2,1,0:T(8,128)S(1)}, u32[]{:S(2)}, u32[]{:S(2)}) %collective-permute-start.18) | collective-permute-done | bytes 8224 | tf_op jit(solution)/shard_map/ppermute | solution.py:13
  91.6 1.3 %collective-permute-start.13 = (f32[1,32,64]{2,1,0:T(8,128)S(1)}, f32[1,32,64]{2,1,0:T(8,128)S(1)}, u32[]{:S(2)}, u32[]{:S(2)}) collective-permute-start(f32[1,32,64]{2,1,0:T(8,128)S(1)} %fusion.22), channel_id=1, source_target_pairs={{0,6},{1,7},{2,8},{3,9},{4,10},{5,11},{6,12},{7,13},{8,14},{9,15},... | collective-permute-start | bytes 24584 | tf_op jit(solution)/shard_map/ppermute | solution.py:13
  92.9 0.8 fusion.15
  93.8 5.2 %collective-permute-done.13 = f32[1,32,64]{2,1,0:T(8,128)S(1)} collective-permute-done((f32[1,32,64]{2,1,0:T(8,128)S(1)}, f32[1,32,64]{2,1,0:T(8,128)S(1)}, u32[]{:S(2)}, u32[]{:S(2)}) %collective-permute-start.13) | collective-permute-done | bytes 8224 | tf_op jit(solution)/shard_map/ppermute | solution.py:13
  99.0 1.9 %collective-permute-start = (f32[8,32,64]{2,1,0:T(8,128)S(1)}, f32[8,32,64]{2,1,0:T(8,128)S(1)}, u32[]{:S(2)}, u32[]{:S(2)}) collective-permute-start(f32[8,32,64]{2,1,0:T(8,128)S(1)} %fusion.269), channel_id=1, source_target_pairs={{0,1},{1,2},{2,3},{3,4},{4,5},{5,6},{6,7},{7,8},{8,9},{9,10},{10,1... | collective-permute-start | bytes 196616 | tf_op jit(solution)/shard_map/ppermute | solution.py:13
  100.9 0.8 fusion.20
  101.9 4.5 %collective-permute-start.1 = (f32[8,32,64]{2,1,0:T(8,128)S(1)}, f32[8,32,64]{2,1,0:T(8,128)S(1)}, u32[]{:S(2)}, u32[]{:S(2)}) collective-permute-start(f32[8,32,64]{2,1,0:T(8,128)S(1)} %fusion.269), channel_id=1, source_target_pairs={{1,0},{2,1},{3,2},{4,3},{5,4},{6,5},{7,6},{8,7},{9,8},{10,9},{11,1... | collective-permute-start | bytes 196616 | tf_op jit(solution)/shard_map/ppermute | solution.py:13
  106.5 0.8 fusion.25
  107.3 0.8 convolution_bitcast_fusion.6
  108.2 0.9 convolution_bitcast_fusion.7
  109.1 1.9 %collective-permute-start.22 = (bf16[32,1,256]{2,0,1:T(8,128)(2,1)S(1)}, bf16[32,1,256]{2,0,1:T(8,128)(2,1)S(1)}, u32[]{:S(2)}, u32[]{:S(2)}) collective-permute-start(bf16[32,1,256]{2,0,1:T(8,128)(2,1)S(1)} %get-tuple-element.30), channel_id=1, source_target_pairs={{0,1},{1,2},{2,3},{3,4},{4,5},{5,6},{6,7},{7,8},{8,9},{9,10},{10,1... | collective-permute-start | bytes 49160 | tf_op jit(solution)/shard_map/ppermute | solution.py:33
  111.2 0.9 convolution_bitcast_fusion.4
  112.1 0.9 convolution_bitcast_fusion.5
  113.0 4.5 %collective-permute-start.23 = (bf16[32,1,256]{2,0,1:T(8,128)(2,1)S(1)}, bf16[32,1,256]{2,0,1:T(8,128)(2,1)S(1)}, u32[]{:S(2)}, u32[]{:S(2)}) collective-permute-start(bf16[32,1,256]{2,0,1:T(8,128)(2,1)S(1)} %get-tuple-element.29), channel_id=1, source_target_pairs={{1,0},{2,1},{3,2},{4,3},{5,4},{6,5},{7,6},{8,7},{9,8},{10,9},{11,1... | collective-permute-start | bytes 49160 | tf_op jit(solution)/shard_map/ppermute | solution.py:34
  118.6 0.9 convolution_bitcast_fusion.2
  119.5 0.9 convolution_bitcast_fusion.3
  (56 shorter events, 7.8 us)
Async XLA Ops:
  0.0 1.0 copy-start
  0.0 31.2 %copy-start.2 = (bf16[12,4,64,64]{3,2,1,0:T(8,128)(2,1)S(1)}, bf16[12,4,64,64]{3,2,1,0:T(8,128)(2,1)}, u32[]{:S(2)}) copy-start(bf16[12,4,64,64]{3,2,1,0:T(8,128)(2,1)} %param.10) | copy-start | bytes 1179652
  7.3 16.0 %collective-permute-start.12 = (f32[1,32,64]{2,1,0:T(8,128)S(1)}, f32[1,32,64]{2,1,0:T(8,128)S(1)}, u32[]{:S(2)}, u32[]{:S(2)}) collective-permute-start(f32[1,32,64]{2,1,0:T(8,128)S(1)} %fusion.27), channel_id=1, source_target_pairs={{0,1},{1,0},{2,3},{3,2},{4,5},{5,4},{6,7},{7,6},{8,9},{9,8},{10,11... | collective-permute-start | bytes 24584 | tf_op jit(solution)/shard_map/ppermute | solution.py:23
  7.3 20.1 %collective-permute-start.11 = (f32[1,32,64]{2,1,0:T(8,128)S(1)}, f32[1,32,64]{2,1,0:T(8,128)S(1)}, u32[]{:S(2)}, u32[]{:S(2)}) collective-permute-start(f32[1,32,64]{2,1,0:T(8,128)S(1)} %fusion.27), channel_id=1, source_target_pairs={{3,0},{4,1},{5,2},{6,3},{7,4},{8,5},{9,6},{10,7},{11,8},{12,9},{13... | collective-permute-start | bytes 24584 | tf_op jit(solution)/shard_map/ppermute | solution.py:13
  9.8 22.1 %collective-permute-start.10 = (f32[1,32,64]{2,1,0:T(8,128)S(1)}, f32[1,32,64]{2,1,0:T(8,128)S(1)}, u32[]{:S(2)}, u32[]{:S(2)}) collective-permute-start(f32[1,32,64]{2,1,0:T(8,128)S(1)} %fusion.27), channel_id=1, source_target_pairs={{2,0},{3,1},{4,2},{5,3},{6,4},{7,5},{8,6},{9,7},{10,8},{11,9},{12,... | collective-permute-start | bytes 24584 | tf_op jit(solution)/shard_map/ppermute | solution.py:13
  13.1 21.6 %collective-permute-start.9 = (f32[1,32,64]{2,1,0:T(8,128)S(1)}, f32[1,32,64]{2,1,0:T(8,128)S(1)}, u32[]{:S(2)}, u32[]{:S(2)}) collective-permute-start(f32[1,32,64]{2,1,0:T(8,128)S(1)} %fusion.27), channel_id=1, source_target_pairs={{0,2},{1,3},{2,4},{3,5},{4,6},{5,7},{6,8},{7,9},{8,10},{9,11},{10,... | collective-permute-start | bytes 24584 | tf_op jit(solution)/shard_map/ppermute | solution.py:13
  15.7 86.3 %collective-permute-start.8 = (f32[1,32,64]{2,1,0:T(8,128)S(1)}, f32[1,32,64]{2,1,0:T(8,128)S(1)}, u32[]{:S(2)}, u32[]{:S(2)}) collective-permute-start(f32[1,32,64]{2,1,0:T(8,128)S(1)} %fusion.27), channel_id=1, source_target_pairs={{0,3},{1,4},{2,5},{3,6},{4,7},{5,8},{6,9},{7,10},{8,11},{9,12},{10... | collective-permute-start | bytes 24584 | tf_op jit(solution)/shard_map/ppermute | solution.py:13
  23.3 15.1 %collective-permute-start.6 = (f32[2,32,64]{2,1,0:T(8,128)S(1)}, f32[2,32,64]{2,1,0:T(8,128)S(1)}, u32[]{:S(2)}, u32[]{:S(2)}) collective-permute-start(f32[2,32,64]{2,1,0:T(8,128)S(1)} %fusion.12), channel_id=1, source_target_pairs={{1,0},{2,1},{3,2},{4,3},{5,4},{6,5},{7,6},{8,7},{9,8},{10,9},{11,1... | collective-permute-start | bytes 49160 | tf_op jit(solution)/shard_map/ppermute | solution.py:13
  27.5 17.5 %collective-permute-start.7 = (f32[2,32,64]{2,1,0:T(8,128)S(1)}, f32[2,32,64]{2,1,0:T(8,128)S(1)}, u32[]{:S(2)}, u32[]{:S(2)}) collective-permute-start(f32[2,32,64]{2,1,0:T(8,128)S(1)} %fusion.12), channel_id=1, source_target_pairs={{2,0},{3,1},{4,2},{5,3},{6,4},{7,5},{8,6},{9,7},{10,8},{11,9},{12,... | collective-permute-start | bytes 49160 | tf_op jit(solution)/shard_map/ppermute | solution.py:13
  31.9 28.2 %collective-permute-start.5 = (f32[2,32,64]{2,1,0:T(8,128)S(1)}, f32[2,32,64]{2,1,0:T(8,128)S(1)}, u32[]{:S(2)}, u32[]{:S(2)}) collective-permute-start(f32[2,32,64]{2,1,0:T(8,128)S(1)} %fusion.12), channel_id=1, source_target_pairs={{0,1},{1,2},{2,3},{3,4},{4,5},{5,6},{6,7},{7,8},{8,9},{9,10},{10,1... | collective-permute-start | bytes 49160 | tf_op jit(solution)/shard_map/ppermute | solution.py:13
  34.7 74.4 %collective-permute-start.4 = (f32[2,32,64]{2,1,0:T(8,128)S(1)}, f32[2,32,64]{2,1,0:T(8,128)S(1)}, u32[]{:S(2)}, u32[]{:S(2)}) collective-permute-start(f32[2,32,64]{2,1,0:T(8,128)S(1)} %fusion.12), channel_id=1, source_target_pairs={{0,2},{1,3},{2,4},{3,5},{4,6},{5,7},{6,8},{7,9},{8,10},{9,11},{10,... | collective-permute-start | bytes 49160 | tf_op jit(solution)/shard_map/ppermute | solution.py:13
  38.4 3.8 %collective-permute-start.17 = (f32[1,32,64]{2,1,0:T(8,128)S(1)}, f32[1,32,64]{2,1,0:T(8,128)S(1)}, u32[]{:S(2)}, u32[]{:S(2)}) collective-permute-start(f32[1,32,64]{2,1,0:T(8,128)S(1)} %fusion.22), channel_id=1, source_target_pairs={{0,2},{2,0},{1,3},{3,1},{4,6},{6,4},{5,7},{7,5},{8,10},{10,8},{9,1... | collective-permute-start | bytes 24584 | tf_op jit(solution)/shard_map/ppermute | solution.py:23
  42.2 70.8 %collective-permute-start.2 = (f32[4,32,64]{2,1,0:T(8,128)S(1)}, f32[4,32,64]{2,1,0:T(8,128)S(1)}, u32[]{:S(2)}, u32[]{:S(2)}) collective-permute-start(f32[4,32,64]{2,1,0:T(8,128)S(1)} %fusion.8), channel_id=1, source_target_pairs={{0,1},{1,2},{2,3},{3,4},{4,5},{5,6},{6,7},{7,8},{8,9},{9,10},{10,1... | collective-permute-start | bytes 98312 | tf_op jit(solution)/shard_map/ppermute | solution.py:13
  45.0 6.3 %collective-permute-start.14 = (f32[1,32,64]{2,1,0:T(8,128)S(1)}, f32[1,32,64]{2,1,0:T(8,128)S(1)}, u32[]{:S(2)}, u32[]{:S(2)}) collective-permute-start(f32[1,32,64]{2,1,0:T(8,128)S(1)} %fusion.22), channel_id=1, source_target_pairs={{0,4},{1,5},{2,6},{3,7},{4,8},{5,9},{6,10},{7,11},{8,12},{9,13},{1... | collective-permute-start | bytes 24584 | tf_op jit(solution)/shard_map/ppermute | solution.py:13
  51.3 5.2 %collective-permute-start.15 = (f32[1,32,64]{2,1,0:T(8,128)S(1)}, f32[1,32,64]{2,1,0:T(8,128)S(1)}, u32[]{:S(2)}, u32[]{:S(2)}) collective-permute-start(f32[1,32,64]{2,1,0:T(8,128)S(1)} %fusion.22), channel_id=1, source_target_pairs={{4,0},{5,1},{6,2},{7,3},{8,4},{9,5},{10,6},{11,7},{12,8},{13,9},{1... | collective-permute-start | bytes 24584 | tf_op jit(solution)/shard_map/ppermute | solution.py:13
  56.5 61.5 %collective-permute-start.3 = (f32[4,32,64]{2,1,0:T(8,128)S(1)}, f32[4,32,64]{2,1,0:T(8,128)S(1)}, u32[]{:S(2)}, u32[]{:S(2)}) collective-permute-start(f32[4,32,64]{2,1,0:T(8,128)S(1)} %fusion.8), channel_id=1, source_target_pairs={{1,0},{2,1},{3,2},{4,3},{5,4},{6,5},{7,6},{8,7},{9,8},{10,9},{11,1... | collective-permute-start | bytes 98312 | tf_op jit(solution)/shard_map/ppermute | solution.py:13
  60.2 61.5 %copy-start.3 = (bf16[8,3,256,256]{3,2,1,0:T(8,128)(2,1)S(1)}, bf16[8,3,256,256]{3,2,1,0:T(8,128)(2,1)}, u32[]{:S(2)}) copy-start(bf16[8,3,256,256]{3,2,1,0:T(8,128)(2,1)} %param.8) | copy-start | bytes 9437188
  60.2 6.0 %collective-permute-start.16 = (f32[1,32,64]{2,1,0:T(8,128)S(1)}, f32[1,32,64]{2,1,0:T(8,128)S(1)}, u32[]{:S(2)}, u32[]{:S(2)}) collective-permute-start(f32[1,32,64]{2,1,0:T(8,128)S(1)} %fusion.22), channel_id=1, source_target_pairs={{6,0},{7,1},{8,2},{9,3},{10,4},{11,5},{12,6},{13,7},{14,8},{15,9},... | collective-permute-start | bytes 24584 | tf_op jit(solution)/shard_map/ppermute | solution.py:13
  66.1 6.7 %collective-permute-start.19 = (f32[1,32,64]{2,1,0:T(8,128)S(1)}, f32[1,32,64]{2,1,0:T(8,128)S(1)}, u32[]{:S(2)}, u32[]{:S(2)}) collective-permute-start(f32[1,32,64]{2,1,0:T(8,128)S(1)} %fusion.17), channel_id=1, source_target_pairs={{0,8},{1,9},{2,10},{3,11},{4,12},{5,13},{6,14},{7,15},{16,24},{17,... | collective-permute-start | bytes 24584 | tf_op jit(solution)/shard_map/ppermute | solution.py:13
  72.8 2.9 %collective-permute-start.20 = (f32[1,32,64]{2,1,0:T(8,128)S(1)}, f32[1,32,64]{2,1,0:T(8,128)S(1)}, u32[]{:S(2)}, u32[]{:S(2)}) collective-permute-start(f32[1,32,64]{2,1,0:T(8,128)S(1)} %fusion.17), channel_id=1, source_target_pairs={{8,0},{9,1},{10,2},{11,3},{12,4},{13,5},{14,6},{15,7},{24,16},{25,... | collective-permute-start | bytes 24584 | tf_op jit(solution)/shard_map/ppermute | solution.py:13
  75.7 8.4 %collective-permute-start.21 = (f32[1,32,64]{2,1,0:T(8,128)S(1)}, f32[1,32,64]{2,1,0:T(8,128)S(1)}, u32[]{:S(2)}, u32[]{:S(2)}) collective-permute-start(f32[1,32,64]{2,1,0:T(8,128)S(1)} %fusion.17), channel_id=1, source_target_pairs={{12,0},{13,1},{14,2},{15,3},{28,16},{29,17},{30,18},{31,19}} | collective-permute-start | bytes 24584 | tf_op jit(solution)/shard_map/ppermute | solution.py:13
  84.2 7.4 %collective-permute-start.18 = (f32[1,32,64]{2,1,0:T(8,128)S(1)}, f32[1,32,64]{2,1,0:T(8,128)S(1)}, u32[]{:S(2)}, u32[]{:S(2)}) collective-permute-start(f32[1,32,64]{2,1,0:T(8,128)S(1)} %fusion.17), channel_id=1, source_target_pairs={{0,12},{1,13},{2,14},{3,15},{16,28},{17,29},{18,30},{19,31}} | collective-permute-start | bytes 24584 | tf_op jit(solution)/shard_map/ppermute | solution.py:13
  91.6 7.4 %collective-permute-start.13 = (f32[1,32,64]{2,1,0:T(8,128)S(1)}, f32[1,32,64]{2,1,0:T(8,128)S(1)}, u32[]{:S(2)}, u32[]{:S(2)}) collective-permute-start(f32[1,32,64]{2,1,0:T(8,128)S(1)} %fusion.22), channel_id=1, source_target_pairs={{0,6},{1,7},{2,8},{3,9},{4,10},{5,11},{6,12},{7,13},{8,14},{9,15},... | collective-permute-start | bytes 24584 | tf_op jit(solution)/shard_map/ppermute | solution.py:13
  99.0 21.4 %collective-permute-start = (f32[8,32,64]{2,1,0:T(8,128)S(1)}, f32[8,32,64]{2,1,0:T(8,128)S(1)}, u32[]{:S(2)}, u32[]{:S(2)}) collective-permute-start(f32[8,32,64]{2,1,0:T(8,128)S(1)} %fusion.269), channel_id=1, source_target_pairs={{0,1},{1,2},{2,3},{3,4},{4,5},{5,6},{6,7},{7,8},{8,9},{9,10},{10,1... | collective-permute-start | bytes 196616 | tf_op jit(solution)/shard_map/ppermute | solution.py:13
  101.9 19.0 %collective-permute-start.1 = (f32[8,32,64]{2,1,0:T(8,128)S(1)}, f32[8,32,64]{2,1,0:T(8,128)S(1)}, u32[]{:S(2)}, u32[]{:S(2)}) collective-permute-start(f32[8,32,64]{2,1,0:T(8,128)S(1)} %fusion.269), channel_id=1, source_target_pairs={{1,0},{2,1},{3,2},{4,3},{5,4},{6,5},{7,6},{8,7},{9,8},{10,9},{11,1... | collective-permute-start | bytes 196616 | tf_op jit(solution)/shard_map/ppermute | solution.py:13
  109.1 12.6 %collective-permute-start.22 = (bf16[32,1,256]{2,0,1:T(8,128)(2,1)S(1)}, bf16[32,1,256]{2,0,1:T(8,128)(2,1)S(1)}, u32[]{:S(2)}, u32[]{:S(2)}) collective-permute-start(bf16[32,1,256]{2,0,1:T(8,128)(2,1)S(1)} %get-tuple-element.30), channel_id=1, source_target_pairs={{0,1},{1,2},{2,3},{3,4},{4,5},{5,6},{6,7},{7,8},{8,9},{9,10},{10,1... | collective-permute-start | bytes 49160 | tf_op jit(solution)/shard_map/ppermute | solution.py:33
  113.0 9.5 %collective-permute-start.23 = (bf16[32,1,256]{2,0,1:T(8,128)(2,1)S(1)}, bf16[32,1,256]{2,0,1:T(8,128)(2,1)S(1)}, u32[]{:S(2)}, u32[]{:S(2)}) collective-permute-start(bf16[32,1,256]{2,0,1:T(8,128)(2,1)S(1)} %get-tuple-element.29), channel_id=1, source_target_pairs={{1,0},{2,1},{3,2},{4,3},{5,4},{6,5},{7,6},{8,7},{9,8},{10,9},{11,1... | collective-permute-start | bytes 49160 | tf_op jit(solution)/shard_map/ppermute | solution.py:34
  118.1 4.0 %copy-start.1 = (bf16[32,2048]{1,0:T(8,128)(2,1)S(1)}, bf16[32,2048]{1,0:T(8,128)(2,1)}, u32[]{:S(2)}) copy-start(bf16[32,2048]{1,0:T(8,128)(2,1)} %param.6) | copy-start | bytes 393220
where the time goes:
time: 126 us; the launch traced here: 124 us
  starting transfers between devices  61.1 us (48%)
  matrix products  28.7 us (23%)
  waiting for transfers between devices  26.2 us (21%)
  other arithmetic  3.57 us (3%)
  local copies, waits for them, and re-layouts  3.35 us (3%)
    ppermute x20, starting transfers between devices, passed_along(): return lax.ppermute(x, axis, pairs)  54.5 us
    ppermute x20, waiting for transfers between devices, passed_along(): return lax.ppermute(x, axis, pairs)  22.6 us
    dot_general x34, matrix products, forward_map(): jnp.einsum('crk,kj->crj', coef, matrix, precision=lax.Precision.HIGHEST)  20.4 us
    dot_general x10, matrix products, backward_map(): jnp.einsum('crj,kj->crk', coef, matrix, precision=lax.Precision.HIGHEST)  5.91 us
    ppermute x1, starting transfers between devices, with_halo(): after = lax.ppermute(leading, axis, down)  4.54 us
    ppermute x2, waiting for transfers between devices, swapped(): return lax.ppermute(block, axis, route)  3.52 us
  transfers between devices with their start and end apart: 24, of which 9 were waited for; matrix products, arithmetic and copies ran while one was open for 22% of the time, Pallas kernels for 0%

commit v1 on v0

v1 whole, which is shorter than its diff:
```python
import functools

import jax
import jax.numpy as jnp
from jax import lax
from jax.experimental import pallas as pl
from jax.experimental.pallas import tpu as pltpu
from jax.sharding import PartitionSpec as P

ROOT_HALF = 0.7071067811865476
OFFSETS = (-3, -2, 2, 3)
AXES = ("leaf", "sub")
BF = jnp.bfloat16
F32 = jnp.float32
VMEM = pl.BlockSpec(memory_space=pltpu.VMEM)
SMEM = pl.BlockSpec(memory_space=pltpu.SMEM)


def mm(a, b):
    return lax.dot_general(a, b, (((1,), (0,)), ((), ())), preferred_element_type=F32)


def mm_t(a, b):
    return lax.dot_general(a, b, (((1,), (1,)), ((), ())), preferred_element_type=F32)


def split(a):
    high = a.astype(BF)
    low = (a - high.astype(F32)).astype(BF)
    return jnp.concatenate([high, low], axis=0)


def mm2(a, b, product=mm):
    out = product(split(a), b)
    return out[: a.shape[0]] + out[a.shape[0] :]


def side(*parts):
    return jnp.concatenate(parts, axis=1)


def stack(*parts):
    return jnp.concatenate(parts, axis=0)


def stages_of(devices):
    bits = devices.bit_length() - 1
    return [(b, 2 if b + 1 < bits else 1) for b in range(0, bits, 2)]


def exchanged(x, apart):
    devices = lax.axis_size(AXES)
    return lax.ppermute(x, AXES, [(i, i ^ apart) for i in range(devices)])


def up_kernel(pos, x, bases, transfer, pay_a, pay_c, own0, own1, own2):
    leaves, rank, size = bases.shape
    rows = x.shape[0]
    up = [mm_t(x[:, i * size : (i + 1) * size], bases[i]) for i in range(leaves)]
    pairs = [side(up[i], up[i + 1]) for i in range(0, leaves, 2)]
    u0 = stack(*pairs)
    own0[...] = u0.astype(BF)
    up1 = mm2(u0, transfer[0].reshape(2 * rank, rank)) * ROOT_HALF
    up1 = [up1[i * rows : (i + 1) * rows] for i in range(leaves // 2)]
    pairs1 = [side(up1[i], up1[i + 1]) for i in range(0, leaves // 2, 2)]
    u1 = stack(*pairs1)
    own1[...] = u1.astype(BF)
    up2 = mm2(u1, transfer[1].reshape(2 * rank, rank)) * ROOT_HALF
    u2 = side(up2[:rows], up2[rows:]).astype(BF)
    own2[...] = u2
    half = size // 2
    end = leaves * size
    right = stack(
        x[:, end - size : end - half],
        x[:, end - half : end],
        pairs[-1].astype(BF),
        pairs1[-1].astype(BF),
        side(up[-3], up1[-3]).astype(BF),
    )
    left = stack(
        x[:, :half],
        x[:, half:size],
        pairs[0].astype(BF),
        pairs1[0].astype(BF),
        side(up[2], up1[2]).astype(BF),
    )
    even = pos[0] % 2 == 0
    edge = right.shape[0]
    pay_a[:edge] = jnp.where(even, right, left)
    pay_c[:edge] = jnp.where(even, left, right)
    pay_a[edge:] = u2
    pay_c[edge:] = u2


def near_kernel(devices, pos, codes, x, blocks, near, ends, masks):
    leaf = pl.program_id(0)
    leaves = pl.num_programs(0)
    size = blocks.shape[-1]
    at = lambda i: x[:, pl.ds(pl.multiple_of(i * size, size), size)]
    before = jnp.maximum(leaf - 1, 0)
    after = jnp.minimum(leaf + 1, leaves - 1)
    zero = jnp.zeros((x.shape[0], size), BF)
    total = mm_t(at(leaf), blocks[0, 1])
    total += mm_t(jnp.where(leaf > 0, at(before), zero), blocks[0, 0])
    total += mm_t(jnp.where(leaf < leaves - 1, at(after), zero), blocks[0, 2])
    near[:, pl.ds(pl.multiple_of(leaf * size, size), size)] = total

    @pl.when(leaf == 0)
    def _():
        ends[0] = blocks[0, 0]
        p = pos[0]
        lane = lax.broadcasted_iota(jnp.int32, (1, masks.shape[1]), 1) // (masks.shape[1] // 4)
        offset = jnp.where(lane < 2, lane - 3, lane)
        row = 0
        for level, count in mask_rows(devices, ends_leaves(near, size)):
            total_clusters = devices * count if count > 0 else devices >> -count
            for c in range(max(count, 1)):
                index = p * count + c if count > 0 else p >> -count
                hit = jnp.zeros(lane.shape, jnp.bool_)
                for slot in range(codes.shape[1]):
                    hit = hit | (lane == codes[level, slot, index])
                partner = index + offset
                hit = hit & (partner >= 0) & (partner < total_clusters)
                masks[row : row + 1] = jnp.where(hit, 1.0, 0.0).astype(F32)
                row += 1

    @pl.when(leaf == leaves - 1)
    def _():
        ends[1] = blocks[0, 2]


def ends_leaves(near, size):
    return near.shape[1] // size


def mask_rows(devices, leaves):
    rows = []
    level = 0
    while leaves > 1:
        rows.append((level, leaves))
        leaves //= 2
        level += 1
    k = 0
    while devices >> k >= 4:
        rows.append((level, 1 if k == 0 else -k))
        level += 1
        k += 1
    return rows


def down_kernel(devices, stages, *refs):
    refs = list(refs)
    pos, own0, own1, own2 = refs[:4]
    refs = refs[4:]
    received = []
    for _, radix in stages:
        count = 3 if radix == 2 else 1
        received.append(refs[:count])
        refs = refs[count:]
    masks, couple, transfer, bases, near, ends, out, gathered, *ups = refs
    leaves, rank, size = bases.shape
    rows = own2.shape[0]
    edge = received[0][0].shape[0] - rows
    p = pos[0]
    table = lambda level: transfer[level].reshape(2 * rank, rank)
    links = lambda level: couple[level].reshape(4 * rank, rank)

    gathered[0] = own2[...]
    filled = 1
    for got in received:
        for j, ref in enumerate(got):
            skip = edge if j != 1 else 0
            piece = ref[skip:].reshape(filled, rows, 2 * rank)
            gathered[(j + 1) * filled : (j + 2) * filled] = piece
        filled *= len(got) + 1

    even = p % 2 == 0
    first = received[0][0][:edge]
    other = jnp.zeros_like(first)
    open_ = jnp.bool_(True)
    for number, ((b, radix), got) in enumerate(zip(stages, received)):
        digit = (p >> b) & (2**radix - 1)
        digit = jnp.where(even, digit, 2**radix - 1 - digit)
        if number > 0:
            other = jnp.where(open_ & (digit % 2 == 1), got[0][:edge], other)
        if radix == 2:
            other = jnp.where(open_ & (digit == 2), got[2][:edge], other)
        open_ = open_ & (digit == 0)
    left = jnp.where(even, other, first)
    right = jnp.where(even, first, other)

    flat = gathered[...].reshape(devices * rows, 2 * rank)
    level = 3
    up = mm(flat, table(2)) * ROOT_HALF
    count = devices
    ups[0][...] = up.reshape(count, rows, rank)
    for k in range(1, len(ups)):
        bit = (p >> (k - 1)) & 1
        pairs = up.reshape(count // 2, 2, rows, rank)
        count //= 2
        even_part = pairs[:, 0].reshape(count * rows, rank)
        odd_part = pairs[:, 1].reshape(count * rows, rank)
        turned = stack(transfer[level, bit], transfer[level, 1 - bit])
        up = mm2(side(even_part, odd_part), turned) * ROOT_HALF
        ups[k][...] = up.reshape(count, rows, rank)
        level += 1

    row = leaves + leaves // 2 + leaves // 4
    fars = []
    for k in range(len(ups)):
        a = p >> k
        n = devices >> k
        parts = [ups[k][a ^ jnp.clip(a + o, 0, n - 1)] for o in OFFSETS]
        masked = side(*parts) * masks[row + k : row + k + 1]
        fars.append(mm2(masked, links(3 + k)))

    state = fars[-1]
    for k in reversed(range(len(ups) - 1)):
        state = fars[k] + mm2(state, transfer[3 + k, (p >> k) & 1], mm_t)

    at = lambda o: gathered[p ^ jnp.clip(p + o, 0, devices - 1)]
    b2, b1, a1, a2 = at(-2), at(-1), at(1), at(2)
    m = lambda c: masks[c : c + 1].astype(BF)
    row = leaves + leaves // 2
    lhs = stack(
        side(b2[:, rank:], b1[:, :rank], a1) * m(row),
        side(b1, a1[:, rank:], a2[:, :rank]) * m(row + 1),
    )
    far = mm(lhs, links(2))
    state = mm2(state, table(2), mm_t)
    state = far + stack(state[:, :rank], state[:, rank:])

    lo = slice(0, rank)
    hi = slice(rank, 2 * rank)
    s = slice(edge - 2 * rows, edge - rows)
    t = slice(edge - rows, edge)
    ext = [left[t, hi], left[s, lo], left[s, hi]]
    for j in range(leaves // 4):
        ext += [own1[j * rows : (j + 1) * rows, lo], own1[j * rows : (j + 1) * rows, hi]]
    ext += [right[s, lo], right[s, hi], right[t, hi]]
    row = leaves
    lhs = [
        side(*[ext[c + 3 + o] for o in OFFSETS]) * m(row + c) for c in range(leaves // 2)
    ]
    far = mm(stack(*lhs), links(1))
    state = mm2(state, table(1), mm_t)
    state = far + stack(*[state[c // 2 * rows : (c // 2 + 1) * rows, (lo, hi)[c % 2]] for c in range(leaves // 2)])

    s = slice(edge - 3 * rows, edge - 2 * rows)
    ext = [left[t, lo], left[s, lo], left[s, hi]]
    for j in range(leaves // 2):
        ext += [own0[j * rows : (j + 1) * rows, lo], own0[j * rows : (j + 1) * rows, hi]]
    ext += [right[s, lo], right[s, hi], right[t, lo]]
    lhs = [side(*[ext[c + 3 + o] for o in OFFSETS]) * m(c) for c in range(leaves)]
    far = mm(stack(*lhs), links(0))
    state = mm2(state, table(0), mm_t)
    x_left = side(left[:rows], left[rows : 2 * rows])
    x_right = side(right[:rows], right[rows : 2 * rows])
    for c in range(leaves):
        coef = state[c // 2 * rows : (c // 2 + 1) * rows, (lo, hi)[c % 2]] + far[c * rows : (c + 1) * rows]
        cols = slice(c * size, (c + 1) * size)
        total = mm(coef.astype(BF), bases[c]) + near[:, cols]
        if c == 0:
            total += mm_t(x_left, ends[0])
        if c == leaves - 1:
            total += mm_t(x_right, ends[1])
        out[:, cols] = total.astype(BF)


def shards(rhs, bases, near_blocks, transfer, couple, codes):
    rows = rhs.shape[0]
    leaves, rank, size = bases.shape
    devices = lax.axis_size(AXES)
    stages = stages_of(devices)
    pos = lax.axis_index(AXES).astype(jnp.int32).reshape(1)
    edge = 5 * rows
    pay = jax.ShapeDtypeStruct((edge + rows, 2 * rank), BF)
    pay_a, pay_c, own0, own1, own2 = pl.pallas_call(
        up_kernel,
        out_shape=[
            pay,
            pay,
            jax.ShapeDtypeStruct((leaves // 2 * rows, 2 * rank), BF),
            jax.ShapeDtypeStruct((leaves // 4 * rows, 2 * rank), BF),
            jax.ShapeDtypeStruct((rows, 2 * rank), BF),
        ],
        grid=(1,),
        in_specs=[
            SMEM,
            pl.BlockSpec(rhs.shape, lambda i: (0, 0)),
            pl.BlockSpec(bases.shape, lambda i: (0, 0, 0)),
            pl.BlockSpec((2, 2, rank, rank), lambda i: (0, 0, 0, 0)),
        ],
        out_specs=[VMEM] * 5,
        name="up_sweep",
    )(pos, rhs, bases, transfer)

    row_count = sum(max(count, 1) for _, count in mask_rows(devices, leaves))
    near, ends, masks = pl.pallas_call(
        functools.partial(near_kernel, devices),
        out_shape=[
            jax.ShapeDtypeStruct((rows, leaves * size), F32),
            jax.ShapeDtypeStruct((2, size, size), BF),
            jax.ShapeDtypeStruct((-(-row_count // 8) * 8, 4 * rank), F32),
        ],
        grid=(leaves,),
        in_specs=[
            SMEM,
            SMEM,
            VMEM,
            pl.BlockSpec((1, 3, size, size), lambda i: (i, 0, 0, 0)),
        ],
        out_specs=[VMEM] * 3,
        name="near_field",
        cost_estimate=pl.CostEstimate(flops=3 * leaves * rows * size * size * 2, bytes_accessed=3 * leaves * size * size * 2, transcendentals=0),
    )(pos, codes, rhs, near_blocks)

    received = []
    gathered = own2
    relay = None
    for b, radix in stages:
        if relay is not None:
            pay_a = pay_c = stack(relay, gathered)
        if radix == 1:
            got = [exchanged(pay_a, 1 << b)]
        else:
            got = [exchanged(pay_a, 1 << b), exchanged(gathered, 2 << b), exchanged(pay_c, 3 << b)]
        received.append(got)
        relay = got[-1][:edge]
        gathered = stack(gathered, *[g[edge:] if j != 1 else g for j, g in enumerate(got)])

    levels = [k for k in range(devices.bit_length()) if devices >> k >= 4]
    flat = [g for got in received for g in got]
    operands = [own0, own1, own2, *flat, masks, couple, transfer, bases, near, ends]
    return pl.pallas_call(
        functools.partial(down_kernel, devices, stages),
        out_shape=jax.ShapeDtypeStruct((rows, leaves * size), BF),
        in_specs=[SMEM] + [VMEM] * len(operands),
        out_specs=VMEM,
        scratch_shapes=[pltpu.VMEM((devices, rows, 2 * rank), BF)]
        + [pltpu.VMEM((devices >> k, rows, rank), F32) for k in levels],
        name="down_sweep",
    )(pos, *operands)


def solution(mesh):
    return jax.shard_map(
        shards,
        mesh=mesh,
        in_specs=(
            P(None, ("groups", "leaf", "sub")),
            P(("groups", "leaf", "sub"), None, None),
            P(("groups", "leaf", "sub"), None, None, None),
            P(),
            P(),
            P(),
        ),
        out_specs=P(None, ("groups", "leaf", "sub")),
        check_vma=False,
    )
```

time: 126 us -> 25.5 us (0.20)
  the two profiles are of different devices: /device:TPU:24 before, /device:TPU:0 now
where the time goes in v1:
time: 25.5 us; the launch traced here: 25.2 us
  Pallas kernels  13 us (51%)
  starting transfers between devices  7.55 us (30%)
  waiting for transfers between devices  2.45 us (10%)
  local copies, waits for them, and re-layouts  1.38 us (5%)
  other arithmetic  0.7 us (3%)
    ppermute x6, starting transfers between devices, exchanged(): return lax.ppermute(x, AXES, [(i, i ^ apart) for i in range(devices)])  7.55 us
    pallas_call x1, Pallas kernels, shards(): pl.pallas_call(functools.partial(near_kernel, devices), out_shape=[jax.Sh...  6.51 us
    pallas_call x1, Pallas kernels, shards(): pl.pallas_call(functools.partial(down_kernel, devices, stages), out_shape...  4.24 us
    ppermute x6, waiting for transfers between devices, exchanged(): return lax.ppermute(x, AXES, [(i, i ^ apart) for i in range(devices)])  2.45 us
    pallas_call x1, Pallas kernels, shards(): pl.pallas_call(up_kernel, out_shape=[pay, pay, jax.ShapeDtypeStruct((leav...  2.28 us
    unnamed x15, local copies, waits for them, and re-layouts  1.36 us
    concatenate x1, other arithmetic, stack(): return jnp.concatenate(parts, axis=0)  0.7 us
  transfers between devices with their start and end apart: 6, of which 2 were waited for; matrix products, arithmetic and copies ran while one was open for 6% of the time, Pallas kernels for 26%

profile of v1, /device:TPU:0, one launch (start us, length us, event | category | flops | bytes accessed | tf_op | source)
XLA Modules:
  0.0 25.2 jit_solution(13181941776089478959)
XLA Ops:
  0.0 2.3 %up_sweep.1 = (bf16[192,128]{1,0:T(8,128)(2,1)}, bf16[192,128]{1,0:T(8,128)(2,1)}, bf16[128,128]{1,0:T(8,128)(2,1)}, bf16[64,128]{1,0:T(8,128)(2,1)}, bf16[32,128]{1,0:T(8,128)(2,1)}) custom-call(s32[1]{0:T(128)} %bitcast.pos.refs_0_, bf16[32,2048]{1,0:T(8,128)(2,1)} %x.3, bf16[8,64,256]{2,1,0:T(8,128)(2,1)} %refs_13_.1, bf16[12,2,64,64]{3,2,1,0:T(8,128)(2,1)} %refs_12_.1), custom_call_target="tpu_custom_call" | custom-call | tf_op jit(solution)/shard_map/up_sweep/pallas_call | solution.py:278
  2.3 2.4 %collective-permute-start.2 = (bf16[192,128]{1,0:T(8,128)(2,1)}, bf16[192,128]{1,0:T(8,128)(2,1)S(1)}, u32[]{:S(2)}, u32[]{:S(2)}) collective-permute-start(bf16[192,128]{1,0:T(8,128)(2,1)} %get-tuple-element.17), channel_id=1, source_target_pairs={{0,3},{1,2},{2,1},{3,0},{4,7},{5,6},{6,5},{7,4},{8,11},{9,10},{10,... | collective-permute-start | bytes 147464 | tf_op jit(solution)/shard_map/ppermute | solution.py:53
  4.7 0.6 %collective-permute-start.1 = (bf16[32,128]{1,0:T(8,128)(2,1)}, bf16[32,128]{1,0:T(8,128)(2,1)S(1)}, u32[]{:S(2)}, u32[]{:S(2)}) collective-permute-start(bf16[32,128]{1,0:T(8,128)(2,1)} %get-tuple-element.15.refs_3_), channel_id=1, source_target_pairs={{0,2},{1,3},{2,0},{3,1},{4,6},{5,7},{6,4},{7,5},{8,10},{9,11},{10,... | collective-permute-start | bytes 24584 | tf_op jit(solution)/shard_map/ppermute | solution.py:53
  5.3 0.1 collective-permute-start
  5.3 1.8 %collective-permute-done.2.refs_6_ = bf16[192,128]{1,0:T(8,128)(2,1)S(1)} collective-permute-done((bf16[192,128]{1,0:T(8,128)(2,1)}, bf16[192,128]{1,0:T(8,128)(2,1)S(1)}, u32[]{:S(2)}, u32[]{:S(2)}) %collective-permute-start.2) | collective-permute-done | bytes 49184 | tf_op jit(solution)/shard_map/ppermute | solution.py:53
  7.1 0.0 copy-start
  7.1 0.7 %constant_dynamic-update-slice_fusion.3 = bf16[288,128]{1,0:T(8,128)(2,1)S(1)} fusion(bf16[288,128]{1,0:T(8,128)(2,1)S(1)} %slice_dynamic-update-slice_fusion, bf16[32,128]{1,0:T(8,128)(2,1)} %get-tuple-element.15.refs_3_), kind=kLoop, calls=%fused_computation.5 | loop fusion | bytes 16384
  7.8 0.0 collective-permute-done.refs_4_
  7.8 0.0 copy-start.4
  7.9 0.7 %collective-permute-done.1.refs_5_ = bf16[32,128]{1,0:T(8,128)(2,1)S(1)} collective-permute-done((bf16[32,128]{1,0:T(8,128)(2,1)}, bf16[32,128]{1,0:T(8,128)(2,1)S(1)}, u32[]{:S(2)}, u32[]{:S(2)}) %collective-permute-start.1) | collective-permute-done | bytes 8224 | tf_op jit(solution)/shard_map/ppermute | solution.py:53
  8.5 0.0 copy-start.1
  8.5 3.9 %collective-permute-start.5 = (bf16[288,128]{1,0:T(8,128)(2,1)S(1)}, bf16[288,128]{1,0:T(8,128)(2,1)S(1)}, u32[]{:S(2)}, u32[]{:S(2)}) collective-permute-start(bf16[288,128]{1,0:T(8,128)(2,1)S(1)} %get-tuple-element.24), channel_id=1, source_target_pairs={{0,12},{1,13},{2,14},{3,15},{4,8},{5,9},{6,10},{7,11},{8,4},{9,5},... | collective-permute-start | bytes 221192 | tf_op jit(solution)/shard_map/ppermute | solution.py:53
  12.4 0.0 collective-permute-start.3
  12.4 0.7 %pad_maximum_fusion = bf16[128,128]{1,0:T(8,128)(2,1)S(1)} fusion(bf16[32,128]{1,0:T(8,128)(2,1)S(1)} %get-tuple-element.23, bf16[32,128]{1,0:T(8,128)(2,1)S(1)} %collective-permute-done.1.refs_5_, bf16[32,128]{1,0:T(8,128)(2,1)S(1)} %get-tuple-element.21, bf16[32,128]{1,0:T(8,128)(2,1)} %get-tuple-element.15.refs_3_), kind=kLoop, calls=%fused_computation.1 | loop fusion | flops 131072 | bytes 65536 | tf_op jit(solution)/shard_map/concatenate | solution.py:43
  13.1 0.6 %collective-permute-start.4 = (bf16[128,128]{1,0:T(8,128)(2,1)S(1)}, bf16[128,128]{1,0:T(8,128)(2,1)S(1)}, u32[]{:S(2)}, u32[]{:S(2)}) collective-permute-start(bf16[128,128]{1,0:T(8,128)(2,1)S(1)} %pad_maximum_fusion), channel_id=1, source_target_pairs={{0,8},{1,9},{2,10},{3,11},{4,12},{5,13},{6,14},{7,15},{8,0},{9,1},... | collective-permute-start | bytes 98312 | tf_op jit(solution)/shard_map/ppermute | solution.py:53
  13.7 6.5 %near_field.1 = (f32[32,2048]{1,0:T(8,128)}, bf16[2,256,256]{2,1,0:T(8,128)(2,1)}, f32[24,256]{1,0:T(8,128)}) custom-call(s32[1]{0:T(128)} %bitcast.pos.refs_0_, s32[12,3,128]{2,1,0:T(4,128)} %codes.1, bf16[32,2048]{1,0:T(8,128)(2,1)} %x.3, bf16[8,3,256,256]{3,2,1,0:T(8,128)(2,1)} %blocks.1), custom_call_target="tpu_custom_call" | custom-call | flops 100663296 | bytes 3145728 | tf_op jit(solution)/shard_map/near_field/pallas_call | solution.py:299
  20.2 0.0 collective-permute-done.4.refs_8_
  20.2 0.0 copy-start.5
  20.3 0.0 collective-permute-done.5.refs_9_
  20.3 0.0 copy-start.2
  20.3 0.0 collective-permute-done.3.refs_7_
  20.3 0.0 copy-start.3
  20.3 0.0 copy-done
  20.3 0.0 copy-done.4
  20.3 0.0 copy-done.1
  20.3 0.5 %copy-done.5 = bf16[128,128]{1,0:T(8,128)(2,1)} copy-done((bf16[128,128]{1,0:T(8,128)(2,1)}, bf16[128,128]{1,0:T(8,128)(2,1)S(1)}, u32[]{:S(2)}) %copy-start.5) | copy-done | bytes 32792
  20.9 0.0 copy-done.2
  20.9 0.0 copy-done.3
  20.9 4.2 %down_sweep.1 = bf16[32,2048]{1,0:T(8,128)(2,1)} custom-call(s32[1]{0:T(128)} %bitcast.pos.refs_0_, bf16[128,128]{1,0:T(8,128)(2,1)} %get-tuple-element.13.refs_1_, bf16[64,128]{1,0:T(8,128)(2,1)} %get-tuple-element.14.refs_2_, bf16[32,128]{1,0:T(8,128)(2,1)} %get-tuple-element.15.refs_3_, bf16[192,128]{1,0:T(8,128)(2,1)} %copy-done.4, ...), custom_call_target="tpu_custom_call" | custom-call | tf_op jit(solution)/shard_map/down_sweep/pallas_call | solution.py:335
  (4 shorter events, 0.0 us)
Async XLA Ops:
  2.3 4.8 %collective-permute-start.2 = (bf16[192,128]{1,0:T(8,128)(2,1)}, bf16[192,128]{1,0:T(8,128)(2,1)S(1)}, u32[]{:S(2)}, u32[]{:S(2)}) collective-permute-start(bf16[192,128]{1,0:T(8,128)(2,1)} %get-tuple-element.17), channel_id=1, source_target_pairs={{0,3},{1,2},{2,1},{3,0},{4,7},{5,6},{6,5},{7,4},{8,11},{9,10},{10,... | collective-permute-start | bytes 147464 | tf_op jit(solution)/shard_map/ppermute | solution.py:53
  4.7 3.9 %collective-permute-start.1 = (bf16[32,128]{1,0:T(8,128)(2,1)}, bf16[32,128]{1,0:T(8,128)(2,1)S(1)}, u32[]{:S(2)}, u32[]{:S(2)}) collective-permute-start(bf16[32,128]{1,0:T(8,128)(2,1)} %get-tuple-element.15.refs_3_), channel_id=1, source_target_pairs={{0,2},{1,3},{2,0},{3,1},{4,6},{5,7},{6,4},{7,5},{8,10},{9,11},{10,... | collective-permute-start | bytes 24584 | tf_op jit(solution)/shard_map/ppermute | solution.py:53
  5.3 2.6 %collective-permute-start = (bf16[192,128]{1,0:T(8,128)(2,1)}, bf16[192,128]{1,0:T(8,128)(2,1)S(1)}, u32[]{:S(2)}, u32[]{:S(2)}) collective-permute-start(bf16[192,128]{1,0:T(8,128)(2,1)} %get-tuple-element.16), channel_id=1, source_target_pairs={{0,1},{1,0},{2,3},{3,2},{4,5},{5,4},{6,7},{7,6},{8,9},{9,8},{10,11... | collective-permute-start | bytes 147464 | tf_op jit(solution)/shard_map/ppermute | solution.py:53
  7.1 13.2 %copy-start = (bf16[192,128]{1,0:T(8,128)(2,1)}, bf16[192,128]{1,0:T(8,128)(2,1)S(1)}, u32[]{:S(2)}) copy-start(bf16[192,128]{1,0:T(8,128)(2,1)S(1)} %collective-permute-done.2.refs_6_) | copy-start | bytes 147460
  7.8 12.5 %copy-start.4 = (bf16[192,128]{1,0:T(8,128)(2,1)}, bf16[192,128]{1,0:T(8,128)(2,1)S(1)}, u32[]{:S(2)}) copy-start(bf16[192,128]{1,0:T(8,128)(2,1)S(1)} %collective-permute-done.refs_4_) | copy-start | bytes 147460
  8.5 11.8 %copy-start.1 = (bf16[32,128]{1,0:T(8,128)(2,1)}, bf16[32,128]{1,0:T(8,128)(2,1)S(1)}, u32[]{:S(2)}) copy-start(bf16[32,128]{1,0:T(8,128)(2,1)S(1)} %collective-permute-done.1.refs_5_) | copy-start | bytes 24580
  8.5 11.7 %collective-permute-start.5 = (bf16[288,128]{1,0:T(8,128)(2,1)S(1)}, bf16[288,128]{1,0:T(8,128)(2,1)S(1)}, u32[]{:S(2)}, u32[]{:S(2)}) collective-permute-start(bf16[288,128]{1,0:T(8,128)(2,1)S(1)} %get-tuple-element.24), channel_id=1, source_target_pairs={{0,12},{1,13},{2,14},{3,15},{4,8},{5,9},{6,10},{7,11},{8,4},{9,5},... | collective-permute-start | bytes 221192 | tf_op jit(solution)/shard_map/ppermute | solution.py:53
  12.4 7.9 %collective-permute-start.3 = (bf16[288,128]{1,0:T(8,128)(2,1)S(1)}, bf16[288,128]{1,0:T(8,128)(2,1)S(1)}, u32[]{:S(2)}, u32[]{:S(2)}) collective-permute-start(bf16[288,128]{1,0:T(8,128)(2,1)S(1)} %get-tuple-element.24), channel_id=1, source_target_pairs={{0,4},{1,5},{2,6},{3,7},{4,0},{5,1},{6,2},{7,3},{8,12},{9,13},{10,... | collective-permute-start | bytes 221192 | tf_op jit(solution)/shard_map/ppermute | solution.py:53
  13.1 7.2 %collective-permute-start.4 = (bf16[128,128]{1,0:T(8,128)(2,1)S(1)}, bf16[128,128]{1,0:T(8,128)(2,1)S(1)}, u32[]{:S(2)}, u32[]{:S(2)}) collective-permute-start(bf16[128,128]{1,0:T(8,128)(2,1)S(1)} %pad_maximum_fusion), channel_id=1, source_target_pairs={{0,8},{1,9},{2,10},{3,11},{4,12},{5,13},{6,14},{7,15},{8,0},{9,1},... | collective-permute-start | bytes 98312 | tf_op jit(solution)/shard_map/ppermute | solution.py:53
  20.2 0.6 %copy-start.5 = (bf16[128,128]{1,0:T(8,128)(2,1)}, bf16[128,128]{1,0:T(8,128)(2,1)S(1)}, u32[]{:S(2)}) copy-start(bf16[128,128]{1,0:T(8,128)(2,1)S(1)} %collective-permute-done.4.refs_8_) | copy-start | bytes 98308
  20.3 0.6 %copy-start.2 = (bf16[288,128]{1,0:T(8,128)(2,1)}, bf16[288,128]{1,0:T(8,128)(2,1)S(1)}, u32[]{:S(2)}) copy-start(bf16[288,128]{1,0:T(8,128)(2,1)S(1)} %collective-permute-done.5.refs_9_) | copy-start | bytes 221188
  20.3 0.7 %copy-start.3 = (bf16[288,128]{1,0:T(8,128)(2,1)}, bf16[288,128]{1,0:T(8,128)(2,1)S(1)}, u32[]{:S(2)}) copy-start(bf16[288,128]{1,0:T(8,128)(2,1)S(1)} %collective-permute-done.3.refs_7_) | copy-start | bytes 221188

commit v2 on v1

v2 whole, which is shorter than its diff:
```python
import functools

import jax
import jax.numpy as jnp
from jax import lax
from jax.experimental import pallas as pl
from jax.experimental.pallas import tpu as pltpu
from jax.sharding import PartitionSpec as P

ROOT_HALF = 0.7071067811865476
OFFSETS = (-3, -2, 2, 3)
AXES = ("leaf", "sub")
BF = jnp.bfloat16
F32 = jnp.float32


def mm(a, b):
    return lax.dot_general(a, b, (((1,), (0,)), ((), ())), preferred_element_type=F32)


def mm_t(a, b):
    return lax.dot_general(a, b, (((1,), (1,)), ((), ())), preferred_element_type=F32)


def split(a):
    high = a.astype(BF)
    low = (a - high.astype(F32)).astype(BF)
    return jnp.concatenate([high, low], axis=0)


def mm2(a, b, product=mm):
    out = product(split(a), b)
    return out[: a.shape[0]] + out[a.shape[0] :]


def side(*parts):
    return jnp.concatenate(parts, axis=1)


def stack(*parts):
    return jnp.concatenate(parts, axis=0)


def stages_of(devices):
    bits = [1 << b for b in range(1, devices.bit_length() - 1)]
    rounds = []
    while len(bits) > 1:
        low, high, *bits = bits
        rounds.append((low, high, low | high))
    return rounds + [(b,) for b in bits] + [(1,)]


def slots_of(stages):
    held = [[0]]
    for masks in stages:
        held.append(held[-1] + [slot ^ m for m in masks for slot in held[-1]])
    return held


def exchanged(x, apart):
    devices = lax.axis_size(AXES)
    return lax.ppermute(x, AXES, [(i, i ^ apart) for i in range(devices)])


def load_kernel(count, *refs):
    copies = [
        pltpu.make_async_copy(refs[i], refs[count + i], refs[-1].at[i]) for i in range(count)
    ]
    for copy in copies:
        copy.start()
    for copy in copies:
        copy.wait()


def up_kernel(x, bases, transfer, facing, away, own0, own1, own2):
    leaves, rank, size = bases.shape
    rows = x.shape[0]
    up = [mm_t(x[:, i * size : (i + 1) * size], bases[i]) for i in range(leaves)]
    pairs = [side(up[i], up[i + 1]) for i in range(0, leaves, 2)]
    u0 = stack(*pairs)
    own0[...] = u0.astype(BF)
    up1 = mm2(u0, transfer[0].reshape(2 * rank, rank)) * ROOT_HALF
    up1 = [up1[i * rows : (i + 1) * rows] for i in range(leaves // 2)]
    pairs1 = [side(up1[i], up1[i + 1]) for i in range(0, leaves // 2, 2)]
    u1 = stack(*pairs1)
    own1[...] = u1.astype(BF)
    up2 = mm2(u1, transfer[1].reshape(2 * rank, rank)) * ROOT_HALF
    own2[...] = side(up2[:rows], up2[rows:]).astype(BF)
    half = size // 2
    end = leaves * size
    right = stack(
        x[:, end - size : end - half],
        x[:, end - half : end],
        pairs[-1].astype(BF),
        pairs1[-1].astype(BF),
        side(up[-3], up1[-3]).astype(BF),
    )
    left = stack(
        x[:, :half],
        x[:, half:size],
        pairs[0].astype(BF),
        pairs1[0].astype(BF),
        side(up[2], up1[2]).astype(BF),
    )
    even = lax.axis_index(AXES) % 2 == 0
    facing[...] = jnp.where(even, right, left)
    away[...] = jnp.where(even, left, right)


def pack_kernel(after, *refs):
    *parts, out = refs
    at = 0
    for part in parts:
        out[at : at + part.shape[0]] = part[...]
        at += part.shape[0]


def near_kernel(codes, x, blocks, near, ends, masks):
    leaves, _, size, _ = blocks.shape
    at = lambda i: x[:, i * size : (i + 1) * size]
    for i in range(leaves):
        total = mm_t(at(i), blocks[i, 1])
        if i > 0:
            total += mm_t(at(i - 1), blocks[i, 0])
        if i < leaves - 1:
            total += mm_t(at(i + 1), blocks[i, 2])
        near[:, i * size : (i + 1) * size] = total
    ends[0] = blocks[0, 0]
    ends[1] = blocks[leaves - 1, 2]

    p = lax.axis_index(AXES)
    wide = codes.shape[2]
    quarter = masks.shape[1] // 4
    across = lax.broadcasted_iota(jnp.int32, (8, masks.shape[1]), 1) // quarter
    offset = jnp.where(across < 2, across - 3, across)
    cluster = lax.broadcasted_iota(jnp.int32, (8, masks.shape[1]), 0)
    diagonal = lax.broadcasted_iota(jnp.int32, (8, wide), 0) == lax.broadcasted_iota(jnp.int32, (8, wide), 1)
    for level in range(masks.shape[0] // 8):
        count = leaves >> level
        index = p * count if count > 0 else p >> level - (leaves.bit_length() - 1)
        clusters = wide >> level
        hit = jnp.zeros(across.shape, jnp.bool_)
        for slot in range(codes.shape[1]):
            row = jnp.broadcast_to(codes[level, slot : slot + 1], (8, wide))
            row = pltpu.roll(row, lax.rem(wide - index, wide), 1)
            code = jnp.sum(jnp.where(diagonal, row, 0).astype(F32), axis=1, keepdims=True)
            hit = hit | (across.astype(F32) == code)
        partner = index + cluster + offset
        hit = hit & (partner >= 0) & (partner < clusters)
        masks[8 * level : 8 * level + 8] = jnp.where(hit, 1.0, 0.0)


def climb(up, count, transfer, level, bit, rows):
    rank = up.shape[1]
    pairs = up.reshape(count // 2, 2, rows, rank)
    halves = [pairs[:, i].reshape(count // 2 * rows, rank) for i in range(2)]
    turned = stack(transfer[level, bit], transfer[level, 1 - bit])
    return mm2(side(*halves), turned) * ROOT_HALF


def down_kernel(devices, stages, *refs):
    refs = list(refs)
    own0, own1, own2, across = refs[:4]
    refs = refs[4:]
    received = []
    for group in stages:
        received.append(refs[: len(group)])
        refs = refs[len(group) :]
    masks, couple, transfer, bases, near, ends, out, gathered, *ups = refs
    leaves, rank, size = bases.shape
    rows = own2.shape[0]
    edge = across.shape[0]
    p = lax.axis_index(AXES)
    table = lambda level: transfer[level].reshape(2 * rank, rank)
    links = lambda level: couple[level].reshape(4 * rank, rank)

    gathered[0] = own2[...]
    for group, got, held in zip(stages, received, slots_of(stages)):
        for m, ref in zip(group, got):
            skip = edge if m == 1 else 0
            for i, slot in enumerate(held):
                at = skip + i * rows
                gathered[slot ^ m] = ref[at : at + rows]

    even = p % 2 == 0
    first = received[-1][0][:edge]
    other = across[...]
    left = jnp.where(even, other, first)
    right = jnp.where(even, first, other)

    count = devices
    up = mm(gathered[...].reshape(devices * rows, 2 * rank), table(2)) * ROOT_HALF
    ups[0][...] = up.reshape(count, rows, rank)
    for k in range(1, len(ups)):
        up = climb(up, count, transfer, 2 + k, (p >> (k - 1)) & 1, rows)
        count //= 2
        ups[k][...] = up.reshape(count, rows, rank)

    fars = []
    for k in range(len(ups)):
        a = p >> k
        n = devices >> k
        parts = [ups[k][a ^ jnp.clip(a + o, 0, n - 1)] for o in OFFSETS]
        masked = side(*parts) * masks[8 * (3 + k) : 8 * (3 + k) + 1]
        fars.append(mm2(masked, links(3 + k)))

    state = fars[-1]
    for k in reversed(range(len(ups) - 1)):
        state = fars[k] + mm2(state, transfer[3 + k, (p >> k) & 1], mm_t)

    at = lambda o: gathered[p ^ jnp.clip(p + o, 0, devices - 1)]
    b2, b1, a1, a2 = at(-2), at(-1), at(1), at(2)
    m = lambda c: masks[c : c + 1].astype(BF)
    row = 16
    lhs = stack(
        side(b2[:, rank:], b1[:, :rank], a1) * m(row),
        side(b1, a1[:, rank:], a2[:, :rank]) * m(row + 1),
    )
    far = mm(lhs, links(2))
    state = mm2(state, table(2), mm_t)
    state = far + stack(state[:, :rank], state[:, rank:])

    lo = slice(0, rank)
    hi = slice(rank, 2 * rank)
    s = slice(edge - 2 * rows, edge - rows)
    t = slice(edge - rows, edge)
    ext = [left[t, hi], left[s, lo], left[s, hi]]
    for j in range(leaves // 4):
        ext += [own1[j * rows : (j + 1) * rows, lo], own1[j * rows : (j + 1) * rows, hi]]
    ext += [right[s, lo], right[s, hi], right[t, hi]]
    row = 8
    lhs = [
        side(*[ext[c + 3 + o] for o in OFFSETS]) * m(row + c) for c in range(leaves // 2)
    ]
    far = mm(stack(*lhs), links(1))
    state = mm2(state, table(1), mm_t)
    state = far + stack(*[state[c // 2 * rows : (c // 2 + 1) * rows, (lo, hi)[c % 2]] for c in range(leaves // 2)])

    s = slice(edge - 3 * rows, edge - 2 * rows)
    ext = [left[t, lo], left[s, lo], left[s, hi]]
    for j in range(leaves // 2):
        ext += [own0[j * rows : (j + 1) * rows, lo], own0[j * rows : (j + 1) * rows, hi]]
    ext += [right[s, lo], right[s, hi], right[t, lo]]
    lhs = [side(*[ext[c + 3 + o] for o in OFFSETS]) * m(c) for c in range(leaves)]
    far = mm(stack(*lhs), links(0))
    state = mm2(state, table(0), mm_t)
    x_left = side(left[:rows], left[rows : 2 * rows])
    x_right = side(right[:rows], right[rows : 2 * rows])
    for c in range(leaves):
        coef = state[c // 2 * rows : (c // 2 + 1) * rows, (lo, hi)[c % 2]] + far[c * rows : (c + 1) * rows]
        cols = slice(c * size, (c + 1) * size)
        total = mm(coef.astype(BF), bases[c]) + near[:, cols]
        if c == 0:
            total += mm_t(x_left, ends[0])
        if c == leaves - 1:
            total += mm_t(x_right, ends[1])
        out[:, cols] = total.astype(BF)


def inside(x):
    return pltpu.with_memory_space_constraint(x, pltpu.VMEM)


def outside(x):
    return pltpu.with_memory_space_constraint(x, pltpu.HBM)


def shards(rhs, bases, near_blocks, transfer, couple, codes):
    rows = rhs.shape[0]
    leaves, rank, size = bases.shape
    devices = lax.axis_size(AXES)
    stages = stages_of(devices)
    edge = 5 * rows
    params = pltpu.CompilerParams(vmem_limit_bytes=16 << 20)
    anywhere = pl.BlockSpec(memory_space=pl.ANY)
    loaded = (rhs, bases, transfer, codes)
    x, bases, transfer, codes = pl.pallas_call(
        functools.partial(load_kernel, len(loaded)),
        out_shape=[pltpu.VMEM(a.shape, a.dtype) for a in loaded],
        in_specs=[anywhere] * len(loaded),
        scratch_shapes=[pltpu.SemaphoreType.DMA((len(loaded),))],
        compiler_params=params,
        name="load",
    )(*map(outside, loaded))

    facing, away, own0, own1, own2 = pl.pallas_call(
        up_kernel,
        out_shape=[
            pltpu.VMEM((edge, 2 * rank), BF),
            pltpu.VMEM((edge, 2 * rank), BF),
            pltpu.VMEM((leaves // 2 * rows, 2 * rank), BF),
            pltpu.VMEM((leaves // 4 * rows, 2 * rank), BF),
            pltpu.VMEM((rows, 2 * rank), BF),
        ],
        compiler_params=params,
        cost_estimate=pl.CostEstimate(flops=1 << 32, bytes_accessed=1 << 20, transcendentals=0),
        name="up_sweep",
    )(*map(inside, (x, bases, transfer)))

    levels = [k for k in range(devices.bit_length()) if devices >> k >= 4]
    near, ends, masks = pl.pallas_call(
        near_kernel,
        out_shape=[
            pltpu.VMEM((rows, leaves * size), F32),
            pltpu.VMEM((2, size, size), BF),
            pltpu.VMEM((8 * (3 + len(levels)), 4 * rank), F32),
        ],
        compiler_params=params,
        name="near_field",
        cost_estimate=pl.CostEstimate(
            flops=3 * leaves * rows * size * size * 2,
            bytes_accessed=3 * leaves * size * size * 2,
            transcendentals=0,
        ),
    )(*map(inside, (codes, x, near_blocks)))

    across = [(i, i + 1) for i in range(1, devices - 1, 2)]
    across = lax.ppermute(away, AXES, across + [(j, i) for i, j in across])
    received = []
    gathered = own2
    for group in stages:
        if group is not stages[-1]:
            got = [exchanged(gathered, m) for m in group]
            if group is not stages[-2]:
                gathered = stack(gathered, *got)
        else:
            parts = (facing, gathered, *(received[-1] if received else ()))
            size_all = sum(part.shape[0] for part in parts)
            pay = pl.pallas_call(
                pack_kernel,
                out_shape=pltpu.VMEM((size_all, 2 * rank), BF),
                compiler_params=params,
                name="pack",
            )(*map(inside, (across, *parts)))
            got = [exchanged(pay, 1)]
        received.append(got)

    flat = [g for got in received for g in got]
    operands = [own0, own1, own2, across, *flat, masks, couple, transfer, bases, near, ends]
    return pl.pallas_call(
        functools.partial(down_kernel, devices, stages),
        out_shape=jax.ShapeDtypeStruct((rows, leaves * size), BF),
        scratch_shapes=[pltpu.VMEM((devices, rows, 2 * rank), BF)]
        + [pltpu.VMEM((devices >> k, rows, rank), F32) for k in levels],
        compiler_params=params,
        name="down_sweep",
    )(*map(inside, operands))


def solution(mesh):
    return jax.shard_map(
        shards,
        mesh=mesh,
        in_specs=(
            P(None, ("groups", "leaf", "sub")),
            P(("groups", "leaf", "sub"), None, None),
            P(("groups", "leaf", "sub"), None, None, None),
            P(),
            P(),
            P(),
        ),
        out_specs=P(None, ("groups", "leaf", "sub")),
        check_vma=False,
    )
```

time: 25.5 us -> 19 us (0.75)
  Pallas kernels: 13 us -> 5.39 us
  waiting for transfers between devices: 2.45 us -> 5.37 us
  local copies, waits for them, and re-layouts: 1.38 us -> 0.04 us
  other arithmetic: 0.7 us -> 0 us
  starting transfers between devices: 7.55 us -> 7.99 us
    pallas_call x2 -> x4, Pallas kernels: 8.79 us -> 2.79 us  [the longest x1 1.18 us: shards(): pl.pallas_call(functools.partial(load_kernel, len(loaded)), out_shape=[pl...]
    ppermute x6 -> x5, waiting for transfers between devices: 2.45 us -> 5.37 us  [exchanged(): return lax.ppermute(x, AXES, [(i, i ^ apart) for i in range(devices)])]
    pallas_call x1, Pallas kernels: 4.24 us -> 2.6 us  [shards(): pl.pallas_call(functools.partial(down_kernel, devices, stages), out_shape...]
    unnamed x15 -> x7, local copies, waits for them, and re-layouts: 1.36 us -> 0.03 us
    concatenate x1 -> x0, other arithmetic: 0.7 us -> none  [stack(): return jnp.concatenate(parts, axis=0)]
    ppermute x0 -> x1, starting transfers between devices: none -> 0.65 us  [shards(): across = lax.ppermute(away, AXES, across + [(j, i) for i, j in across])]
    ppermute x6 -> x5, starting transfers between devices: 7.55 us -> 7.34 us  [exchanged(): return lax.ppermute(x, AXES, [(i, i ^ apart) for i in range(devices)])]
  transfers between devices with their start and end apart: 6 -> 6, of which waited for: 2 -> 3; matrix products, arithmetic and copies ran while one was open for 6% -> 0% of each run, Pallas kernels for 26% -> 5%
where the time goes in v2:
time: 19 us; the launch traced here: 18.9 us
  starting transfers between devices  7.99 us (42%)
  Pallas kernels  5.39 us (28%)
  waiting for transfers between devices  5.37 us (28%)
    ppermute x5, starting transfers between devices, exchanged(): return lax.ppermute(x, AXES, [(i, i ^ apart) for i in range(devices)])  7.34 us
    ppermute x5, waiting for transfers between devices, exchanged(): return lax.ppermute(x, AXES, [(i, i ^ apart) for i in range(devices)])  5.37 us
    pallas_call x1, Pallas kernels, shards(): pl.pallas_call(functools.partial(down_kernel, devices, stages), out_shape...  2.6 us
    pallas_call x1, Pallas kernels, shards(): pl.pallas_call(functools.partial(load_kernel, len(loaded)), out_shape=[pl...  1.18 us
    pallas_call x1, Pallas kernels, shards(): pl.pallas_call(near_kernel, out_shape=[pltpu.VMEM((rows, leaves * size),...  0.94 us
    pallas_call x1, Pallas kernels, shards(): pl.pallas_call(up_kernel, out_shape=[pltpu.VMEM((edge, 2 * rank), BF), pl...  0.67 us
    ppermute x1, starting transfers between devices, shards(): across = lax.ppermute(away, AXES, across + [(j, i) for i, j in across])  0.65 us
  transfers between devices with their start and end apart: 6, of which 3 were waited for; matrix products, arithmetic and copies ran while one was open for 0% of the time, Pallas kernels for 5%

profile of v2, /device:TPU:0, one launch (start us, length us, event | category | flops | bytes accessed | tf_op | source)
XLA Modules:
  0.0 18.9 jit_solution(12583456520230008134)
XLA Ops:
  0.0 1.2 %load.1 = (bf16[32,2048]{1,0:T(8,128)(2,1)S(1)}, bf16[8,64,256]{2,1,0:T(8,128)(2,1)S(1)}, bf16[12,2,64,64]{3,2,1,0:T(8,128)(2,1)S(1)}, s32[12,3,128]{2,1,0:T(4,128)S(1)}) custom-call(bf16[32,2048]{1,0:T(8,128)(2,1)} %refs_0_.1, bf16[8,64,256]{2,1,0:T(8,128)(2,1)} %refs_1_.1, bf16[12,2,64,64]{3,2,1,0:T(8,128)(2,1)} %refs_2_.1, s32[12,3,128]{2,1,0:T(4,128)} %refs_3_.1), custom_call_target="tpu_custom_call" | custom-call | tf_op jit(solution)/shard_map/load/pallas_call | solution.py:277
  1.2 0.0 copy-start
  1.2 0.7 %up_sweep.1 = (bf16[160,128]{1,0:T(8,128)(2,1)S(1)}, bf16[160,128]{1,0:T(8,128)(2,1)S(1)}, bf16[128,128]{1,0:T(8,128)(2,1)S(1)}, bf16[64,128]{1,0:T(8,128)(2,1)S(1)}, bf16[32,128]{1,0:T(8,128)(2,1)S(1)}) custom-call(bf16[32,2048]{1,0:T(8,128)(2,1)S(1)} %get-tuple-element.17.x, bf16[8,64,256]{2,1,0:T(8,128)(2,1)S(1)} %get-tuple-element.18.bases.refs_12_, ...), custom_call_target="tpu_custom_call" | custom-call | flops 4294967296 | bytes 1048576 | tf_op jit(solution)/shard_map/up_sweep/pallas_call | solution.py:286
  1.9 0.0 copy-start.1
  1.9 4.0 %collective-permute-start.3 = (bf16[32,128]{1,0:T(8,128)(2,1)S(1)}, bf16[32,128]{1,0:T(8,128)(2,1)S(1)}, u32[]{:S(2)}, u32[]{:S(2)}) collective-permute-start(bf16[32,128]{1,0:T(8,128)(2,1)S(1)} %get-tuple-element.22.refs_2_), channel_id=1, source_target_pairs={{0,6},{1,7},{2,4},{3,5},{4,2},{5,3},{6,0},{7,1},{8,14},{9,15},{10,... | collective-permute-start | bytes 24584 | tf_op jit(solution)/shard_map/ppermute | solution.py:62
  5.8 0.4 %collective-permute-start.2 = (bf16[32,128]{1,0:T(8,128)(2,1)S(1)}, bf16[32,128]{1,0:T(8,128)(2,1)S(1)}, u32[]{:S(2)}, u32[]{:S(2)}) collective-permute-start(bf16[32,128]{1,0:T(8,128)(2,1)S(1)} %get-tuple-element.22.refs_2_), channel_id=1, source_target_pairs={{0,4},{1,5},{2,6},{3,7},{4,0},{5,1},{6,2},{7,3},{8,12},{9,13},{10,... | collective-permute-start | bytes 24584 | tf_op jit(solution)/shard_map/ppermute | solution.py:62
  6.3 0.2 %collective-permute-start.1 = (bf16[32,128]{1,0:T(8,128)(2,1)S(1)}, bf16[32,128]{1,0:T(8,128)(2,1)S(1)}, u32[]{:S(2)}, u32[]{:S(2)}) collective-permute-start(bf16[32,128]{1,0:T(8,128)(2,1)S(1)} %get-tuple-element.22.refs_2_), channel_id=1, source_target_pairs={{0,2},{1,3},{2,0},{3,1},{4,6},{5,7},{6,4},{7,5},{8,10},{9,11},{10,... | collective-permute-start | bytes 24584 | tf_op jit(solution)/shard_map/ppermute | solution.py:62
  6.5 0.7 %collective-permute-start = (bf16[160,128]{1,0:T(8,128)(2,1)S(1)}, bf16[160,128]{1,0:T(8,128)(2,1)S(1)}, u32[]{:S(2)}, u32[]{:S(2)}) collective-permute-start(bf16[160,128]{1,0:T(8,128)(2,1)S(1)} %get-tuple-element.23), channel_id=1, source_target_pairs={{1,2},{3,4},{5,6},{7,8},{9,10},{11,12},{13,14},{2,1},{4,3},{6,5},{... | collective-permute-start | bytes 122888 | tf_op jit(solution)/shard_map/ppermute | solution.py:318
  7.2 2.8 %collective-permute-done.1.refs_4_ = bf16[32,128]{1,0:T(8,128)(2,1)S(1)} collective-permute-done((bf16[32,128]{1,0:T(8,128)(2,1)S(1)}, bf16[32,128]{1,0:T(8,128)(2,1)S(1)}, u32[]{:S(2)}, u32[]{:S(2)}) %collective-permute-start.1) | collective-permute-done | bytes 8224 | tf_op jit(solution)/shard_map/ppermute | solution.py:62
  10.0 0.0 collective-permute-done.2.refs_5_
  10.0 0.0 collective-permute-done.3.refs_6_
  10.0 2.7 %collective-permute-start.4 = (bf16[128,128]{1,0:T(8,128)(2,1)S(1)}, bf16[128,128]{1,0:T(8,128)(2,1)S(1)}, u32[]{:S(2)}, u32[]{:S(2)}) collective-permute-start(bf16[128,128]{1,0:T(8,128)(2,1)S(1)} %constant_dynamic-update-slice_fusion.refs_1_), channel_id=1, source_target_pairs={{0,8},{1,9},{2,10},{3,11},{4,12},{5,13},{6,14},{7,15},{8,0},{9,1},... | collective-permute-start | bytes 98312 | tf_op jit(solution)/shard_map/ppermute | solution.py:62
  12.6 2.2 %collective-permute-done.4.refs_2_.refs_7_ = bf16[128,128]{1,0:T(8,128)(2,1)S(1)} collective-permute-done((bf16[128,128]{1,0:T(8,128)(2,1)S(1)}, bf16[128,128]{1,0:T(8,128)(2,1)S(1)}, u32[]{:S(2)}, u32[]{:S(2)}) %collective-permute-start.4) | collective-permute-done | bytes 32800 | tf_op jit(solution)/shard_map/ppermute | solution.py:62
  14.9 0.0 collective-permute-done.after.refs_3_
  14.9 0.1 collective-permute-start.5
  15.0 0.0 copy-done
  15.0 0.9 %near_field.1 = (f32[32,2048]{1,0:T(8,128)S(1)}, bf16[2,256,256]{2,1,0:T(8,128)(2,1)S(1)}, f32[48,256]{1,0:T(8,128)S(1)}) custom-call(s32[12,3,128]{2,1,0:T(4,128)S(1)} %get-tuple-element.25.codes, bf16[32,2048]{1,0:T(8,128)(2,1)S(1)} %get-tuple-element.17.x, bf16[8,3,256,256]{3,2,1,0:T(8,128)(2,1)S(1)} %copy-done), custom_call_target="tpu_custom_call" | custom-call | flops 100663296 | bytes 3145728 | tf_op jit(solution)/shard_map/near_field/pallas_call | solution.py:301
  15.9 0.4 %collective-permute-done.5.refs_8_ = bf16[416,128]{1,0:T(8,128)(2,1)S(1)} collective-permute-done((bf16[416,128]{1,0:T(8,128)(2,1)S(1)}, bf16[416,128]{1,0:T(8,128)(2,1)S(1)}, u32[]{:S(2)}, u32[]{:S(2)}) %collective-permute-start.5) | collective-permute-done | bytes 106528 | tf_op jit(solution)/shard_map/ppermute | solution.py:62
  16.3 0.0 copy-done.1
  16.3 2.6 %down_sweep.1 = bf16[32,2048]{1,0:T(8,128)(2,1)} custom-call(bf16[128,128]{1,0:T(8,128)(2,1)S(1)} %get-tuple-element.20.refs_0_, bf16[64,128]{1,0:T(8,128)(2,1)S(1)} %get-tuple-element.21.refs_1_, bf16[32,128]{1,0:T(8,128)(2,1)S(1)} %get-tuple-element.22.refs_2_, bf16[160,128]{1,0:T(8,128)(2,1)S(1)} %collective-permute-done.after.refs_3_, ...), custom_call_target="tpu_custom_call" | custom-call | tf_op jit(solution)/shard_map/down_sweep/pallas_call | solution.py:340
  (5 shorter events, 0.0 us)
Async XLA Ops:
  1.2 13.8 %copy-start = (bf16[8,3,256,256]{3,2,1,0:T(8,128)(2,1)S(1)}, bf16[8,3,256,256]{3,2,1,0:T(8,128)(2,1)}, u32[]{:S(2)}) copy-start(bf16[8,3,256,256]{3,2,1,0:T(8,128)(2,1)} %blocks.1) | copy-start | bytes 9437188
  1.9 14.4 %copy-start.1 = (bf16[12,4,64,64]{3,2,1,0:T(8,128)(2,1)S(1)}, bf16[12,4,64,64]{3,2,1,0:T(8,128)(2,1)}, u32[]{:S(2)}) copy-start(bf16[12,4,64,64]{3,2,1,0:T(8,128)(2,1)} %refs_10_.1) | copy-start | bytes 1179652
  1.9 8.1 %collective-permute-start.3 = (bf16[32,128]{1,0:T(8,128)(2,1)S(1)}, bf16[32,128]{1,0:T(8,128)(2,1)S(1)}, u32[]{:S(2)}, u32[]{:S(2)}) collective-permute-start(bf16[32,128]{1,0:T(8,128)(2,1)S(1)} %get-tuple-element.22.refs_2_), channel_id=1, source_target_pairs={{0,6},{1,7},{2,4},{3,5},{4,2},{5,3},{6,0},{7,1},{8,14},{9,15},{10,... | collective-permute-start | bytes 24584 | tf_op jit(solution)/shard_map/ppermute | solution.py:62
  5.8 4.1 %collective-permute-start.2 = (bf16[32,128]{1,0:T(8,128)(2,1)S(1)}, bf16[32,128]{1,0:T(8,128)(2,1)S(1)}, u32[]{:S(2)}, u32[]{:S(2)}) collective-permute-start(bf16[32,128]{1,0:T(8,128)(2,1)S(1)} %get-tuple-element.22.refs_2_), channel_id=1, source_target_pairs={{0,4},{1,5},{2,6},{3,7},{4,0},{5,1},{6,2},{7,3},{8,12},{9,13},{10,... | collective-permute-start | bytes 24584 | tf_op jit(solution)/shard_map/ppermute | solution.py:62
  6.3 3.7 %collective-permute-start.1 = (bf16[32,128]{1,0:T(8,128)(2,1)S(1)}, bf16[32,128]{1,0:T(8,128)(2,1)S(1)}, u32[]{:S(2)}, u32[]{:S(2)}) collective-permute-start(bf16[32,128]{1,0:T(8,128)(2,1)S(1)} %get-tuple-element.22.refs_2_), channel_id=1, source_target_pairs={{0,2},{1,3},{2,0},{3,1},{4,6},{5,7},{6,4},{7,5},{8,10},{9,11},{10,... | collective-permute-start | bytes 24584 | tf_op jit(solution)/shard_map/ppermute | solution.py:62
  6.5 8.4 %collective-permute-start = (bf16[160,128]{1,0:T(8,128)(2,1)S(1)}, bf16[160,128]{1,0:T(8,128)(2,1)S(1)}, u32[]{:S(2)}, u32[]{:S(2)}) collective-permute-start(bf16[160,128]{1,0:T(8,128)(2,1)S(1)} %get-tuple-element.23), channel_id=1, source_target_pairs={{1,2},{3,4},{5,6},{7,8},{9,10},{11,12},{13,14},{2,1},{4,3},{6,5},{... | collective-permute-start | bytes 122888 | tf_op jit(solution)/shard_map/ppermute | solution.py:318
  10.0 4.9 %collective-permute-start.4 = (bf16[128,128]{1,0:T(8,128)(2,1)S(1)}, bf16[128,128]{1,0:T(8,128)(2,1)S(1)}, u32[]{:S(2)}, u32[]{:S(2)}) collective-permute-start(bf16[128,128]{1,0:T(8,128)(2,1)S(1)} %constant_dynamic-update-slice_fusion.refs_1_), channel_id=1, source_target_pairs={{0,8},{1,9},{2,10},{3,11},{4,12},{5,13},{6,14},{7,15},{8,0},{9,1},... | collective-permute-start | bytes 98312 | tf_op jit(solution)/shard_map/ppermute | solution.py:62
  14.9 1.4 %collective-permute-start.5 = (bf16[416,128]{1,0:T(8,128)(2,1)S(1)}, bf16[416,128]{1,0:T(8,128)(2,1)S(1)}, u32[]{:S(2)}, u32[]{:S(2)}) collective-permute-start(bf16[416,128]{1,0:T(8,128)(2,1)S(1)} %pack.1), channel_id=1, source_target_pairs={{0,1},{1,0},{2,3},{3,2},{4,5},{5,4},{6,7},{7,6},{8,9},{9,8},{10,11... | collective-permute-start | bytes 319496 | tf_op jit(solution)/shard_map/ppermute | solution.py:62

commit v3 on v2

v3 whole, which is shorter than its diff:
```python
import functools

import jax
import jax.numpy as jnp
from jax import lax
from jax.experimental import pallas as pl
from jax.experimental.pallas import tpu as pltpu
from jax.sharding import PartitionSpec as P

ROOT_HALF = 0.7071067811865476
OFFSETS = (-3, -2, 2, 3)
AXES = ("leaf", "sub")
BF = jnp.bfloat16
F32 = jnp.float32
LANES = 64


def mm(a, b):
    return lax.dot_general(a, b, (((1,), (0,)), ((), ())), preferred_element_type=F32)


def mm_t(a, b):
    return lax.dot_general(a, b, (((1,), (1,)), ((), ())), preferred_element_type=F32)


def split(a):
    high = a.astype(BF)
    low = (a - high.astype(F32)).astype(BF)
    return jnp.concatenate([high, low], axis=0)


def mm2(a, b, product=mm):
    out = product(split(a), b)
    return out[: a.shape[0]] + out[a.shape[0] :]


def halves(a, axis):
    high = a.astype(BF)
    return jnp.concatenate([high, (a - high.astype(F32)).astype(BF)], axis=axis)


def side(*parts):
    return jnp.concatenate(parts, axis=1)


def stack(*parts):
    return jnp.concatenate(parts, axis=0)


def stages_of(devices):
    bits = [1 << b for b in range(1, devices.bit_length() - 1)]
    rounds = [(bits.pop() | 1,)] if len(bits) % 2 else []
    while bits:
        high, low = bits.pop(), bits.pop()
        rounds.append((low | 1, high | 1, low | high))
    return rounds + [(1,)]


def slots_of(stages):
    held = [[0]]
    for masks in stages:
        held.append(held[-1] + [slot ^ m for m in masks for slot in held[-1]])
    return held


def exchanged(x, apart):
    devices = lax.axis_size(AXES)
    return lax.ppermute(x, AXES, [(i, i ^ apart) for i in range(devices)])


def across_pairs(x):
    groups, devices = lax.axis_size("groups"), lax.axis_size(AXES)
    pairs = []
    for g in range(groups):
        for i in range(devices):
            j = i + 1 if i % 2 else i - 1
            to = (g, j) if 0 <= j < devices else ((g + 1) % groups, i)
            pairs.append((g * devices + i, to[0] * devices + to[1]))
    return lax.ppermute(x, ("groups", *AXES), pairs)


def load_kernel(count, *refs):
    copies = [
        pltpu.make_async_copy(refs[i], refs[count + i], refs[-1].at[i]) for i in range(count)
    ]
    for copy in copies:
        copy.start()
    for copy in copies:
        copy.wait()


def up_kernel(x, bases, transfer, facing, away, own0, own1, own2):
    leaves, rank, size = bases.shape
    rows = x.shape[0]
    up = [mm_t(x[:, i * size : (i + 1) * size], bases[i]) for i in range(leaves)]
    pairs = [side(up[i], up[i + 1]) for i in range(0, leaves, 2)]
    u0 = stack(*pairs)
    own0[...] = u0.astype(BF)
    up1 = mm2(u0, transfer[0].reshape(2 * rank, rank)) * ROOT_HALF
    up1 = [up1[i * rows : (i + 1) * rows] for i in range(leaves // 2)]
    pairs1 = [side(up1[i], up1[i + 1]) for i in range(0, leaves // 2, 2)]
    u1 = stack(*pairs1)
    own1[...] = u1.astype(BF)
    up2 = mm2(u1, transfer[1].reshape(2 * rank, rank)) * ROOT_HALF
    u2 = side(up2[:rows], up2[rows:]).astype(BF)
    own2[...] = u2
    half = size // 2
    end = leaves * size
    right = stack(
        x[:, end - size : end - half],
        x[:, end - half : end],
        pairs[-1].astype(BF),
        pairs1[-1].astype(BF),
        side(up[-3], up1[-3]).astype(BF),
        u2,
    )
    left = stack(
        x[:, :half],
        x[:, half:size],
        pairs[0].astype(BF),
        pairs1[0].astype(BF),
        side(up[2], up1[2]).astype(BF),
        u2,
    )
    even = lax.axis_index(AXES) % 2 == 0
    facing[...] = jnp.where(even, right, left)
    away[...] = jnp.where(even, left, right)


def pack_kernel(after, *refs):
    *parts, out = refs
    at = 0
    for part in parts:
        out[at : at + part.shape[0]] = part[...]
        at += part.shape[0]


def sides_of(facing, away):
    p = lax.axis_index(AXES)
    even = p % 2 == 0
    away = jnp.where((p > 0) & (p < lax.axis_size(AXES) - 1), away, jnp.zeros_like(away))
    return jnp.where(even, away, facing), jnp.where(even, facing, away)


def near_kernel(facing, away, x, blocks, near):
    leaves, _, size, _ = blocks.shape
    rows = x.shape[0]
    left, right = sides_of(facing[: 2 * rows], away[: 2 * rows])
    before = side(left[:rows], left[rows:])
    after = side(right[:rows], right[rows:])
    at = lambda i: before if i < 0 else after if i == leaves else x[:, i * size : (i + 1) * size]
    for i in range(leaves):
        total = mm_t(at(i), blocks[i, 1])
        total += mm_t(at(i - 1), blocks[i, 0])
        total += mm_t(at(i + 1), blocks[i, 2])
        near[:, i * size : (i + 1) * size] = total


def mask_of(codes, level, leaves):
    p = lax.axis_index(AXES)
    wide = codes.shape[2]
    lanes = lax.broadcasted_iota(jnp.int32, (8, 4 * LANES), 1) // LANES
    offset = jnp.where(lanes < 2, lanes - 3, lanes)
    cluster = lax.broadcasted_iota(jnp.int32, (8, 4 * LANES), 0)
    diagonal = lax.broadcasted_iota(jnp.int32, (8, wide), 0) == lax.broadcasted_iota(jnp.int32, (8, wide), 1)
    count = leaves >> level
    index = p * count if count > 0 else p >> level - (leaves.bit_length() - 1)
    hit = jnp.zeros(lanes.shape, jnp.bool_)
    for slot in range(codes.shape[1]):
        row = jnp.broadcast_to(codes[level, slot : slot + 1], (8, wide))
        row = pltpu.roll(row, lax.rem(wide - index, wide), 1)
        code = jnp.sum(jnp.where(diagonal, row, 0).astype(F32), axis=1, keepdims=True)
        hit = hit | (lanes.astype(F32) == code)
    partner = index + cluster + offset
    hit = hit & (partner >= 0) & (partner < wide >> level)
    return jnp.where(hit, 1.0, 0.0)


def plan_kernel(
    levels, facing, away, own0, own1, own2, codes, transfer, couple, state, spread, links_out, masks, *lifts
):
    rows = own2.shape[0]
    rank = transfer.shape[-1]
    leaves = own0.shape[0] // rows * 2
    p = lax.axis_index(AXES)
    table = lambda level: transfer[level].reshape(2 * rank, rank)
    links = lambda level: couple[level].reshape(4 * rank, rank)
    lo = slice(0, rank)
    hi = slice(rank, 2 * rank)
    left, right = sides_of(facing[...], away[...])
    block = lambda a, i: a[i * rows : (i + 1) * rows]

    mask = [mask_of(codes, level, leaves) for level in range(3 + levels)]
    masks[:8] = mask[2]
    for k in range(levels):
        masks[8 * (k + 1) : 8 * (k + 2)] = mask[3 + k]

    def coupled(level, ext, count):
        weights = mask[level].astype(BF)
        lhs = [side(*[ext[c + 3 + o] for o in OFFSETS]) * weights[c : c + 1] for c in range(count)]
        return mm(stack(*lhs), links(level))

    zero = jnp.zeros((rows, rank), BF)
    ext = [zero, block(left, 5)[:, lo], block(left, 5)[:, hi], zero, zero]
    ext += [block(right, 5)[:, lo], block(right, 5)[:, hi], zero]
    far2 = coupled(2, ext, 2)
    ext = [block(left, 4)[:, hi], block(left, 3)[:, lo], block(left, 3)[:, hi]]
    ext += [block(own1, c // 2)[:, (lo, hi)[c % 2]] for c in range(leaves // 2)]
    ext += [block(right, 3)[:, lo], block(right, 3)[:, hi], block(right, 4)[:, hi]]
    far1 = coupled(1, ext, leaves // 2)
    ext = [block(left, 4)[:, lo], block(left, 2)[:, lo], block(left, 2)[:, hi]]
    ext += [block(own0, c // 2)[:, (lo, hi)[c % 2]] for c in range(leaves)]
    ext += [block(right, 2)[:, lo], block(right, 2)[:, hi], block(right, 4)[:, lo]]
    far0 = coupled(0, ext, leaves)

    def lowered(value, level, size):
        out = mm2(value, table(level), mm_t)
        return stack(*[out[c // 2 * size : (c // 2 + 1) * size, (lo, hi)[c % 2]] for c in range(2 * (out.shape[0] // size))])

    down = far0 + lowered(far1 + lowered(far2, 1, rows), 0, rows)
    state[...] = side(*[block(down, c) for c in range(leaves)])

    first = couple[2, 0].astype(F32)
    second = couple[2, 3].astype(F32)
    eye = lowered(transfer[2, 0].astype(F32).T, 1, rank)
    one = lowered(transfer[2, 1].astype(F32).T, 1, rank)
    both = lowered(stack(eye, one), 0, rank)
    both = side(*[both[c * rank : (c + 1) * rank] for c in range(leaves)])
    high = both.astype(BF)
    spread[:rank] = high
    spread[rank : 2 * rank] = high
    spread[2 * rank : 3 * rank] = (both - high.astype(F32)).astype(BF)
    half = leaves // 2
    for i, start in enumerate((first, second)):
        out = lowered(lowered(start, 1, rank), 0, rank)
        out = side(*[out[c * rank : (c + 1) * rank] for c in range(half)]).astype(BF)
        none = jnp.zeros_like(out)
        spread[(3 + i) * rank : (4 + i) * rank] = side(out, none) if i == 0 else side(none, out)

    for k in range(levels):
        value = links(3 + k).astype(F32)
        for i in reversed(range(k)):
            value = mm2(value, transfer[3 + i, (p >> i) & 1], mm_t)
        links_out[4 * rank * k : 4 * rank * (k + 1)] = halves(value, 1)

    parts = [table(2).astype(F32) * ROOT_HALF]
    for k, lift in enumerate(lifts):
        b = (p >> k) & 1
        parts = [mm2(a, transfer[3 + k, bit]) * ROOT_HALF for bit in (b, 1 - b) for a in parts]
        lift[...] = halves(stack(*parts), 1)


def climb(up, count, transfer, level, bit, rows):
    rank = up.shape[1]
    pairs = up.reshape(count // 2, 2, rows, rank)
    children = [pairs[:, i].reshape(count // 2 * rows, rank) for i in range(2)]
    turned = stack(transfer[level, bit], transfer[level, 1 - bit])
    return mm2(side(*children), turned) * ROOT_HALF


def down_kernel(devices, stages, levels, *refs):
    refs = list(refs)
    own2 = refs.pop(0)
    received = []
    for group in stages:
        received.append(refs[: len(group)])
        refs = refs[len(group) :]
    lifts = [refs.pop(0) for _ in range(min(levels - 1, 2))]
    state, spread, links, masks, transfer, bases, near, out, gathered, *ups = refs
    leaves, rank, size = bases.shape
    rows = own2.shape[0]
    p = lax.axis_index(AXES)

    gathered[0] = own2[...]
    for group, got, held in zip(stages, received, slots_of(stages)):
        for m, ref in zip(group, got):
            for i, slot in enumerate(held):
                gathered[slot ^ m] = ref[i * rows : (i + 1) * rows]

    every = gathered[...]
    for k in range(levels):
        count = devices >> k
        if k == 0:
            up = mm(every.reshape(devices * rows, 2 * rank), transfer[2].reshape(2 * rank, rank)) * ROOT_HALF
        elif k <= len(lifts):
            sets = every.reshape(count, 1 << k, rows, 2 * rank)
            sets = side(*[sets[:, i].reshape(count * rows, 2 * rank) for i in range(1 << k)])
            up = mm(sets, lifts[k - 1][...])
            up = up[:, :rank] + up[:, rank:]
        else:
            up = climb(up, 2 * count, transfer, 2 + k, (p >> (k - 1)) & 1, rows)
        ups[k][...] = up.reshape(count, rows, rank)

    lhs = []
    for k in range(levels):
        a = p >> k
        n = devices >> k
        parts = [ups[k][a ^ jnp.clip(a + o, 0, n - 1)] for o in OFFSETS]
        lhs.append(side(*parts) * masks[8 * (k + 1) : 8 * (k + 1) + 1])
    top = mm(halves(side(*lhs), 0), links[...])
    top = top[:rows, :rank] + top[:rows, rank:] + top[rows:, :rank] + top[rows:, rank:]

    at = lambda o: gathered[p ^ jnp.clip(p + o, 0, devices - 1)]
    weights = masks[:8].astype(BF)
    before = at(-2)[:, rank:] * weights[0:1, :rank]
    after = at(2)[:, :rank] * weights[1:2, 3 * rank :]
    lhs = side(halves(top, 1), top.astype(BF), before, after)
    coef = (mm(lhs, spread[...]) + state[...]).astype(BF)
    for c in range(leaves):
        cols = slice(c * size, (c + 1) * size)
        out[:, cols] = (mm(coef[:, c * rank : (c + 1) * rank], bases[c]) + near[:, cols]).astype(BF)


def inside(x):
    return pltpu.with_memory_space_constraint(x, pltpu.VMEM)


def outside(x):
    return pltpu.with_memory_space_constraint(x, pltpu.HBM)


def shards(rhs, bases, near_blocks, transfer, couple, codes):
    rows = rhs.shape[0]
    leaves, rank, size = bases.shape
    devices = lax.axis_size(AXES)
    stages = stages_of(devices)
    levels = devices.bit_length() - 2
    params = pltpu.CompilerParams(vmem_limit_bytes=16 << 20)

    def call(kernel, shapes, operands, name, flops=0, place=inside, **more):
        single = not isinstance(shapes, list)
        return pl.pallas_call(
            kernel,
            out_shape=shapes if single else list(shapes),
            compiler_params=params,
            cost_estimate=pl.CostEstimate(flops=flops, bytes_accessed=1 << 20, transcendentals=0),
            name=name,
            **more,
        )(*map(place, operands))

    loaded = (rhs, bases, transfer, codes)
    x, bases, transfer, codes = call(
        functools.partial(load_kernel, len(loaded)),
        [pltpu.VMEM(a.shape, a.dtype) for a in loaded],
        loaded,
        "load",
        place=outside,
        in_specs=[pl.BlockSpec(memory_space=pl.ANY)] * len(loaded),
        scratch_shapes=[pltpu.SemaphoreType.DMA((len(loaded),))],
    )
    facing, away, own0, own1, own2 = call(
        up_kernel,
        [
            pltpu.VMEM((6 * rows, 2 * rank), BF),
            pltpu.VMEM((6 * rows, 2 * rank), BF),
            pltpu.VMEM((leaves // 2 * rows, 2 * rank), BF),
            pltpu.VMEM((leaves // 4 * rows, 2 * rank), BF),
            pltpu.VMEM((rows, 2 * rank), BF),
        ],
        (x, bases, transfer),
        "up_sweep",
        1 << 32,
    )

    facing = exchanged(facing, 1)
    away = across_pairs(away)

    lifts = [pltpu.VMEM(((2 << k) * 2 * rank, 2 * rank), BF) for k in range(min(levels - 1, 2))]
    state, spread, links, masks, *lifts = call(
        functools.partial(plan_kernel, levels),
        [
            pltpu.VMEM((rows, leaves * rank), F32),
            pltpu.VMEM((5 * rank, leaves * rank), BF),
            pltpu.VMEM((levels * 4 * rank, 2 * rank), BF),
            pltpu.VMEM((8 * (levels + 1), 4 * rank), F32),
            *lifts,
        ],
        (facing, away, own0, own1, own2, codes, transfer, couple),
        "plan",
        1 << 30,
    )
    near = call(
        near_kernel,
        pltpu.VMEM((rows, leaves * size), F32),
        (facing, away, x, near_blocks),
        "near_field",
        3 * leaves * rows * size * size * 2,
    )

    received = []
    gathered = own2
    for group in stages[:-1]:
        got = [exchanged(gathered, m) for m in group]
        received.append(got)
        if group is not stages[-2]:
            gathered = stack(gathered, *got)
    parts = (gathered, *(received[-1] if received else ()))
    pay = call(
        pack_kernel,
        pltpu.VMEM((sum(part.shape[0] for part in parts), 2 * rank), BF),
        (masks, *parts),
        "pack",
    )
    received.append([exchanged(pay, 1)])

    flat = [g for got in received for g in got]
    return call(
        functools.partial(down_kernel, devices, stages, levels),
        jax.ShapeDtypeStruct((rows, leaves * size), BF),
        (own2, *flat, *lifts, state, spread, links, masks, transfer, bases, near),
        "down_sweep",
        scratch_shapes=[pltpu.VMEM((devices, rows, 2 * rank), BF)]
        + [pltpu.VMEM((devices >> k, rows, rank), F32) for k in range(levels)],
    )


def solution(mesh):
    return jax.shard_map(
        shards,
        mesh=mesh,
        in_specs=(
            P(None, ("groups", "leaf", "sub")),
            P(("groups", "leaf", "sub"), None, None),
            P(("groups", "leaf", "sub"), None, None, None),
            P(),
            P(),
            P(),
        ),
        out_specs=P(None, ("groups", "leaf", "sub")),
        check_vma=False,
    )
```

time: 19 us -> 16.4 us (0.86)
  waiting for transfers between devices: 5.37 us -> 0.46 us
  starting transfers between devices: 7.99 us -> 9.29 us
  Pallas kernels: 5.39 us -> 6.45 us
    ppermute x5 -> x6, waiting for transfers between devices: 5.37 us -> 0.46 us  [exchanged(): return lax.ppermute(x, AXES, [(i, i ^ apart) for i in range(devices)])]
    pallas_call x5 -> x6, Pallas kernels: 5.39 us -> 6.45 us  [call(): pl.pallas_call(kernel, out_shape=shapes if single else list(shapes), comp...]
    ppermute x1, starting transfers between devices: 0.65 us -> 1.52 us  [across_pairs(): return lax.ppermute(x, ('groups', *AXES), pairs)]
    ppermute x5 -> x6, starting transfers between devices: 7.34 us -> 7.77 us  [exchanged(): return lax.ppermute(x, AXES, [(i, i ^ apart) for i in range(devices)])]
  transfers between devices with their start and end apart: 6 -> 7, of which waited for: 3 -> 2; matrix products, arithmetic and copies ran while one was open for 0% -> 0% of each run, Pallas kernels for 5% -> 18%
where the time goes in v3:
time: 16.4 us; the launch traced here: 16.3 us
  starting transfers between devices  9.29 us (57%)
  Pallas kernels  6.45 us (39%)
  waiting for transfers between devices  0.46 us (3%)
    ppermute x6, starting transfers between devices, exchanged(): return lax.ppermute(x, AXES, [(i, i ^ apart) for i in range(devices)])  7.77 us
    pallas_call x6, Pallas kernels, call(): pl.pallas_call(kernel, out_shape=shapes if single else list(shapes), comp...  6.45 us
    ppermute x1, starting transfers between devices, across_pairs(): return lax.ppermute(x, ('groups', *AXES), pairs)  1.52 us
    ppermute x6, waiting for transfers between devices, exchanged(): return lax.ppermute(x, AXES, [(i, i ^ apart) for i in range(devices)])  0.46 us
  transfers between devices with their start and end apart: 7, of which 2 were waited for; matrix products, arithmetic and copies ran while one was open for 0% of the time, Pallas kernels for 18%

profile of v3, /device:TPU:0, one launch (start us, length us, event | category | flops | bytes accessed | tf_op | source)
XLA Modules:
  0.0 16.3 jit_solution(7273090569092049258)
XLA Ops:
  0.0 1.2 %load.1 = (bf16[32,2048]{1,0:T(8,128)(2,1)S(1)}, bf16[8,64,256]{2,1,0:T(8,128)(2,1)S(1)}, bf16[12,2,64,64]{3,2,1,0:T(8,128)(2,1)S(1)}, s32[12,3,128]{2,1,0:T(4,128)S(1)}) custom-call(bf16[32,2048]{1,0:T(8,128)(2,1)} %refs_0_.1, bf16[8,64,256]{2,1,0:T(8,128)(2,1)} %refs_1_.1, bf16[12,2,64,64]{3,2,1,0:T(8,128)(2,1)} %refs_2_.1, s32[12,3,128]{2,1,0:T(4,128)} %refs_3_.1), custom_call_target="tpu_custom_call" | custom-call | bytes 1048576 | tf_op jit(solution)/shard_map/load/pallas_call | solution.py:332
  1.2 0.0 copy-start.1
  1.2 0.7 %up_sweep.1 = (bf16[192,128]{1,0:T(8,128)(2,1)S(1)}, bf16[192,128]{1,0:T(8,128)(2,1)S(1)}, bf16[128,128]{1,0:T(8,128)(2,1)S(1)}, bf16[64,128]{1,0:T(8,128)(2,1)S(1)}, bf16[32,128]{1,0:T(8,128)(2,1)S(1)}) custom-call(bf16[32,2048]{1,0:T(8,128)(2,1)S(1)} %get-tuple-element.20.x, bf16[8,64,256]{2,1,0:T(8,128)(2,1)S(1)} %get-tuple-element.21.bases.refs_13_, ...), custom_call_target="tpu_custom_call" | custom-call | flops 4294967296 | bytes 1048576 | tf_op jit(solution)/shard_map/up_sweep/pallas_call | solution.py:332
  1.9 0.0 copy-start
  1.9 3.5 %collective-permute-start = (bf16[32,128]{1,0:T(8,128)(2,1)S(1)}, bf16[32,128]{1,0:T(8,128)(2,1)S(1)}, u32[]{:S(2)}, u32[]{:S(2)}) collective-permute-start(bf16[32,128]{1,0:T(8,128)(2,1)S(1)} %get-tuple-element.23.own2.refs_0_), channel_id=1, source_target_pairs={{0,9},{1,8},{2,11},{3,10},{4,13},{5,12},{6,15},{7,14},{8,1},{9,0},... | collective-permute-start | bytes 24584 | tf_op jit(solution)/shard_map/ppermute | solution.py:68
  5.4 0.7 %collective-permute-start.4 = (bf16[192,128]{1,0:T(8,128)(2,1)S(1)}, bf16[192,128]{1,0:T(8,128)(2,1)S(1)}, u32[]{:S(2)}, u32[]{:S(2)}) collective-permute-start(bf16[192,128]{1,0:T(8,128)(2,1)S(1)} %get-tuple-element.24), channel_id=1, source_target_pairs={{0,1},{1,0},{2,3},{3,2},{4,5},{5,4},{6,7},{7,6},{8,9},{9,8},{10,11... | collective-permute-start | bytes 147464 | tf_op jit(solution)/shard_map/ppermute | solution.py:68
  6.0 1.5 %collective-permute-start.5 = (bf16[192,128]{1,0:T(8,128)(2,1)S(1)}, bf16[192,128]{1,0:T(8,128)(2,1)S(1)}, u32[]{:S(2)}, u32[]{:S(2)}) collective-permute-start(bf16[192,128]{1,0:T(8,128)(2,1)S(1)} %get-tuple-element.25), channel_id=1, source_target_pairs={{0,16},{1,2},{2,1},{3,4},{4,3},{5,6},{6,5},{7,8},{8,7},{9,10},{10,... | collective-permute-start | bytes 147464 | tf_op jit(solution)/shard_map/ppermute | solution.py:79
  7.6 0.0 collective-permute-done.refs_1_
  7.6 2.2 %collective-permute-start.3 = (bf16[64,128]{1,0:T(8,128)(2,1)S(1)}, bf16[64,128]{1,0:T(8,128)(2,1)S(1)}, u32[]{:S(2)}, u32[]{:S(2)}) collective-permute-start(bf16[64,128]{1,0:T(8,128)(2,1)S(1)} %constant_dynamic-update-slice_fusion.refs_0_), channel_id=1, source_target_pairs={{0,6},{1,7},{2,4},{3,5},{4,2},{5,3},{6,0},{7,1},{8,14},{9,15},{10,... | collective-permute-start | bytes 49160 | tf_op jit(solution)/shard_map/ppermute | solution.py:68
  9.8 0.2 %collective-permute-start.2 = (bf16[64,128]{1,0:T(8,128)(2,1)S(1)}, bf16[64,128]{1,0:T(8,128)(2,1)S(1)}, u32[]{:S(2)}, u32[]{:S(2)}) collective-permute-start(bf16[64,128]{1,0:T(8,128)(2,1)S(1)} %constant_dynamic-update-slice_fusion.refs_0_), channel_id=1, source_target_pairs={{0,5},{1,4},{2,7},{3,6},{4,1},{5,0},{6,3},{7,2},{8,13},{9,12},{10,... | collective-permute-start | bytes 49160 | tf_op jit(solution)/shard_map/ppermute | solution.py:68
  10.1 0.8 %collective-permute-start.1 = (bf16[64,128]{1,0:T(8,128)(2,1)S(1)}, bf16[64,128]{1,0:T(8,128)(2,1)S(1)}, u32[]{:S(2)}, u32[]{:S(2)}) collective-permute-start(bf16[64,128]{1,0:T(8,128)(2,1)S(1)} %constant_dynamic-update-slice_fusion.refs_0_), channel_id=1, source_target_pairs={{0,3},{1,2},{2,1},{3,0},{4,7},{5,6},{6,5},{7,4},{8,11},{9,10},{10,... | collective-permute-start | bytes 49160 | tf_op jit(solution)/shard_map/ppermute | solution.py:68
  10.8 0.0 collective-permute-done.4.facing
  10.9 0.0 collective-permute-done.5.away
  10.9 0.0 copy-done.1
  10.9 1.9 %plan.1 = (f32[32,512]{1,0:T(8,128)S(1)}, bf16[320,512]{1,0:T(8,128)(2,1)S(1)}, bf16[768,128]{1,0:T(8,128)(2,1)S(1)}, f32[32,256]{1,0:T(8,128)S(1)}, bf16[256,12...) custom-call(bf16[192,128]{1,0:T(8,128)(2,1)S(1)} %collective-permute-done.4.facing, ...), custom_call_target="tpu_custom_call" | custom-call | flops 1073741824 | bytes 1048576 | tf_op jit(solution)/shard_map/plan/pallas_call | solution.py:332
  12.8 0.0 collective-permute-done.3.refs_3_.refs_4_
  12.8 0.4 %collective-permute-done.2.refs_2_.refs_3_ = bf16[64,128]{1,0:T(8,128)(2,1)S(1)} collective-permute-done((bf16[64,128]{1,0:T(8,128)(2,1)S(1)}, bf16[64,128]{1,0:T(8,128)(2,1)S(1)}, u32[]{:S(2)}, u32[]{:S(2)}) %collective-permute-start.2) | collective-permute-done | bytes 16416 | tf_op jit(solution)/shard_map/ppermute | solution.py:68
  13.1 0.1 collective-permute-done.1.refs_1_.refs_2_
  13.2 0.3 %collective-permute-start.6 = (bf16[256,128]{1,0:T(8,128)(2,1)S(1)}, bf16[256,128]{1,0:T(8,128)(2,1)S(1)}, u32[]{:S(2)}, u32[]{:S(2)}) collective-permute-start(bf16[256,128]{1,0:T(8,128)(2,1)S(1)} %pack.1), channel_id=1, source_target_pairs={{0,1},{1,0},{2,3},{3,2},{4,5},{5,4},{6,7},{7,6},{8,9},{9,8},{10,11... | collective-permute-start | bytes 196616 | tf_op jit(solution)/shard_map/ppermute | solution.py:68
  13.6 0.0 copy-done
  13.6 1.0 %near_field.1.refs_14_ = f32[32,2048]{1,0:T(8,128)S(1)} custom-call(bf16[192,128]{1,0:T(8,128)(2,1)S(1)} %collective-permute-done.4.facing, bf16[192,128]{1,0:T(8,128)(2,1)S(1)} %collective-permute-done.5.away, bf16[32,2048]{1,0:T(8,128)(2,1)S(1)} %get-tuple-element.20.x, bf16[8,3,256,256]{3,2,1,0:T(8,128)(2,1)S(1)} %copy-done), custom_call_target="tpu_custom_call" | custom-call | flops 100663296 | bytes 1048576 | tf_op jit(solution)/shard_map/near_field/pallas_call | solution.py:332
  14.6 0.0 collective-permute-done.6.refs_5_
  14.6 1.7 %down_sweep.1 = bf16[32,2048]{1,0:T(8,128)(2,1)} custom-call(bf16[32,128]{1,0:T(8,128)(2,1)S(1)} %get-tuple-element.23.own2.refs_0_, bf16[32,128]{1,0:T(8,128)(2,1)S(1)} %collective-permute-done.refs_1_, bf16[64,128]{1,0:T(8,128)(2,1)S(1)} %collective-permute-done.1.refs_1_.refs_2_, bf16[64,128]{1,0:T(8,128)(2,1)S(1)} %collective-permute-done.2.refs_2_.refs_3_, ...), custom_call_target="tpu_custom_call" | custom-call | bytes 1048576 | tf_op jit(solution)/shard_map/down_sweep/pallas_call | solution.py:332
  (3 shorter events, 0.0 us)
Async XLA Ops:
  1.2 9.7 %copy-start.1 = (bf16[12,4,64,64]{3,2,1,0:T(8,128)(2,1)S(1)}, bf16[12,4,64,64]{3,2,1,0:T(8,128)(2,1)}, u32[]{:S(2)}) copy-start(bf16[12,4,64,64]{3,2,1,0:T(8,128)(2,1)} %couple.1) | copy-start | bytes 1179652
  1.9 11.7 %copy-start = (bf16[8,3,256,256]{3,2,1,0:T(8,128)(2,1)S(1)}, bf16[8,3,256,256]{3,2,1,0:T(8,128)(2,1)}, u32[]{:S(2)}) copy-start(bf16[8,3,256,256]{3,2,1,0:T(8,128)(2,1)} %blocks.1) | copy-start | bytes 9437188
  1.9 5.7 %collective-permute-start = (bf16[32,128]{1,0:T(8,128)(2,1)S(1)}, bf16[32,128]{1,0:T(8,128)(2,1)S(1)}, u32[]{:S(2)}, u32[]{:S(2)}) collective-permute-start(bf16[32,128]{1,0:T(8,128)(2,1)S(1)} %get-tuple-element.23.own2.refs_0_), channel_id=1, source_target_pairs={{0,9},{1,8},{2,11},{3,10},{4,13},{5,12},{6,15},{7,14},{8,1},{9,0},... | collective-permute-start | bytes 24584 | tf_op jit(solution)/shard_map/ppermute | solution.py:68
  5.4 5.5 %collective-permute-start.4 = (bf16[192,128]{1,0:T(8,128)(2,1)S(1)}, bf16[192,128]{1,0:T(8,128)(2,1)S(1)}, u32[]{:S(2)}, u32[]{:S(2)}) collective-permute-start(bf16[192,128]{1,0:T(8,128)(2,1)S(1)} %get-tuple-element.24), channel_id=1, source_target_pairs={{0,1},{1,0},{2,3},{3,2},{4,5},{5,4},{6,7},{7,6},{8,9},{9,8},{10,11... | collective-permute-start | bytes 147464 | tf_op jit(solution)/shard_map/ppermute | solution.py:68
  6.0 4.8 %collective-permute-start.5 = (bf16[192,128]{1,0:T(8,128)(2,1)S(1)}, bf16[192,128]{1,0:T(8,128)(2,1)S(1)}, u32[]{:S(2)}, u32[]{:S(2)}) collective-permute-start(bf16[192,128]{1,0:T(8,128)(2,1)S(1)} %get-tuple-element.25), channel_id=1, source_target_pairs={{0,16},{1,2},{2,1},{3,4},{4,3},{5,6},{6,5},{7,8},{8,7},{9,10},{10,... | collective-permute-start | bytes 147464 | tf_op jit(solution)/shard_map/ppermute | solution.py:79
  7.6 5.2 %collective-permute-start.3 = (bf16[64,128]{1,0:T(8,128)(2,1)S(1)}, bf16[64,128]{1,0:T(8,128)(2,1)S(1)}, u32[]{:S(2)}, u32[]{:S(2)}) collective-permute-start(bf16[64,128]{1,0:T(8,128)(2,1)S(1)} %constant_dynamic-update-slice_fusion.refs_0_), channel_id=1, source_target_pairs={{0,6},{1,7},{2,4},{3,5},{4,2},{5,3},{6,0},{7,1},{8,14},{9,15},{10,... | collective-permute-start | bytes 49160 | tf_op jit(solution)/shard_map/ppermute | solution.py:68
  9.8 3.3 %collective-permute-start.2 = (bf16[64,128]{1,0:T(8,128)(2,1)S(1)}, bf16[64,128]{1,0:T(8,128)(2,1)S(1)}, u32[]{:S(2)}, u32[]{:S(2)}) collective-permute-start(bf16[64,128]{1,0:T(8,128)(2,1)S(1)} %constant_dynamic-update-slice_fusion.refs_0_), channel_id=1, source_target_pairs={{0,5},{1,4},{2,7},{3,6},{4,1},{5,0},{6,3},{7,2},{8,13},{9,12},{10,... | collective-permute-start | bytes 49160 | tf_op jit(solution)/shard_map/ppermute | solution.py:68
  10.1 3.2 %collective-permute-start.1 = (bf16[64,128]{1,0:T(8,128)(2,1)S(1)}, bf16[64,128]{1,0:T(8,128)(2,1)S(1)}, u32[]{:S(2)}, u32[]{:S(2)}) collective-permute-start(bf16[64,128]{1,0:T(8,128)(2,1)S(1)} %constant_dynamic-update-slice_fusion.refs_0_), channel_id=1, source_target_pairs={{0,3},{1,2},{2,1},{3,0},{4,7},{5,6},{6,5},{7,4},{8,11},{9,10},{10,... | collective-permute-start | bytes 49160 | tf_op jit(solution)/shard_map/ppermute | solution.py:68
  13.2 1.3 %collective-permute-start.6 = (bf16[256,128]{1,0:T(8,128)(2,1)S(1)}, bf16[256,128]{1,0:T(8,128)(2,1)S(1)}, u32[]{:S(2)}, u32[]{:S(2)}) collective-permute-start(bf16[256,128]{1,0:T(8,128)(2,1)S(1)} %pack.1), channel_id=1, source_target_pairs={{0,1},{1,0},{2,3},{3,2},{4,5},{5,4},{6,7},{7,6},{8,9},{9,8},{10,11... | collective-permute-start | bytes 196616 | tf_op jit(solution)/shard_map/ppermute | solution.py:68

commit v4 on v3

v4 whole, which is shorter than its diff:
```python
import functools

import jax
import jax.numpy as jnp
from jax import lax
from jax.experimental import pallas as pl
from jax.experimental.pallas import tpu as pltpu
from jax.sharding import PartitionSpec as P

ROOT_HALF = 0.7071067811865476
OFFSETS = (-3, -2, 2, 3)
AXES = ("leaf", "sub")
BF = jnp.bfloat16
F32 = jnp.float32
LANES = 64


def mm(a, b):
    return lax.dot_general(a, b, (((1,), (0,)), ((), ())), preferred_element_type=F32)


def mm_t(a, b):
    return lax.dot_general(a, b, (((1,), (1,)), ((), ())), preferred_element_type=F32)


def split(a):
    high = a.astype(BF)
    low = (a - high.astype(F32)).astype(BF)
    return jnp.concatenate([high, low], axis=0)


def mm2(a, b, product=mm):
    out = product(split(a), b)
    return out[: a.shape[0]] + out[a.shape[0] :]


def halves(a, axis):
    high = a.astype(BF)
    return jnp.concatenate([high, (a - high.astype(F32)).astype(BF)], axis=axis)


def side(*parts):
    return jnp.concatenate(parts, axis=1)


def stack(*parts):
    return jnp.concatenate(parts, axis=0)


def stages_of(devices):
    bits = [1 << b for b in range(1, devices.bit_length() - 1)]
    rounds = [(bits.pop() | 1,)] if len(bits) % 2 else []
    while bits:
        high, low = bits.pop(), bits.pop()
        rounds.append((low | 1, high | 1, low | high))
    return rounds + [(1,)]


def slots_of(stages):
    held = [[0]]
    for masks in stages:
        so_far = [slot for part in held for slot in part]
        held += [[slot ^ m for slot in so_far] for m in masks]
    return held


def exchanged(x, apart):
    devices = lax.axis_size(AXES)
    return lax.ppermute(x, AXES, [(i, i ^ apart) for i in range(devices)])


def across_pairs(x):
    groups, devices = lax.axis_size("groups"), lax.axis_size(AXES)
    pairs = []
    for g in range(groups):
        for i in range(devices):
            j = i + 1 if i % 2 else i - 1
            to = (g, j) if 0 <= j < devices else ((g + 1) % groups, i)
            pairs.append((g * devices + i, to[0] * devices + to[1]))
    return lax.ppermute(x, ("groups", *AXES), pairs)


def first_kernel(rhs_hbm, bases_hbm, transfer_hbm, x, bases, low, leaf_coef, own2, sems):
    leaves, rank, size = bases.shape
    rows = x.shape[0]
    pairs = (
        (transfer_hbm.at[pl.ds(0, 2)], low),
        (bases_hbm, bases),
        (rhs_hbm, x),
    )
    copies = [pltpu.make_async_copy(*pair, sems.at[i]) for i, pair in enumerate(pairs)]
    for copy in copies:
        copy.start()
    copies[0].wait()
    table = low[0].reshape(2 * rank, rank)
    product = halves(stack(mm(table, low[1, 0]), mm(table, low[1, 1])) * (ROOT_HALF * ROOT_HALF), 1)
    copies[1].wait()
    copies[2].wait()
    at = lambda i: x[:, i * size : (i + 1) * size]
    first = lax.broadcasted_iota(jnp.int32, (rows, 2 * rank), 1) < rank
    parts = []
    for i in range(0, leaves, 2):
        both = mm_t(stack(at(i), at(i + 1)), bases[i : i + 2].reshape(2 * rank, size))
        parts.append(jnp.where(first, both[:rows], both[rows:]))
    leaf_coef[...] = stack(*parts)
    fours = stack(*[side(parts[i], parts[i + 1]) for i in range(0, leaves // 2, 2)])
    up = mm(halves(fours, 0), product)
    count = fours.shape[0]
    up = up[:count, :rank] + up[:count, rank:] + up[count:, :rank]
    own2[...] = side(*[up[i : i + rows] for i in range(0, count, rows)]).astype(BF)


def edges_kernel(leaf_coef, low, x, u2, facing, away, own0, own1):
    rank = low.shape[-1]
    rows = x.shape[0]
    own0[...] = leaf_coef[...].astype(BF)
    up1 = mm2(leaf_coef[...], low[0].reshape(2 * rank, rank)) * ROOT_HALF
    up1 = [up1[i : i + rows] for i in range(0, up1.shape[0], rows)]
    own1[...] = stack(*[side(up1[i], up1[i + 1]) for i in range(0, len(up1), 2)]).astype(BF)
    end = x.shape[1]
    size = end // (2 * len(up1))
    half = size // 2
    last0, last1 = own0.shape[0] - rows, own1.shape[0] - rows
    right = stack(
        x[:, end - size : end - half],
        x[:, end - half :],
        own0[last0:],
        own1[last1:],
        side(own0[last0 - rows : last0, rank:], own1[last1 - rows : last1, rank:]),
        u2[...],
    )
    left = stack(
        x[:, :half],
        x[:, half:size],
        own0[:rows],
        own1[:rows],
        side(own0[rows : 2 * rows, :rank], own1[rows : 2 * rows, :rank]),
        u2[...],
    )
    even = lax.axis_index(AXES) % 2 == 0
    facing[...] = jnp.where(even, right, left)
    away[...] = jnp.where(even, left, right)


def pack_kernel(after, *refs):
    *parts, out = refs
    at = 0
    for part in parts:
        out[at : at + part.shape[0]] = part[...]
        at += part.shape[0]


def mask_of(codes, level, leaves):
    p = lax.axis_index(AXES)
    wide = codes.shape[2]
    lanes = lax.broadcasted_iota(jnp.int32, (8, 4 * LANES), 1) // LANES
    offset = jnp.where(lanes < 2, lanes - 3, lanes)
    cluster = lax.broadcasted_iota(jnp.int32, (8, 4 * LANES), 0)
    diagonal = lax.broadcasted_iota(jnp.int32, (8, wide), 0) == lax.broadcasted_iota(jnp.int32, (8, wide), 1)
    count = leaves >> level
    index = p * count if count > 0 else p >> level - (leaves.bit_length() - 1)
    hit = jnp.zeros(lanes.shape, jnp.bool_)
    for slot in range(codes.shape[1]):
        row = jnp.broadcast_to(codes[level, slot : slot + 1], (8, wide))
        row = pltpu.roll(row, lax.rem(wide - index, wide), 1)
        code = jnp.sum(jnp.where(diagonal, row, 0).astype(F32), axis=1, keepdims=True)
        hit = hit | (lanes.astype(F32) == code)
    partner = index + cluster + offset
    hit = hit & (partner >= 0) & (partner < wide >> level)
    return jnp.where(hit, 1.0, 0.0)


def lowered(value, table, size):
    rank = value.shape[1]
    out = mm2(value, table, mm_t)
    parts = [out[i : i + size, j : j + rank] for i in range(0, out.shape[0], size) for j in (0, rank)]
    return stack(*parts)


def plan_kernel(facing, away, own0, own1, codes, transfer, couple, state, spread, links_out, masks, *lifts):
    rank = transfer.shape[-1]
    levels = masks.shape[0] // 8 - 3
    leaves = spread.shape[1] // rank
    p = lax.axis_index(AXES)
    table = lambda level: transfer[level].reshape(2 * rank, rank)
    beside = lambda rows: side(*[rows[i : i + rank] for i in range(0, rows.shape[0], rank)])

    mask = [mask_of(codes, level, leaves) for level in range(3 + levels)]
    masks[...] = stack(*mask)
    state[...] = couplings(facing, away, own0, own1, mask, transfer, couple)

    both = stack(transfer[2, 0].astype(F32).T, transfer[2, 1].astype(F32).T, couple[2, 0].astype(F32), couple[2, 3].astype(F32))
    both = beside(lowered(lowered(both, table(1), rank), table(0), rank))
    wide = leaves * rank
    high = both[:, :wide].astype(BF)
    spread[:rank] = high
    spread[rank : 2 * rank] = high
    spread[2 * rank : 3 * rank] = (both[:, :wide] - high.astype(F32)).astype(BF)
    first, second = both[:, wide : wide * 3 // 2].astype(BF), both[:, wide * 3 // 2 :].astype(BF)
    none = jnp.zeros_like(first)
    spread[3 * rank : 4 * rank] = side(first, none)
    spread[4 * rank :] = side(none, second)

    for k in range(levels):
        value = couple[3 + k].reshape(4 * rank, rank).astype(F32)
        for i in reversed(range(k)):
            value = mm2(value, transfer[3 + i, (p >> i) & 1], mm_t)
        links_out[4 * rank * k : 4 * rank * (k + 1)] = halves(value, 1)

    value = table(2).astype(F32) * ROOT_HALF
    for k, lift in enumerate(lifts):
        if k > 0:
            b = (p >> (k - 1)) & 1
            value = stack(*[mm2(value, transfer[2 + k, bit]) * ROOT_HALF for bit in (b, 1 - b)])
        lift[...] = halves(value, 1)


def sides_of(facing, away):
    p = lax.axis_index(AXES)
    even = p % 2 == 0
    away = jnp.where((p > 0) & (p < lax.axis_size(AXES) - 1), away, jnp.zeros_like(away))
    return jnp.where(even, away, facing), jnp.where(even, facing, away)


def near_kernel(facing, away, x, blocks, near):
    leaves, _, size, _ = blocks.shape
    rows = x.shape[0]
    left, right = sides_of(facing[: 2 * rows], away[: 2 * rows])
    before = side(left[:rows], left[rows:])
    after = side(right[:rows], right[rows:])
    at = lambda i: before if i < 0 else after if i == leaves else x[:, i * size : (i + 1) * size]
    for i in range(leaves):
        total = mm_t(at(i), blocks[i, 1])
        total += mm_t(at(i - 1), blocks[i, 0])
        total += mm_t(at(i + 1), blocks[i, 2])
        near[:, i * size : (i + 1) * size] = total


def couplings(facing, away, own0, own1, mask, transfer, couple):
    rank = transfer.shape[-1]
    leaves = mask[0].shape[0]
    rows = own0.shape[0] // leaves * 2
    table = lambda level: transfer[level].reshape(2 * rank, rank)
    left, right = sides_of(facing[...], away[...])
    block = lambda a, i: a[i * rows : (i + 1) * rows]
    lo = slice(0, rank)
    hi = slice(rank, 2 * rank)

    def coupled(level, ext, count):
        weights = mask[level].astype(BF)
        lhs = [side(*[ext[c + 3 + o] for o in OFFSETS]) * weights[c : c + 1] for c in range(count)]
        return mm(stack(*lhs), couple[level].reshape(4 * rank, rank))

    zero = jnp.zeros((rows, rank), BF)
    ext = [zero, block(left, 5)[:, lo], block(left, 5)[:, hi], zero, zero]
    ext += [block(right, 5)[:, lo], block(right, 5)[:, hi], zero]
    far2 = coupled(2, ext, 2)
    ext = [block(left, 4)[:, hi], block(left, 3)[:, lo], block(left, 3)[:, hi]]
    ext += [block(own1, c // 2)[:, (lo, hi)[c % 2]] for c in range(leaves // 2)]
    ext += [block(right, 3)[:, lo], block(right, 3)[:, hi], block(right, 4)[:, hi]]
    far1 = coupled(1, ext, leaves // 2)
    ext = [block(left, 4)[:, lo], block(left, 2)[:, lo], block(left, 2)[:, hi]]
    ext += [block(own0, c // 2)[:, (lo, hi)[c % 2]] for c in range(leaves)]
    ext += [block(right, 2)[:, lo], block(right, 2)[:, hi], block(right, 4)[:, lo]]
    far0 = coupled(0, ext, leaves)
    down = far0 + lowered(far1 + lowered(far2, table(1), rows), table(0), rows)
    return side(*[block(down, c) for c in range(leaves)])


def climb(up, count, transfer, level, bit, rows):
    rank = up.shape[1]
    pairs = up.reshape(count // 2, 2, rows, rank)
    children = [pairs[:, i].reshape(count // 2 * rows, rank) for i in range(2)]
    turned = stack(transfer[level, bit], transfer[level, 1 - bit])
    return mm2(side(*children), turned) * ROOT_HALF


def down_kernel(devices, stages, levels, *refs):
    refs = list(refs)
    slots = slots_of(stages)
    received = refs[: len(slots)]
    refs = refs[len(slots) :]
    lifts = [refs.pop(0) for _ in range(min(levels, 3))]
    state, spread, links, masks, transfer, bases, near, out, gathered, *ups = refs
    leaves, rank, size = bases.shape
    rows = out.shape[0]
    p = lax.axis_index(AXES)

    for part, ref in zip(slots, received):
        for i, slot in enumerate(part):
            gathered[slot] = ref[i * rows : (i + 1) * rows]

    def raised(k, first, count):
        sets = [side(*[gathered[first[i] + j] for j in range(1 << k)]) for i in range(count)]
        up = mm(stack(*sets), lifts[k][...])
        return up[:, :rank] + up[:, rank:]

    if ups:
        count = devices >> 2
        up = raised(2, [4 * i for i in range(count)], count)
        for k in range(3, levels):
            up = climb(up, count, transfer, 2 + k, (p >> (k - 1)) & 1, rows)
            count //= 2
            ups[k - 3][...] = up.reshape(count, rows, rank)
    lhs = []
    for k in range(levels):
        a = p >> k
        n = devices >> k
        places = [a ^ jnp.clip(a + o, 0, n - 1) for o in OFFSETS]
        if k < 3:
            up = raised(k, [place << k for place in places], 4)
            parts = [up[i * rows : (i + 1) * rows] for i in range(4)]
        else:
            parts = [ups[k - 3][place] for place in places]
        lhs.append(side(*parts) * masks[8 * (3 + k) : 8 * (3 + k) + 1])
    top = mm(halves(side(*lhs), 0), links[...])
    top = top[:rows, :rank] + top[:rows, rank:] + top[rows:, :rank] + top[rows:, rank:]

    at = lambda o: gathered[p ^ jnp.clip(p + o, 0, devices - 1)]
    weights = masks[16:24].astype(BF)
    before = at(-2)[:, rank:] * weights[0:1, :rank]
    after = at(2)[:, :rank] * weights[1:2, 3 * rank :]
    lhs = side(halves(top, 1), top.astype(BF), before, after)
    coef = (mm(lhs, spread[...]) + state[...]).astype(BF)
    for c in range(leaves):
        cols = slice(c * size, (c + 1) * size)
        out[:, cols] = (mm(coef[:, c * rank : (c + 1) * rank], bases[c]) + near[:, cols]).astype(BF)


def inside(x):
    return pltpu.with_memory_space_constraint(x, pltpu.VMEM)


def outside(x):
    return pltpu.with_memory_space_constraint(x, pltpu.HBM)


def shards(rhs, bases, near_blocks, transfer, couple, codes):
    rows = rhs.shape[0]
    leaves, rank, size = bases.shape
    devices = lax.axis_size(AXES)
    stages = stages_of(devices)
    levels = devices.bit_length() - 2
    params = pltpu.CompilerParams(vmem_limit_bytes=16 << 20)

    def call(kernel, shapes, operands, name, flops=0, place=inside, **more):
        single = not isinstance(shapes, list)
        return pl.pallas_call(
            kernel,
            out_shape=shapes if single else list(shapes),
            compiler_params=params,
            cost_estimate=pl.CostEstimate(flops=flops, bytes_accessed=1 << 20, transcendentals=0),
            name=name,
            **more,
        )(*map(place, operands))

    x, bases, low, leaf_coef, own2 = call(
        first_kernel,
        [
            pltpu.VMEM(rhs.shape, BF),
            pltpu.VMEM(bases.shape, BF),
            pltpu.VMEM((2, 2, rank, rank), BF),
            pltpu.VMEM((leaves // 2 * rows, 2 * rank), F32),
            pltpu.VMEM((rows, 2 * rank), BF),
        ],
        (rhs, bases, transfer),
        "first",
        1 << 32,
        place=outside,
        in_specs=[pl.BlockSpec(memory_space=pl.ANY)] * 3,
        scratch_shapes=[pltpu.SemaphoreType.DMA((3,))],
    )
    facing, away, own0, own1 = call(
        edges_kernel,
        [
            pltpu.VMEM((6 * rows, 2 * rank), BF),
            pltpu.VMEM((6 * rows, 2 * rank), BF),
            pltpu.VMEM((leaves // 2 * rows, 2 * rank), BF),
            pltpu.VMEM((leaves // 4 * rows, 2 * rank), BF),
        ],
        (leaf_coef, low, x, own2),
        "edges",
    )

    facing = exchanged(facing, 1)
    away = across_pairs(away)

    lifts = [pltpu.VMEM(((2 << k) * rank, 2 * rank), BF) for k in range(min(levels, 3))]
    state, spread, links, masks, *lifts = call(
        plan_kernel,
        [
            pltpu.VMEM((rows, leaves * rank), F32),
            pltpu.VMEM((5 * rank, leaves * rank), BF),
            pltpu.VMEM((levels * 4 * rank, 2 * rank), BF),
            pltpu.VMEM((8 * (3 + levels), 4 * rank), F32),
            *lifts,
        ],
        (facing, away, own0, own1, codes, transfer, couple),
        "plan",
        1 << 30,
    )

    gathered = own2
    received = [own2]
    for group in stages[:-1]:
        got = [exchanged(gathered, m) for m in group]
        received += got
        if group is not stages[-2]:
            gathered = stack(gathered, *got)
    parts = (gathered, *got) if len(stages) > 1 else (gathered,)
    pay = call(
        pack_kernel,
        pltpu.VMEM((sum(part.shape[0] for part in parts), 2 * rank), BF),
        (masks, *parts),
        "pack",
    )
    received.append(exchanged(pay, 1))

    near = call(
        near_kernel,
        pltpu.VMEM((rows, leaves * size), F32),
        (facing, away, x, near_blocks),
        "near_field",
        3 * leaves * rows * size * size * 2,
    )
    return call(
        functools.partial(down_kernel, devices, stages, levels),
        jax.ShapeDtypeStruct((rows, leaves * size), BF),
        (*received, *lifts, state, spread, links, masks, transfer, bases, near),
        "down_sweep",
        scratch_shapes=[pltpu.VMEM((devices, rows, 2 * rank), BF)]
        + [pltpu.VMEM((devices >> k, rows, rank), F32) for k in range(3, levels)],
    )


def solution(mesh):
    return jax.shard_map(
        shards,
        mesh=mesh,
        in_specs=(
            P(None, ("groups", "leaf", "sub")),
            P(("groups", "leaf", "sub"), None, None),
            P(("groups", "leaf", "sub"), None, None, None),
            P(),
            P(),
            P(),
        ),
        out_specs=P(None, ("groups", "leaf", "sub")),
        check_vma=False,
    )
```

time: 16.4 us -> 16.4 us (level)
  waiting for transfers between devices: 0.46 us -> 0.86 us
  Pallas kernels: 6.45 us -> 6.2 us
    ppermute x6, waiting for transfers between devices: 0.46 us -> 0.85 us  [exchanged(): return lax.ppermute(x, AXES, [(i, i ^ apart) for i in range(devices)])]
    pallas_call x6, Pallas kernels: 6.45 us -> 6.2 us  [call(): pl.pallas_call(kernel, out_shape=shapes if single else list(shapes), comp...]
  transfers between devices with their start and end apart: 7 -> 7, of which waited for: 2 -> 3; matrix products, arithmetic and copies ran while one was open for 0% -> 0% of each run, Pallas kernels for 18% -> 18%
where the time goes in v4:
time: 16.4 us; the launch traced here: 16.3 us
  starting transfers between devices  9.14 us (56%)
  Pallas kernels  6.2 us (38%)
  waiting for transfers between devices  0.86 us (5%)
    ppermute x6, starting transfers between devices, exchanged(): return lax.ppermute(x, AXES, [(i, i ^ apart) for i in range(devices)])  7.62 us
    pallas_call x6, Pallas kernels, call(): pl.pallas_call(kernel, out_shape=shapes if single else list(shapes), comp...  6.2 us
    ppermute x1, starting transfers between devices, across_pairs(): return lax.ppermute(x, ('groups', *AXES), pairs)  1.52 us
    ppermute x6, waiting for transfers between devices, exchanged(): return lax.ppermute(x, AXES, [(i, i ^ apart) for i in range(devices)])  0.85 us
  transfers between devices with their start and end apart: 7, of which 3 were waited for; matrix products, arithmetic and copies ran while one was open for 0% of the time, Pallas kernels for 18%

profile of v4, /device:TPU:0, one launch (start us, length us, event | category | flops | bytes accessed | tf_op | source)
XLA Modules:
  0.0 16.3 jit_solution(17647791812520180915)
XLA Ops:
  0.0 0.0 copy-start.1
  0.0 0.0 copy-start.3
  0.0 0.0 copy-start.2
  0.0 1.7 %first.1 = (bf16[32,2048]{1,0:T(8,128)(2,1)S(1)}, bf16[8,64,256]{2,1,0:T(8,128)(2,1)S(1)}, bf16[2,2,64,64]{3,2,1,0:T(8,128)(2,1)S(1)}, f32[128,128]{1,0:T(8,128)S(1)}, bf16[32,128]{1,0:T(8,128)(2,1)S(1)}) custom-call(bf16[32,2048]{1,0:T(8,128)(2,1)} %rhs_hbm.1, bf16[8,64,256]{2,1,0:T(8,128)(2,1)} %bases_hbm.1, bf16[12,2,64,64]{3,2,1,0:T(8,128)(2,1)} %refs_13_.1), custom_call_target="tpu_custom_call" | custom-call | flops 4294967296 | bytes 1048576 | tf_op jit(solution)/shard_map/first/pallas_call | solution.py:348
  1.7 0.0 copy-start
  1.7 3.5 %collective-permute-start = (bf16[32,128]{1,0:T(8,128)(2,1)S(1)}, bf16[32,128]{1,0:T(8,128)(2,1)S(1)}, u32[]{:S(2)}, u32[]{:S(2)}) collective-permute-start(bf16[32,128]{1,0:T(8,128)(2,1)S(1)} %get-tuple-element.21.u2.refs_0_), channel_id=1, source_target_pairs={{0,9},{1,8},{2,11},{3,10},{4,13},{5,12},{6,15},{7,14},{8,1},{9,0},... | collective-permute-start | bytes 24584 | tf_op jit(solution)/shard_map/ppermute | solution.py:69
  5.2 0.3 %edges.1 = (bf16[192,128]{1,0:T(8,128)(2,1)S(1)}, bf16[192,128]{1,0:T(8,128)(2,1)S(1)}, bf16[128,128]{1,0:T(8,128)(2,1)S(1)}, bf16[64,128]{1,0:T(8,128)(2,1)S(1)}) custom-call(f32[128,128]{1,0:T(8,128)S(1)} %get-tuple-element.22.leaf_coef, bf16[2,2,64,64]{3,2,1,0:T(8,128)(2,1)S(1)} %get-tuple-element.23.low, bf16[32,2048]{1,0:T(8,128)(2,1)S(1)} %get-tuple-element.24.x, ...), custom_call_target="tpu_custom_call" | custom-call | bytes 1048576 | tf_op jit(solution)/shard_map/edges/pallas_call | solution.py:348
  5.5 0.7 %collective-permute-start.4 = (bf16[192,128]{1,0:T(8,128)(2,1)S(1)}, bf16[192,128]{1,0:T(8,128)(2,1)S(1)}, u32[]{:S(2)}, u32[]{:S(2)}) collective-permute-start(bf16[192,128]{1,0:T(8,128)(2,1)S(1)} %get-tuple-element.25), channel_id=1, source_target_pairs={{0,1},{1,0},{2,3},{3,2},{4,5},{5,4},{6,7},{7,6},{8,9},{9,8},{10,11... | collective-permute-start | bytes 147464 | tf_op jit(solution)/shard_map/ppermute | solution.py:69
  6.2 1.5 %collective-permute-start.5 = (bf16[192,128]{1,0:T(8,128)(2,1)S(1)}, bf16[192,128]{1,0:T(8,128)(2,1)S(1)}, u32[]{:S(2)}, u32[]{:S(2)}) collective-permute-start(bf16[192,128]{1,0:T(8,128)(2,1)S(1)} %get-tuple-element.26), channel_id=1, source_target_pairs={{0,16},{1,2},{2,1},{3,4},{4,3},{5,6},{6,5},{7,8},{8,7},{9,10},{10,... | collective-permute-start | bytes 147464 | tf_op jit(solution)/shard_map/ppermute | solution.py:80
  7.7 0.0 collective-permute-done.refs_1_
  7.7 1.9 %collective-permute-start.3 = (bf16[64,128]{1,0:T(8,128)(2,1)S(1)}, bf16[64,128]{1,0:T(8,128)(2,1)S(1)}, u32[]{:S(2)}, u32[]{:S(2)}) collective-permute-start(bf16[64,128]{1,0:T(8,128)(2,1)S(1)} %constant_dynamic-update-slice_fusion.refs_0_), channel_id=1, source_target_pairs={{0,6},{1,7},{2,4},{3,5},{4,2},{5,3},{6,0},{7,1},{8,14},{9,15},{10,... | collective-permute-start | bytes 49160 | tf_op jit(solution)/shard_map/ppermute | solution.py:69
  9.7 0.5 %collective-permute-start.2 = (bf16[64,128]{1,0:T(8,128)(2,1)S(1)}, bf16[64,128]{1,0:T(8,128)(2,1)S(1)}, u32[]{:S(2)}, u32[]{:S(2)}) collective-permute-start(bf16[64,128]{1,0:T(8,128)(2,1)S(1)} %constant_dynamic-update-slice_fusion.refs_0_), channel_id=1, source_target_pairs={{0,5},{1,4},{2,7},{3,6},{4,1},{5,0},{6,3},{7,2},{8,13},{9,12},{10,... | collective-permute-start | bytes 49160 | tf_op jit(solution)/shard_map/ppermute | solution.py:69
  10.2 0.8 %collective-permute-start.1 = (bf16[64,128]{1,0:T(8,128)(2,1)S(1)}, bf16[64,128]{1,0:T(8,128)(2,1)S(1)}, u32[]{:S(2)}, u32[]{:S(2)}) collective-permute-start(bf16[64,128]{1,0:T(8,128)(2,1)S(1)} %constant_dynamic-update-slice_fusion.refs_0_), channel_id=1, source_target_pairs={{0,3},{1,2},{2,1},{3,0},{4,7},{5,6},{6,5},{7,4},{8,11},{9,10},{10,... | collective-permute-start | bytes 49160 | tf_op jit(solution)/shard_map/ppermute | solution.py:69
  11.0 0.0 collective-permute-done.4.facing
  11.0 0.0 collective-permute-done.5.away
  11.0 0.0 copy-done.1
  11.0 0.0 copy-done.3
  11.0 0.0 copy-done.2
  11.0 1.6 %plan.1 = (f32[32,512]{1,0:T(8,128)S(1)}, bf16[320,512]{1,0:T(8,128)(2,1)S(1)}, bf16[768,128]{1,0:T(8,128)(2,1)S(1)}, f32[48,256]{1,0:T(8,128)S(1)}, bf16[128,12...) custom-call(bf16[192,128]{1,0:T(8,128)(2,1)S(1)} %collective-permute-done.4.facing, ...), custom_call_target="tpu_custom_call" | custom-call | flops 1073741824 | bytes 1048576 | tf_op jit(solution)/shard_map/plan/pallas_call | solution.py:348
  12.7 0.0 collective-permute-done.3.refs_3_.refs_4_
  12.7 0.3 %collective-permute-done.2.refs_2_.refs_3_ = bf16[64,128]{1,0:T(8,128)(2,1)S(1)} collective-permute-done((bf16[64,128]{1,0:T(8,128)(2,1)S(1)}, bf16[64,128]{1,0:T(8,128)(2,1)S(1)}, u32[]{:S(2)}, u32[]{:S(2)}) %collective-permute-start.2) | collective-permute-done | bytes 16416 | tf_op jit(solution)/shard_map/ppermute | solution.py:69
  13.0 0.4 %collective-permute-done.1.refs_1_.refs_2_ = bf16[64,128]{1,0:T(8,128)(2,1)S(1)} collective-permute-done((bf16[64,128]{1,0:T(8,128)(2,1)S(1)}, bf16[64,128]{1,0:T(8,128)(2,1)S(1)}, u32[]{:S(2)}, u32[]{:S(2)}) %collective-permute-start.1) | collective-permute-done | bytes 16416 | tf_op jit(solution)/shard_map/ppermute | solution.py:69
  13.4 0.1 collective-permute-start.6
  13.5 0.0 copy-done
  13.5 1.0 %near_field.1.refs_15_ = f32[32,2048]{1,0:T(8,128)S(1)} custom-call(bf16[192,128]{1,0:T(8,128)(2,1)S(1)} %collective-permute-done.4.facing, bf16[192,128]{1,0:T(8,128)(2,1)S(1)} %collective-permute-done.5.away, bf16[32,2048]{1,0:T(8,128)(2,1)S(1)} %get-tuple-element.24.x, bf16[8,3,256,256]{3,2,1,0:T(8,128)(2,1)S(1)} %copy-done), custom_call_target="tpu_custom_call" | custom-call | flops 100663296 | bytes 1048576 | tf_op jit(solution)/shard_map/near_field/pallas_call | solution.py:348
  14.5 0.1 collective-permute-done.6.refs_5_
  14.7 1.6 %down_sweep.1 = bf16[32,2048]{1,0:T(8,128)(2,1)} custom-call(bf16[32,128]{1,0:T(8,128)(2,1)S(1)} %get-tuple-element.21.u2.refs_0_, bf16[32,128]{1,0:T(8,128)(2,1)S(1)} %collective-permute-done.refs_1_, bf16[64,128]{1,0:T(8,128)(2,1)S(1)} %collective-permute-done.1.refs_1_.refs_2_, bf16[64,128]{1,0:T(8,128)(2,1)S(1)} %collective-permute-done.2.refs_2_.refs_3_, ...), custom_call_target="tpu_custom_call" | custom-call | bytes 1048576 | tf_op jit(solution)/shard_map/down_sweep/pallas_call | solution.py:348
  (3 shorter events, 0.0 us)
Async XLA Ops:
  0.0 11.0 %copy-start.1 = (bf16[12,2,64,64]{3,2,1,0:T(8,128)(2,1)S(1)}, bf16[12,2,64,64]{3,2,1,0:T(8,128)(2,1)}, u32[]{:S(2)}) copy-start(bf16[12,2,64,64]{3,2,1,0:T(8,128)(2,1)} %refs_13_.1) | copy-start | bytes 589828
  0.0 11.0 %copy-start.3 = (s32[12,3,128]{2,1,0:T(4,128)S(1)}, s32[12,3,128]{2,1,0:T(4,128)}, u32[]{:S(2)}) copy-start(s32[12,3,128]{2,1,0:T(4,128)} %codes.1) | copy-start | bytes 55300
  0.0 11.0 %copy-start.2 = (bf16[12,4,64,64]{3,2,1,0:T(8,128)(2,1)S(1)}, bf16[12,4,64,64]{3,2,1,0:T(8,128)(2,1)}, u32[]{:S(2)}) copy-start(bf16[12,4,64,64]{3,2,1,0:T(8,128)(2,1)} %couple.1) | copy-start | bytes 1179652
  1.7 11.8 %copy-start = (bf16[8,3,256,256]{3,2,1,0:T(8,128)(2,1)S(1)}, bf16[8,3,256,256]{3,2,1,0:T(8,128)(2,1)}, u32[]{:S(2)}) copy-start(bf16[8,3,256,256]{3,2,1,0:T(8,128)(2,1)} %blocks.1) | copy-start | bytes 9437188
  1.7 6.1 %collective-permute-start = (bf16[32,128]{1,0:T(8,128)(2,1)S(1)}, bf16[32,128]{1,0:T(8,128)(2,1)S(1)}, u32[]{:S(2)}, u32[]{:S(2)}) collective-permute-start(bf16[32,128]{1,0:T(8,128)(2,1)S(1)} %get-tuple-element.21.u2.refs_0_), channel_id=1, source_target_pairs={{0,9},{1,8},{2,11},{3,10},{4,13},{5,12},{6,15},{7,14},{8,1},{9,0},... | collective-permute-start | bytes 24584 | tf_op jit(solution)/shard_map/ppermute | solution.py:69
  5.5 5.5 %collective-permute-start.4 = (bf16[192,128]{1,0:T(8,128)(2,1)S(1)}, bf16[192,128]{1,0:T(8,128)(2,1)S(1)}, u32[]{:S(2)}, u32[]{:S(2)}) collective-permute-start(bf16[192,128]{1,0:T(8,128)(2,1)S(1)} %get-tuple-element.25), channel_id=1, source_target_pairs={{0,1},{1,0},{2,3},{3,2},{4,5},{5,4},{6,7},{7,6},{8,9},{9,8},{10,11... | collective-permute-start | bytes 147464 | tf_op jit(solution)/shard_map/ppermute | solution.py:69
  6.2 4.8 %collective-permute-start.5 = (bf16[192,128]{1,0:T(8,128)(2,1)S(1)}, bf16[192,128]{1,0:T(8,128)(2,1)S(1)}, u32[]{:S(2)}, u32[]{:S(2)}) collective-permute-start(bf16[192,128]{1,0:T(8,128)(2,1)S(1)} %get-tuple-element.26), channel_id=1, source_target_pairs={{0,16},{1,2},{2,1},{3,4},{4,3},{5,6},{6,5},{7,8},{8,7},{9,10},{10,... | collective-permute-start | bytes 147464 | tf_op jit(solution)/shard_map/ppermute | solution.py:80
  7.7 4.9 %collective-permute-start.3 = (bf16[64,128]{1,0:T(8,128)(2,1)S(1)}, bf16[64,128]{1,0:T(8,128)(2,1)S(1)}, u32[]{:S(2)}, u32[]{:S(2)}) collective-permute-start(bf16[64,128]{1,0:T(8,128)(2,1)S(1)} %constant_dynamic-update-slice_fusion.refs_0_), channel_id=1, source_target_pairs={{0,6},{1,7},{2,4},{3,5},{4,2},{5,3},{6,0},{7,1},{8,14},{9,15},{10,... | collective-permute-start | bytes 49160 | tf_op jit(solution)/shard_map/ppermute | solution.py:69
  9.7 3.3 %collective-permute-start.2 = (bf16[64,128]{1,0:T(8,128)(2,1)S(1)}, bf16[64,128]{1,0:T(8,128)(2,1)S(1)}, u32[]{:S(2)}, u32[]{:S(2)}) collective-permute-start(bf16[64,128]{1,0:T(8,128)(2,1)S(1)} %constant_dynamic-update-slice_fusion.refs_0_), channel_id=1, source_target_pairs={{0,5},{1,4},{2,7},{3,6},{4,1},{5,0},{6,3},{7,2},{8,13},{9,12},{10,... | collective-permute-start | bytes 49160 | tf_op jit(solution)/shard_map/ppermute | solution.py:69
  10.2 3.2 %collective-permute-start.1 = (bf16[64,128]{1,0:T(8,128)(2,1)S(1)}, bf16[64,128]{1,0:T(8,128)(2,1)S(1)}, u32[]{:S(2)}, u32[]{:S(2)}) collective-permute-start(bf16[64,128]{1,0:T(8,128)(2,1)S(1)} %constant_dynamic-update-slice_fusion.refs_0_), channel_id=1, source_target_pairs={{0,3},{1,2},{2,1},{3,0},{4,7},{5,6},{6,5},{7,4},{8,11},{9,10},{10,... | collective-permute-start | bytes 49160 | tf_op jit(solution)/shard_map/ppermute | solution.py:69
  13.4 1.3 %collective-permute-start.6 = (bf16[256,128]{1,0:T(8,128)(2,1)S(1)}, bf16[256,128]{1,0:T(8,128)(2,1)S(1)}, u32[]{:S(2)}, u32[]{:S(2)}) collective-permute-start(bf16[256,128]{1,0:T(8,128)(2,1)S(1)} %pack.1), channel_id=1, source_target_pairs={{0,1},{1,0},{2,3},{3,2},{4,5},{5,4},{6,7},{7,6},{8,9},{9,8},{10,11... | collective-permute-start | bytes 196616 | tf_op jit(solution)/shard_map/ppermute | solution.py:69

commit v5 on v4

--- a/solution.py
+++ b/solution.py
@@ -13,6 +13,7 @@
 BF = jnp.bfloat16
 F32 = jnp.float32
 LANES = 64
+SHARE = 2
 
 
 def mm(a, b):
@@ -80,7 +81,7 @@
     return lax.ppermute(x, ("groups", *AXES), pairs)
 
 
-def first_kernel(rhs_hbm, bases_hbm, transfer_hbm, x, bases, low, leaf_coef, own2, sems):
+def first_kernel(rhs_hbm, bases_hbm, transfer_hbm, x, bases, facing, away, own0, own1, own2, low, sems):
     leaves, rank, size = bases.shape
     rows = x.shape[0]
     pairs = (
@@ -102,23 +103,19 @@
     for i in range(0, leaves, 2):
         both = mm_t(stack(at(i), at(i + 1)), bases[i : i + 2].reshape(2 * rank, size))
         parts.append(jnp.where(first, both[:rows], both[rows:]))
-    leaf_coef[...] = stack(*parts)
+    leaf_coef = stack(*parts)
     fours = stack(*[side(parts[i], parts[i + 1]) for i in range(0, leaves // 2, 2)])
     up = mm(halves(fours, 0), product)
     count = fours.shape[0]
     up = up[:count, :rank] + up[:count, rank:] + up[count:, :rank]
     own2[...] = side(*[up[i : i + rows] for i in range(0, count, rows)]).astype(BF)
-
-
-def edges_kernel(leaf_coef, low, x, u2, facing, away, own0, own1):
-    rank = low.shape[-1]
-    rows = x.shape[0]
-    own0[...] = leaf_coef[...].astype(BF)
-    up1 = mm2(leaf_coef[...], low[0].reshape(2 * rank, rank)) * ROOT_HALF
+    u2 = own2
+
+    own0[...] = leaf_coef.astype(BF)
+    up1 = mm2(leaf_coef, table) * ROOT_HALF
     up1 = [up1[i : i + rows] for i in range(0, up1.shape[0], rows)]
     own1[...] = stack(*[side(up1[i], up1[i + 1]) for i in range(0, len(up1), 2)]).astype(BF)
     end = x.shape[1]
-    size = end // (2 * len(up1))
     half = size // 2
     last0, last1 = own0.shape[0] - rows, own1.shape[0] - rows
     right = stack(
@@ -150,8 +147,7 @@
         at += part.shape[0]
 
 
-def mask_of(codes, level, leaves):
-    p = lax.axis_index(AXES)
+def mask_of(codes, level, leaves, p):
     wide = codes.shape[2]
     lanes = lax.broadcasted_iota(jnp.int32, (8, 4 * LANES), 1) // LANES
     offset = jnp.where(lanes < 2, lanes - 3, lanes)
@@ -177,18 +173,11 @@
     return stack(*parts)
 
 
-def plan_kernel(facing, away, own0, own1, codes, transfer, couple, state, spread, links_out, masks, *lifts):
+def spread_tables(transfer, couple, spread):
     rank = transfer.shape[-1]
-    levels = masks.shape[0] // 8 - 3
     leaves = spread.shape[1] // rank
-    p = lax.axis_index(AXES)
     table = lambda level: transfer[level].reshape(2 * rank, rank)
     beside = lambda rows: side(*[rows[i : i + rank] for i in range(0, rows.shape[0], rank)])
-
-    mask = [mask_of(codes, level, leaves) for level in range(3 + levels)]
-    masks[...] = stack(*mask)
-    state[...] = couplings(facing, away, own0, own1, mask, transfer, couple)
-
     both = stack(transfer[2, 0].astype(F32).T, transfer[2, 1].astype(F32).T, couple[2, 0].astype(F32), couple[2, 3].astype(F32))
     both = beside(lowered(lowered(both, table(1), rank), table(0), rank))
     wide = leaves * rank
@@ -201,6 +190,19 @@
     spread[3 * rank : 4 * rank] = side(first, none)
     spread[4 * rank :] = side(none, second)
 
+
+def plan_kernel(facing, away, own0, own1, codes, transfer, couple, state, spread, links_out, masks, *lifts):
+    rank = transfer.shape[-1]
+    levels = masks.shape[0] // 8 - 3
+    leaves = spread.shape[1] // rank
+    p = lax.axis_index(AXES)
+    table = lambda level: transfer[level].reshape(2 * rank, rank)
+
+    mask = [mask_of(codes, level, leaves, p) for level in range(3 + levels)]
+    masks[...] = stack(*mask)
+    state[...] = couplings(facing, away, own0, own1, mask, transfer, couple)
+    spread_tables(transfer, couple, spread)
+
     for k in range(levels):
         value = couple[3 + k].reshape(4 * rank, rank).astype(F32)
         for i in reversed(range(k)):
@@ -222,18 +224,19 @@
     return jnp.where(even, away, facing), jnp.where(even, facing, away)
 
 
-def near_kernel(facing, away, x, blocks, near):
-    leaves, _, size, _ = blocks.shape
+def near_kernel(first, facing, away, x, blocks, near):
+    _, _, size, _ = blocks.shape
+    leaves = x.shape[1] // size
     rows = x.shape[0]
     left, right = sides_of(facing[: 2 * rows], away[: 2 * rows])
     before = side(left[:rows], left[rows:])
     after = side(right[:rows], right[rows:])
     at = lambda i: before if i < 0 else after if i == leaves else x[:, i * size : (i + 1) * size]
-    for i in range(leaves):
+    for i in range(first, first + near.shape[1] // size):
         total = mm_t(at(i), blocks[i, 1])
         total += mm_t(at(i - 1), blocks[i, 0])
         total += mm_t(at(i + 1), blocks[i, 2])
-        near[:, i * size : (i + 1) * size] = total
+        near[:, (i - first) * size : (i - first + 1) * size] = total
 
 
 def couplings(facing, away, own0, own1, mask, transfer, couple):
@@ -265,6 +268,87 @@
     far0 = coupled(0, ext, leaves)
     down = far0 + lowered(far1 + lowered(far2, table(1), rows), table(0), rows)
     return side(*[block(down, c) for c in range(leaves)])
+
+
+def dense_plan_kernel(
+    levels, slots, facing, away, own0, own1, codes, transfer, couple, state, spread, masks, weights, chosen
+):
+    rank = transfer.shape[-1]
+    leaves = spread.shape[1] // rank
+    p = lax.axis_index(AXES)
+
+    mask = [mask_of(codes, level, leaves, p) for level in range(3)]
+    masks[:8] = mask[2]
+    masks[8:] = mask_of(codes, 2, leaves, p ^ 1)
+    state[...] = couplings(facing, away, own0, own1, mask, transfer, couple)
+    spread_tables(transfer, couple, spread)
+
+    for k in range(levels):
+        value = couple[3 + k].reshape(4 * rank, rank).astype(F32)
+        for i in reversed(range(1, k)):
+            value = mm2(value, transfer[3 + i, (p >> i) & 1], mm_t)
+        for j in range(2):
+            device = p ^ j
+            low = mm2(value, transfer[3, device & 1], mm_t) if k > 0 else value
+            hit = mask_of(codes, 3 + k, leaves, device)
+            for q in range(4):
+                part = low[q * rank : (q + 1) * rank] * hit[:1, q * rank : (q + 1) * rank]
+                chosen[2 * k + j, q] = part.astype(BF)
+            chosen[2 * k + j, 4] = jnp.zeros((rank, rank), BF)
+
+    lifts = [[transfer[2].reshape(2 * rank, rank).astype(F32) * ROOT_HALF]]
+    for k in range(1, levels):
+        b = (p >> (k - 1)) & 1
+        lifts.append([mm2(a, transfer[2 + k, bit]) * ROOT_HALF for bit in (b, 1 - b) for a in lifts[-1]])
+    lifts = [[halves(a, 0) for a in level] for level in lifts]
+
+    for i, slot in enumerate(slots):
+        picked = []
+        for k in range(levels):
+            both = []
+            for j in range(2):
+                apart = ((p ^ slot) >> k) - ((p ^ j) >> k)
+                q = jnp.where(apart < 0, apart + 3, apart)
+                q = jnp.where((apart >= -3) & (apart <= 3) & (apart * apart >= 4), q, 4)
+                both.append(chosen[2 * k + j, q])
+            picked.append(side(*both))
+        lift = side(*[lifts[k][slot & ((1 << k) - 1)] for k in range(levels)])
+        out = mm(lift, stack(*picked))
+        weights[2 * rank * i : 2 * rank * (i + 1)] = (out[: 2 * rank] + out[2 * rank :]).astype(BF)
+
+
+def half_kernel(devices, slots, waits, masks, weights, *refs):
+    *parts, mine, theirs, gathered = refs
+    parts = parts[: len(parts) - waits]
+    rank = weights.shape[1] // 2
+    rows = mine.shape[0]
+    p = lax.axis_index(AXES)
+    gathered[...] = jnp.zeros(gathered.shape, BF)
+    found = [part[i : i + rows] for part in parts for i in range(0, part.shape[0], rows)]
+    for slot, value in zip(slots, found):
+        gathered[slot] = value
+    top = mm(side(*found), weights[...])
+    for j, out in ((0, mine), (1, theirs)):
+        device = p ^ j
+        at = lambda o: gathered[p ^ jnp.clip(device + o, 0, devices - 1)]
+        hit = masks[8 * j : 8 * j + 8].astype(BF)
+        before = at(-2)[:, rank:] * hit[0:1, :rank]
+        after = at(2)[:, :rank] * hit[1:2, 3 * rank :]
+        out[...] = side(halves(top[:, j * rank : (j + 1) * rank], 1), before, after)
+
+
+def leaves_kernel(count, mine, theirs, state, spread, bases, *refs):
+    out = refs[-1]
+    leaves, rank, size = bases.shape
+    near = [(ref, i) for ref in refs[:count] for i in range(0, ref.shape[1], size)]
+    a, b = mine[...].astype(F32), theirs[...].astype(F32)
+    top = (a[:, :rank] + b[:, :rank]) + (a[:, rank : 2 * rank] + b[:, rank : 2 * rank])
+    lhs = side(halves(top, 1), top.astype(BF), (a[:, 2 * rank :] + b[:, 2 * rank :]).astype(BF))
+    coef = (mm(lhs, spread[...]) + state[...]).astype(BF)
+    for c in range(leaves):
+        ref, at = near[c]
+        total = mm(coef[:, c * rank : (c + 1) * rank], bases[c]) + ref[:, at : at + size]
+        out[:, c * size : (c + 1) * size] = total.astype(BF)
 
 
 def climb(up, count, transfer, level, bit, rows):
@@ -354,13 +438,15 @@
             **more,
         )(*map(place, operands))
 
-    x, bases, low, leaf_coef, own2 = call(
+    x, bases, facing, away, own0, own1, own2 = call(
         first_kernel,
         [
             pltpu.VMEM(rhs.shape, BF),
             pltpu.VMEM(bases.shape, BF),
-            pltpu.VMEM((2, 2, rank, rank), BF),
-            pltpu.VMEM((leaves // 2 * rows, 2 * rank), F32),
+            pltpu.VMEM((6 * rows, 2 * rank), BF),
+            pltpu.VMEM((6 * rows, 2 * rank), BF),
+            pltpu.VMEM((leaves // 2 * rows, 2 * rank), BF),
+            pltpu.VMEM((leaves // 4 * rows, 2 * rank), BF),
             pltpu.VMEM((rows, 2 * rank), BF),
         ],
         (rhs, bases, transfer),
@@ -368,38 +454,55 @@
         1 << 32,
         place=outside,
         in_specs=[pl.BlockSpec(memory_space=pl.ANY)] * 3,
-        scratch_shapes=[pltpu.SemaphoreType.DMA((3,))],
-    )
-    facing, away, own0, own1 = call(
-        edges_kernel,
-        [
-            pltpu.VMEM((6 * rows, 2 * rank), BF),
-            pltpu.VMEM((6 * rows, 2 * rank), BF),
-            pltpu.VMEM((leaves // 2 * rows, 2 * rank), BF),
-            pltpu.VMEM((leaves // 4 * rows, 2 * rank), BF),
-        ],
-        (leaf_coef, low, x, own2),
-        "edges",
+        scratch_shapes=[pltpu.VMEM((2, 2, rank, rank), BF), pltpu.SemaphoreType.DMA((3,))],
     )
 
     facing = exchanged(facing, 1)
     away = across_pairs(away)
 
-    lifts = [pltpu.VMEM(((2 << k) * rank, 2 * rank), BF) for k in range(min(levels, 3))]
-    state, spread, links, masks, *lifts = call(
-        plan_kernel,
-        [
-            pltpu.VMEM((rows, leaves * rank), F32),
-            pltpu.VMEM((5 * rank, leaves * rank), BF),
-            pltpu.VMEM((levels * 4 * rank, 2 * rank), BF),
-            pltpu.VMEM((8 * (3 + levels), 4 * rank), F32),
-            *lifts,
-        ],
-        (facing, away, own0, own1, codes, transfer, couple),
-        "plan",
-        1 << 30,
-    )
-
+    dense = levels <= 3
+    if dense:
+        slots = [slot for part in slots_of(stages)[:-1] for slot in part]
+        state, spread, masks, weights = call(
+            functools.partial(dense_plan_kernel, levels, slots),
+            [
+                pltpu.VMEM((rows, leaves * rank), F32),
+                pltpu.VMEM((5 * rank, leaves * rank), BF),
+                pltpu.VMEM((16, 4 * rank), F32),
+                pltpu.VMEM((2 * rank * len(slots), 2 * rank), BF),
+            ],
+            (facing, away, own0, own1, codes, transfer, couple),
+            "plan",
+            1 << 30,
+            scratch_shapes=[pltpu.VMEM((2 * levels, 5, rank, rank), BF)],
+        )
+    else:
+        lifts = [pltpu.VMEM(((2 << k) * rank, 2 * rank), BF) for k in range(min(levels, 3))]
+        state, spread, links, masks, *lifts = call(
+            plan_kernel,
+            [
+                pltpu.VMEM((rows, leaves * rank), F32),
+                pltpu.VMEM((5 * rank, leaves * rank), BF),
+                pltpu.VMEM((levels * 4 * rank, 2 * rank), BF),
+                pltpu.VMEM((8 * (3 + levels), 4 * rank), F32),
+                *lifts,
+            ],
+            (facing, away, own0, own1, codes, transfer, couple),
+            "plan",
+            1 << 30,
+        )
+
+    def near_of(first, count):
+        return call(
+            functools.partial(near_kernel, first),
+            pltpu.VMEM((rows, count * size), F32),
+            (facing, away, x, near_blocks),
+            "near_field",
+            3 * count * rows * size * size * 2,
+        )
+
+    some = leaves * SHARE // 8 if dense else 0
+    near = (near_of(0, some),) if some else ()
     gathered = own2
     received = [own2]
     for group in stages[:-1]:
@@ -407,26 +510,37 @@
         received += got
         if group is not stages[-2]:
             gathered = stack(gathered, *got)
-    parts = (gathered, *got) if len(stages) > 1 else (gathered,)
-    pay = call(
-        pack_kernel,
-        pltpu.VMEM((sum(part.shape[0] for part in parts), 2 * rank), BF),
-        (masks, *parts),
-        "pack",
-    )
-    received.append(exchanged(pay, 1))
-
-    near = call(
-        near_kernel,
-        pltpu.VMEM((rows, leaves * size), F32),
-        (facing, away, x, near_blocks),
-        "near_field",
-        3 * leaves * rows * size * size * 2,
-    )
+    if dense:
+        mine, theirs = call(
+            functools.partial(half_kernel, devices, slots, len(near)),
+            [pltpu.VMEM((rows, 4 * rank), BF), pltpu.VMEM((rows, 4 * rank), BF)],
+            (masks, weights, *received, *near),
+            "half",
+            scratch_shapes=[pltpu.VMEM((devices, rows, 2 * rank), BF)],
+        )
+        theirs = exchanged(theirs, 1)
+    else:
+        parts = (gathered, *got) if len(stages) > 1 else (gathered,)
+        pay = call(
+            pack_kernel,
+            pltpu.VMEM((sum(part.shape[0] for part in parts), 2 * rank), BF),
+            (masks, *parts),
+            "pack",
+        )
+        received.append(exchanged(pay, 1))
+
+    near = (*near, near_of(some, leaves - some))
+    if dense:
+        return call(
+            functools.partial(leaves_kernel, len(near)),
+            jax.ShapeDtypeStruct((rows, leaves * size), BF),
+            (mine, theirs, state, spread, bases, *near, *received, masks, weights, transfer),
+            "leaves",
+        )
     return call(
         functools.partial(down_kernel, devices, stages, levels),
         jax.ShapeDtypeStruct((rows, leaves * size), BF),
-        (*received, *lifts, state, spread, links, masks, transfer, bases, near),
+        (*received, *lifts, state, spread, links, masks, transfer, bases, *near),
         "down_sweep",
         scratch_shapes=[pltpu.VMEM((devices, rows, 2 * rank), BF)]
         + [pltpu.VMEM((devices >> k, rows, rank), F32) for k in range(3, levels)],

time: 16.4 us -> 15.9 us (0.970)
  waiting for transfers between devices: 0.86 us -> 0.18 us
  starting transfers between devices: 9.14 us -> 9.39 us
    ppermute x6, waiting for transfers between devices: 0.85 us -> 0.18 us  [exchanged(): return lax.ppermute(x, AXES, [(i, i ^ apart) for i in range(devices)])]
    ppermute x6, starting transfers between devices: 7.62 us -> 7.87 us  [exchanged(): return lax.ppermute(x, AXES, [(i, i ^ apart) for i in range(devices)])]
  transfers between devices with their start and end apart: 7 -> 7, of which waited for: 3 -> 2; matrix products, arithmetic and copies ran while one was open for 0% -> 0% of each run, Pallas kernels for 18% -> 19%
where the time goes in v5:
time: 15.9 us; the launch traced here: 15.7 us
  starting transfers between devices  9.39 us (59%)
  Pallas kernels  6.07 us (38%)
  waiting for transfers between devices  0.18 us (1%)
    ppermute x6, starting transfers between devices, exchanged(): return lax.ppermute(x, AXES, [(i, i ^ apart) for i in range(devices)])  7.87 us
    pallas_call x6, Pallas kernels, call(): pl.pallas_call(kernel, out_shape=shapes if single else list(shapes), comp...  6.07 us
    ppermute x1, starting transfers between devices, across_pairs(): return lax.ppermute(x, ('groups', *AXES), pairs)  1.52 us
  transfers between devices with their start and end apart: 7, of which 2 were waited for; matrix products, arithmetic and copies ran while one was open for 0% of the time, Pallas kernels for 19%

profile of v5, /device:TPU:0, one launch (start us, length us, event | category | flops | bytes accessed | tf_op | source)
XLA Modules:
  0.0 15.7 jit_solution(18180124100697246140)
XLA Ops:
  0.0 0.0 copy-start.1
  0.0 0.0 copy-start.3
  0.0 0.0 copy-start.2
  0.0 1.7 %first.1 = (bf16[32,2048]{1,0:T(8,128)(2,1)S(1)}, bf16[8,64,256]{2,1,0:T(8,128)(2,1)S(1)}, bf16[192,128]{1,0:T(8,128)(2,1)S(1)}, bf16[192,128]{1,0:T(8,128)(2,1)...) custom-call(bf16[32,2048]{1,0:T(8,128)(2,1)} %rhs_hbm.1, ...), custom_call_target="tpu_custom_call" | custom-call | flops 4294967296 | bytes 1048576 | tf_op jit(solution)/shard_map/first/pallas_call | solution.py:432
  1.7 0.0 copy-start
  1.7 3.5 %collective-permute-start.2 = (bf16[32,128]{1,0:T(8,128)(2,1)S(1)}, bf16[32,128]{1,0:T(8,128)(2,1)S(1)}, u32[]{:S(2)}, u32[]{:S(2)}) collective-permute-start(bf16[32,128]{1,0:T(8,128)(2,1)S(1)} %get-tuple-element.24.refs_0_.refs_2_), channel_id=1, source_target_pairs={{0,9},{1,8},{2,11},{3,10},{4,13},{5,12},{6,15},{7,14},{8,1},{9,0},... | collective-permute-start | bytes 24584 | tf_op jit(solution)/shard_map/ppermute | solution.py:70
  5.3 0.7 %collective-permute-start = (bf16[192,128]{1,0:T(8,128)(2,1)S(1)}, bf16[192,128]{1,0:T(8,128)(2,1)S(1)}, u32[]{:S(2)}, u32[]{:S(2)}) collective-permute-start(bf16[192,128]{1,0:T(8,128)(2,1)S(1)} %get-tuple-element.18), channel_id=1, source_target_pairs={{0,1},{1,0},{2,3},{3,2},{4,5},{5,4},{6,7},{7,6},{8,9},{9,8},{10,11... | collective-permute-start | bytes 147464 | tf_op jit(solution)/shard_map/ppermute | solution.py:70
  5.9 1.5 %collective-permute-start.1 = (bf16[192,128]{1,0:T(8,128)(2,1)S(1)}, bf16[192,128]{1,0:T(8,128)(2,1)S(1)}, u32[]{:S(2)}, u32[]{:S(2)}) collective-permute-start(bf16[192,128]{1,0:T(8,128)(2,1)S(1)} %get-tuple-element.19), channel_id=1, source_target_pairs={{0,16},{1,2},{2,1},{3,4},{4,3},{5,6},{6,5},{7,8},{8,7},{9,10},{10,... | collective-permute-start | bytes 147464 | tf_op jit(solution)/shard_map/ppermute | solution.py:81
  7.5 0.0 collective-permute-done.2.refs_1_.refs_3_
  7.5 2.2 %collective-permute-start.5 = (bf16[64,128]{1,0:T(8,128)(2,1)S(1)}, bf16[64,128]{1,0:T(8,128)(2,1)S(1)}, u32[]{:S(2)}, u32[]{:S(2)}) collective-permute-start(bf16[64,128]{1,0:T(8,128)(2,1)S(1)} %constant_dynamic-update-slice_fusion), channel_id=1, source_target_pairs={{0,6},{1,7},{2,4},{3,5},{4,2},{5,3},{6,0},{7,1},{8,14},{9,15},{10,... | collective-permute-start | bytes 49160 | tf_op jit(solution)/shard_map/ppermute | solution.py:70
  9.7 0.2 %collective-permute-start.4 = (bf16[64,128]{1,0:T(8,128)(2,1)S(1)}, bf16[64,128]{1,0:T(8,128)(2,1)S(1)}, u32[]{:S(2)}, u32[]{:S(2)}) collective-permute-start(bf16[64,128]{1,0:T(8,128)(2,1)S(1)} %constant_dynamic-update-slice_fusion), channel_id=1, source_target_pairs={{0,5},{1,4},{2,7},{3,6},{4,1},{5,0},{6,3},{7,2},{8,13},{9,12},{10,... | collective-permute-start | bytes 49160 | tf_op jit(solution)/shard_map/ppermute | solution.py:70
  10.0 0.8 %collective-permute-start.3 = (bf16[64,128]{1,0:T(8,128)(2,1)S(1)}, bf16[64,128]{1,0:T(8,128)(2,1)S(1)}, u32[]{:S(2)}, u32[]{:S(2)}) collective-permute-start(bf16[64,128]{1,0:T(8,128)(2,1)S(1)} %constant_dynamic-update-slice_fusion), channel_id=1, source_target_pairs={{0,3},{1,2},{2,1},{3,0},{4,7},{5,6},{6,5},{7,4},{8,11},{9,10},{10,... | collective-permute-start | bytes 49160 | tf_op jit(solution)/shard_map/ppermute | solution.py:70
  10.7 0.0 collective-permute-done.facing
  10.8 0.0 collective-permute-done.1.away
  10.8 0.0 copy-done.1
  10.8 0.0 copy-done.3
  10.8 0.0 copy-done.2
  10.8 1.9 %plan.1 = (f32[32,512]{1,0:T(8,128)S(1)}, bf16[320,512]{1,0:T(8,128)(2,1)S(1)}, f32[16,256]{1,0:T(8,128)S(1)}, bf16[1024,128]{1,0:T(8,128)(2,1)S(1)}) custom-call(bf16[192,128]{1,0:T(8,128)(2,1)S(1)} %collective-permute-done.facing, bf16[192,128]{1,0:T(8,128)(2,1)S(1)} %collective-permute-done.1.away, bf16[128,128]{1,0:T(8,128)(2,1)S(1)} %get-tuple-element.20.own0, ...), custom_call_target="tpu_custom_call" | custom-call | flops 1073741824 | bytes 1048576 | tf_op jit(solution)/shard_map/plan/pallas_call | solution.py:432
  12.7 0.0 copy-done
  12.7 0.3 %near_field.2.refs_5_.refs_0_ = f32[32,512]{1,0:T(8,128)S(1)} custom-call(bf16[192,128]{1,0:T(8,128)(2,1)S(1)} %collective-permute-done.facing, bf16[192,128]{1,0:T(8,128)(2,1)S(1)} %collective-permute-done.1.away, bf16[32,2048]{1,0:T(8,128)(2,1)S(1)} %get-tuple-element.25.x, bf16[8,3,256,256]{3,2,1,0:T(8,128)(2,1)S(1)} %copy-done), custom_call_target="tpu_custom_call" | custom-call | flops 25165824 | bytes 1048576 | tf_op jit(solution)/shard_map/near_field/pallas_call | solution.py:432
  13.0 0.0 collective-permute-done.5.refs_4_.refs_6_
  13.0 0.0 collective-permute-done.4.refs_3_.refs_5_
  13.0 0.1 collective-permute-done.3.refs_2_.refs_4_
  13.1 0.2 %half.1 = (bf16[32,256]{1,0:T(8,128)(2,1)S(1)}, bf16[32,256]{1,0:T(8,128)(2,1)S(1)}) custom-call(f32[16,256]{1,0:T(8,128)S(1)} %get-tuple-element.22.masks.refs_7_, bf16[1024,128]{1,0:T(8,128)(2,1)S(1)} %get-tuple-element.23.weights.refs_8_, bf16[32,128]{1,0:T(8,128)(2,1)S(1)} %get-tuple-element.24.refs_0_.refs_2_, ...), custom_call_target="tpu_custom_call" | custom-call | bytes 1048576 | tf_op jit(solution)/shard_map/half/pallas_call | solution.py:432
  13.4 0.4 %collective-permute-start.6 = (bf16[32,256]{1,0:T(8,128)(2,1)S(1)}, bf16[32,256]{1,0:T(8,128)(2,1)S(1)}, u32[]{:S(2)}, u32[]{:S(2)}) collective-permute-start(bf16[32,256]{1,0:T(8,128)(2,1)S(1)} %get-tuple-element.27), channel_id=1, source_target_pairs={{0,1},{1,0},{2,3},{3,2},{4,5},{5,4},{6,7},{7,6},{8,9},{9,8},{10,11... | collective-permute-start | bytes 49160 | tf_op jit(solution)/shard_map/ppermute | solution.py:70
  13.7 0.8 %near_field.3.refs_1_ = f32[32,1536]{1,0:T(8,128)S(1)} custom-call(bf16[192,128]{1,0:T(8,128)(2,1)S(1)} %collective-permute-done.facing, bf16[192,128]{1,0:T(8,128)(2,1)S(1)} %collective-permute-done.1.away, bf16[32,2048]{1,0:T(8,128)(2,1)S(1)} %get-tuple-element.25.x, bf16[8,3,256,256]{3,2,1,0:T(8,128)(2,1)S(1)} %copy-done), custom_call_target="tpu_custom_call" | custom-call | flops 75497472 | bytes 1048576 | tf_op jit(solution)/shard_map/near_field/pallas_call | solution.py:432
  14.5 0.1 collective-permute-done.6.theirs
  14.6 1.2 %leaves.1 = bf16[32,2048]{1,0:T(8,128)(2,1)} custom-call(bf16[32,256]{1,0:T(8,128)(2,1)S(1)} %get-tuple-element.26.mine, bf16[32,256]{1,0:T(8,128)(2,1)S(1)} %collective-permute-done.6.theirs, f32[32,512]{1,0:T(8,128)S(1)} %get-tuple-element.28.state, bf16[320,512]{1,0:T(8,128)(2,1)S(1)} %get-tuple-element.29.spread, ...), custom_call_target="tpu_custom_call" | custom-call | bytes 1048576 | tf_op jit(solution)/shard_map/leaves/pallas_call | solution.py:432
  (2 shorter events, 0.0 us)
Async XLA Ops:
  0.0 10.8 %copy-start.1 = (bf16[12,2,64,64]{3,2,1,0:T(8,128)(2,1)S(1)}, bf16[12,2,64,64]{3,2,1,0:T(8,128)(2,1)}, u32[]{:S(2)}) copy-start(bf16[12,2,64,64]{3,2,1,0:T(8,128)(2,1)} %refs_9_.1) | copy-start | bytes 589828
  0.0 10.8 %copy-start.3 = (s32[12,3,128]{2,1,0:T(4,128)S(1)}, s32[12,3,128]{2,1,0:T(4,128)}, u32[]{:S(2)}) copy-start(s32[12,3,128]{2,1,0:T(4,128)} %codes.1) | copy-start | bytes 55300
  0.0 10.8 %copy-start.2 = (bf16[12,4,64,64]{3,2,1,0:T(8,128)(2,1)S(1)}, bf16[12,4,64,64]{3,2,1,0:T(8,128)(2,1)}, u32[]{:S(2)}) copy-start(bf16[12,4,64,64]{3,2,1,0:T(8,128)(2,1)} %couple.1) | copy-start | bytes 1179652
  1.7 11.0 %copy-start = (bf16[8,3,256,256]{3,2,1,0:T(8,128)(2,1)S(1)}, bf16[8,3,256,256]{3,2,1,0:T(8,128)(2,1)}, u32[]{:S(2)}) copy-start(bf16[8,3,256,256]{3,2,1,0:T(8,128)(2,1)} %blocks.3) | copy-start | bytes 9437188
  1.7 5.8 %collective-permute-start.2 = (bf16[32,128]{1,0:T(8,128)(2,1)S(1)}, bf16[32,128]{1,0:T(8,128)(2,1)S(1)}, u32[]{:S(2)}, u32[]{:S(2)}) collective-permute-start(bf16[32,128]{1,0:T(8,128)(2,1)S(1)} %get-tuple-element.24.refs_0_.refs_2_), channel_id=1, source_target_pairs={{0,9},{1,8},{2,11},{3,10},{4,13},{5,12},{6,15},{7,14},{8,1},{9,0},... | collective-permute-start | bytes 24584 | tf_op jit(solution)/shard_map/ppermute | solution.py:70
  5.3 5.5 %collective-permute-start = (bf16[192,128]{1,0:T(8,128)(2,1)S(1)}, bf16[192,128]{1,0:T(8,128)(2,1)S(1)}, u32[]{:S(2)}, u32[]{:S(2)}) collective-permute-start(bf16[192,128]{1,0:T(8,128)(2,1)S(1)} %get-tuple-element.18), channel_id=1, source_target_pairs={{0,1},{1,0},{2,3},{3,2},{4,5},{5,4},{6,7},{7,6},{8,9},{9,8},{10,11... | collective-permute-start | bytes 147464 | tf_op jit(solution)/shard_map/ppermute | solution.py:70
  5.9 4.8 %collective-permute-start.1 = (bf16[192,128]{1,0:T(8,128)(2,1)S(1)}, bf16[192,128]{1,0:T(8,128)(2,1)S(1)}, u32[]{:S(2)}, u32[]{:S(2)}) collective-permute-start(bf16[192,128]{1,0:T(8,128)(2,1)S(1)} %get-tuple-element.19), channel_id=1, source_target_pairs={{0,16},{1,2},{2,1},{3,4},{4,3},{5,6},{6,5},{7,8},{8,7},{9,10},{10,... | collective-permute-start | bytes 147464 | tf_op jit(solution)/shard_map/ppermute | solution.py:81
  7.5 5.5 %collective-permute-start.5 = (bf16[64,128]{1,0:T(8,128)(2,1)S(1)}, bf16[64,128]{1,0:T(8,128)(2,1)S(1)}, u32[]{:S(2)}, u32[]{:S(2)}) collective-permute-start(bf16[64,128]{1,0:T(8,128)(2,1)S(1)} %constant_dynamic-update-slice_fusion), channel_id=1, source_target_pairs={{0,6},{1,7},{2,4},{3,5},{4,2},{5,3},{6,0},{7,1},{8,14},{9,15},{10,... | collective-permute-start | bytes 49160 | tf_op jit(solution)/shard_map/ppermute | solution.py:70
  9.7 3.3 %collective-permute-start.4 = (bf16[64,128]{1,0:T(8,128)(2,1)S(1)}, bf16[64,128]{1,0:T(8,128)(2,1)S(1)}, u32[]{:S(2)}, u32[]{:S(2)}) collective-permute-start(bf16[64,128]{1,0:T(8,128)(2,1)S(1)} %constant_dynamic-update-slice_fusion), channel_id=1, source_target_pairs={{0,5},{1,4},{2,7},{3,6},{4,1},{5,0},{6,3},{7,2},{8,13},{9,12},{10,... | collective-permute-start | bytes 49160 | tf_op jit(solution)/shard_map/ppermute | solution.py:70
  10.0 3.2 %collective-permute-start.3 = (bf16[64,128]{1,0:T(8,128)(2,1)S(1)}, bf16[64,128]{1,0:T(8,128)(2,1)S(1)}, u32[]{:S(2)}, u32[]{:S(2)}) collective-permute-start(bf16[64,128]{1,0:T(8,128)(2,1)S(1)} %constant_dynamic-update-slice_fusion), channel_id=1, source_target_pairs={{0,3},{1,2},{2,1},{3,0},{4,7},{5,6},{6,5},{7,4},{8,11},{9,10},{10,... | collective-permute-start | bytes 49160 | tf_op jit(solution)/shard_map/ppermute | solution.py:70
  13.4 1.2 %collective-permute-start.6 = (bf16[32,256]{1,0:T(8,128)(2,1)S(1)}, bf16[32,256]{1,0:T(8,128)(2,1)S(1)}, u32[]{:S(2)}, u32[]{:S(2)}) collective-permute-start(bf16[32,256]{1,0:T(8,128)(2,1)S(1)} %get-tuple-element.27), channel_id=1, source_target_pairs={{0,1},{1,0},{2,3},{3,2},{4,5},{5,4},{6,7},{7,6},{8,9},{9,8},{10,11... | collective-permute-start | bytes 49160 | tf_op jit(solution)/shard_map/ppermute | solution.py:70

commit v6 on v5

--- a/solution.py
+++ b/solution.py
@@ -314,13 +314,13 @@
             picked.append(side(*both))
         lift = side(*[lifts[k][slot & ((1 << k) - 1)] for k in range(levels)])
         out = mm(lift, stack(*picked))
-        weights[2 * rank * i : 2 * rank * (i + 1)] = (out[: 2 * rank] + out[2 * rank :]).astype(BF)
+        weights[2 * rank * i : 2 * rank * (i + 1)] = halves(out[: 2 * rank] + out[2 * rank :], 1)
 
 
 def half_kernel(devices, slots, waits, masks, weights, *refs):
     *parts, mine, theirs, gathered = refs
     parts = parts[: len(parts) - waits]
-    rank = weights.shape[1] // 2
+    rank = weights.shape[1] // 4
     rows = mine.shape[0]
     p = lax.axis_index(AXES)
     gathered[...] = jnp.zeros(gathered.shape, BF)
@@ -328,6 +328,7 @@
     for slot, value in zip(slots, found):
         gathered[slot] = value
     top = mm(side(*found), weights[...])
+    top = top[:, : 2 * rank] + top[:, 2 * rank :]
     for j, out in ((0, mine), (1, theirs)):
         device = p ^ j
         at = lambda o: gathered[p ^ jnp.clip(device + o, 0, devices - 1)]
@@ -469,7 +470,7 @@
                 pltpu.VMEM((rows, leaves * rank), F32),
                 pltpu.VMEM((5 * rank, leaves * rank), BF),
                 pltpu.VMEM((16, 4 * rank), F32),
-                pltpu.VMEM((2 * rank * len(slots), 2 * rank), BF),
+                pltpu.VMEM((2 * rank * len(slots), 4 * rank), BF),
             ],
             (facing, away, own0, own1, codes, transfer, couple),
             "plan",

time: 15.9 us -> 15.9 us (level)
  no operation moved by 1% of the time
where the time goes in v6:
time: 15.9 us; the launch traced here: 15.8 us
  starting transfers between devices  9.38 us (59%)
  Pallas kernels  6.12 us (38%)
  waiting for transfers between devices  0.16 us (1%)
    ppermute x6, starting transfers between devices, exchanged(): return lax.ppermute(x, AXES, [(i, i ^ apart) for i in range(devices)])  7.86 us
    pallas_call x6, Pallas kernels, call(): pl.pallas_call(kernel, out_shape=shapes if single else list(shapes), comp...  6.12 us
    ppermute x1, starting transfers between devices, across_pairs(): return lax.ppermute(x, ('groups', *AXES), pairs)  1.52 us
  transfers between devices with their start and end apart: 7, of which 2 were waited for; matrix products, arithmetic and copies ran while one was open for 0% of the time, Pallas kernels for 19%

profile of v6, /device:TPU:0, one launch (start us, length us, event | category | flops | bytes accessed | tf_op | source)
XLA Modules:
  0.0 15.8 jit_solution(11017342925422891887)
XLA Ops:
  0.0 0.0 copy-start.1
  0.0 0.0 copy-start.3
  0.0 0.0 copy-start.2
  0.0 1.7 %first.1 = (bf16[32,2048]{1,0:T(8,128)(2,1)S(1)}, bf16[8,64,256]{2,1,0:T(8,128)(2,1)S(1)}, bf16[192,128]{1,0:T(8,128)(2,1)S(1)}, bf16[192,128]{1,0:T(8,128)(2,1)...) custom-call(bf16[32,2048]{1,0:T(8,128)(2,1)} %rhs_hbm.1, ...), custom_call_target="tpu_custom_call" | custom-call | flops 4294967296 | bytes 1048576 | tf_op jit(solution)/shard_map/first/pallas_call | solution.py:433
  1.7 0.0 copy-start
  1.7 3.5 %collective-permute-start.2 = (bf16[32,128]{1,0:T(8,128)(2,1)S(1)}, bf16[32,128]{1,0:T(8,128)(2,1)S(1)}, u32[]{:S(2)}, u32[]{:S(2)}) collective-permute-start(bf16[32,128]{1,0:T(8,128)(2,1)S(1)} %get-tuple-element.24.refs_0_.refs_2_), channel_id=1, source_target_pairs={{0,9},{1,8},{2,11},{3,10},{4,13},{5,12},{6,15},{7,14},{8,1},{9,0},... | collective-permute-start | bytes 24584 | tf_op jit(solution)/shard_map/ppermute | solution.py:70
  5.3 0.7 %collective-permute-start = (bf16[192,128]{1,0:T(8,128)(2,1)S(1)}, bf16[192,128]{1,0:T(8,128)(2,1)S(1)}, u32[]{:S(2)}, u32[]{:S(2)}) collective-permute-start(bf16[192,128]{1,0:T(8,128)(2,1)S(1)} %get-tuple-element.18), channel_id=1, source_target_pairs={{0,1},{1,0},{2,3},{3,2},{4,5},{5,4},{6,7},{7,6},{8,9},{9,8},{10,11... | collective-permute-start | bytes 147464 | tf_op jit(solution)/shard_map/ppermute | solution.py:70
  5.9 1.5 %collective-permute-start.1 = (bf16[192,128]{1,0:T(8,128)(2,1)S(1)}, bf16[192,128]{1,0:T(8,128)(2,1)S(1)}, u32[]{:S(2)}, u32[]{:S(2)}) collective-permute-start(bf16[192,128]{1,0:T(8,128)(2,1)S(1)} %get-tuple-element.19), channel_id=1, source_target_pairs={{0,16},{1,2},{2,1},{3,4},{4,3},{5,6},{6,5},{7,8},{8,7},{9,10},{10,... | collective-permute-start | bytes 147464 | tf_op jit(solution)/shard_map/ppermute | solution.py:81
  7.5 0.0 collective-permute-done.2.refs_1_.refs_3_
  7.5 2.2 %collective-permute-start.5 = (bf16[64,128]{1,0:T(8,128)(2,1)S(1)}, bf16[64,128]{1,0:T(8,128)(2,1)S(1)}, u32[]{:S(2)}, u32[]{:S(2)}) collective-permute-start(bf16[64,128]{1,0:T(8,128)(2,1)S(1)} %constant_dynamic-update-slice_fusion), channel_id=1, source_target_pairs={{0,6},{1,7},{2,4},{3,5},{4,2},{5,3},{6,0},{7,1},{8,14},{9,15},{10,... | collective-permute-start | bytes 49160 | tf_op jit(solution)/shard_map/ppermute | solution.py:70
  9.7 0.2 %collective-permute-start.4 = (bf16[64,128]{1,0:T(8,128)(2,1)S(1)}, bf16[64,128]{1,0:T(8,128)(2,1)S(1)}, u32[]{:S(2)}, u32[]{:S(2)}) collective-permute-start(bf16[64,128]{1,0:T(8,128)(2,1)S(1)} %constant_dynamic-update-slice_fusion), channel_id=1, source_target_pairs={{0,5},{1,4},{2,7},{3,6},{4,1},{5,0},{6,3},{7,2},{8,13},{9,12},{10,... | collective-permute-start | bytes 49160 | tf_op jit(solution)/shard_map/ppermute | solution.py:70
  10.0 0.8 %collective-permute-start.3 = (bf16[64,128]{1,0:T(8,128)(2,1)S(1)}, bf16[64,128]{1,0:T(8,128)(2,1)S(1)}, u32[]{:S(2)}, u32[]{:S(2)}) collective-permute-start(bf16[64,128]{1,0:T(8,128)(2,1)S(1)} %constant_dynamic-update-slice_fusion), channel_id=1, source_target_pairs={{0,3},{1,2},{2,1},{3,0},{4,7},{5,6},{6,5},{7,4},{8,11},{9,10},{10,... | collective-permute-start | bytes 49160 | tf_op jit(solution)/shard_map/ppermute | solution.py:70
  10.7 0.0 collective-permute-done.facing
  10.8 0.0 collective-permute-done.1.away
  10.8 0.0 copy-done.1
  10.8 0.0 copy-done.3
  10.8 0.0 copy-done.2
  10.8 1.9 %plan.1 = (f32[32,512]{1,0:T(8,128)S(1)}, bf16[320,512]{1,0:T(8,128)(2,1)S(1)}, f32[16,256]{1,0:T(8,128)S(1)}, bf16[1024,256]{1,0:T(8,128)(2,1)S(1)}) custom-call(bf16[192,128]{1,0:T(8,128)(2,1)S(1)} %collective-permute-done.facing, bf16[192,128]{1,0:T(8,128)(2,1)S(1)} %collective-permute-done.1.away, bf16[128,128]{1,0:T(8,128)(2,1)S(1)} %get-tuple-element.20.own0, ...), custom_call_target="tpu_custom_call" | custom-call | flops 1073741824 | bytes 1048576 | tf_op jit(solution)/shard_map/plan/pallas_call | solution.py:433
  12.7 0.0 copy-done
  12.7 0.3 %near_field.2.refs_5_.refs_0_ = f32[32,512]{1,0:T(8,128)S(1)} custom-call(bf16[192,128]{1,0:T(8,128)(2,1)S(1)} %collective-permute-done.facing, bf16[192,128]{1,0:T(8,128)(2,1)S(1)} %collective-permute-done.1.away, bf16[32,2048]{1,0:T(8,128)(2,1)S(1)} %get-tuple-element.25.x, bf16[8,3,256,256]{3,2,1,0:T(8,128)(2,1)S(1)} %copy-done), custom_call_target="tpu_custom_call" | custom-call | flops 25165824 | bytes 1048576 | tf_op jit(solution)/shard_map/near_field/pallas_call | solution.py:433
  13.0 0.0 collective-permute-done.5.refs_4_.refs_6_
  13.0 0.0 collective-permute-done.4.refs_3_.refs_5_
  13.1 0.1 collective-permute-done.3.refs_2_.refs_4_
  13.1 0.3 %half.1 = (bf16[32,256]{1,0:T(8,128)(2,1)S(1)}, bf16[32,256]{1,0:T(8,128)(2,1)S(1)}) custom-call(f32[16,256]{1,0:T(8,128)S(1)} %get-tuple-element.22.masks.refs_7_, bf16[1024,256]{1,0:T(8,128)(2,1)S(1)} %get-tuple-element.23.weights.refs_8_, bf16[32,128]{1,0:T(8,128)(2,1)S(1)} %get-tuple-element.24.refs_0_.refs_2_, ...), custom_call_target="tpu_custom_call" | custom-call | bytes 1048576 | tf_op jit(solution)/shard_map/half/pallas_call | solution.py:433
  13.4 0.4 %collective-permute-start.6 = (bf16[32,256]{1,0:T(8,128)(2,1)S(1)}, bf16[32,256]{1,0:T(8,128)(2,1)S(1)}, u32[]{:S(2)}, u32[]{:S(2)}) collective-permute-start(bf16[32,256]{1,0:T(8,128)(2,1)S(1)} %get-tuple-element.27), channel_id=1, source_target_pairs={{0,1},{1,0},{2,3},{3,2},{4,5},{5,4},{6,7},{7,6},{8,9},{9,8},{10,11... | collective-permute-start | bytes 49160 | tf_op jit(solution)/shard_map/ppermute | solution.py:70
  13.8 0.8 %near_field.3.refs_1_ = f32[32,1536]{1,0:T(8,128)S(1)} custom-call(bf16[192,128]{1,0:T(8,128)(2,1)S(1)} %collective-permute-done.facing, bf16[192,128]{1,0:T(8,128)(2,1)S(1)} %collective-permute-done.1.away, bf16[32,2048]{1,0:T(8,128)(2,1)S(1)} %get-tuple-element.25.x, bf16[8,3,256,256]{3,2,1,0:T(8,128)(2,1)S(1)} %copy-done), custom_call_target="tpu_custom_call" | custom-call | flops 75497472 | bytes 1048576 | tf_op jit(solution)/shard_map/near_field/pallas_call | solution.py:433
  14.5 0.1 collective-permute-done.6.theirs
  14.6 1.2 %leaves.1 = bf16[32,2048]{1,0:T(8,128)(2,1)} custom-call(bf16[32,256]{1,0:T(8,128)(2,1)S(1)} %get-tuple-element.26.mine, bf16[32,256]{1,0:T(8,128)(2,1)S(1)} %collective-permute-done.6.theirs, f32[32,512]{1,0:T(8,128)S(1)} %get-tuple-element.28.state, bf16[320,512]{1,0:T(8,128)(2,1)S(1)} %get-tuple-element.29.spread, ...), custom_call_target="tpu_custom_call" | custom-call | bytes 1048576 | tf_op jit(solution)/shard_map/leaves/pallas_call | solution.py:433
  (2 shorter events, 0.0 us)
Async XLA Ops:
  0.0 10.8 %copy-start.1 = (bf16[12,2,64,64]{3,2,1,0:T(8,128)(2,1)S(1)}, bf16[12,2,64,64]{3,2,1,0:T(8,128)(2,1)}, u32[]{:S(2)}) copy-start(bf16[12,2,64,64]{3,2,1,0:T(8,128)(2,1)} %refs_9_.1) | copy-start | bytes 589828
  0.0 10.8 %copy-start.3 = (s32[12,3,128]{2,1,0:T(4,128)S(1)}, s32[12,3,128]{2,1,0:T(4,128)}, u32[]{:S(2)}) copy-start(s32[12,3,128]{2,1,0:T(4,128)} %codes.1) | copy-start | bytes 55300
  0.0 10.8 %copy-start.2 = (bf16[12,4,64,64]{3,2,1,0:T(8,128)(2,1)S(1)}, bf16[12,4,64,64]{3,2,1,0:T(8,128)(2,1)}, u32[]{:S(2)}) copy-start(bf16[12,4,64,64]{3,2,1,0:T(8,128)(2,1)} %couple.1) | copy-start | bytes 1179652
  1.7 11.0 %copy-start = (bf16[8,3,256,256]{3,2,1,0:T(8,128)(2,1)S(1)}, bf16[8,3,256,256]{3,2,1,0:T(8,128)(2,1)}, u32[]{:S(2)}) copy-start(bf16[8,3,256,256]{3,2,1,0:T(8,128)(2,1)} %blocks.3) | copy-start | bytes 9437188
  1.7 5.8 %collective-permute-start.2 = (bf16[32,128]{1,0:T(8,128)(2,1)S(1)}, bf16[32,128]{1,0:T(8,128)(2,1)S(1)}, u32[]{:S(2)}, u32[]{:S(2)}) collective-permute-start(bf16[32,128]{1,0:T(8,128)(2,1)S(1)} %get-tuple-element.24.refs_0_.refs_2_), channel_id=1, source_target_pairs={{0,9},{1,8},{2,11},{3,10},{4,13},{5,12},{6,15},{7,14},{8,1},{9,0},... | collective-permute-start | bytes 24584 | tf_op jit(solution)/shard_map/ppermute | solution.py:70
  5.3 5.5 %collective-permute-start = (bf16[192,128]{1,0:T(8,128)(2,1)S(1)}, bf16[192,128]{1,0:T(8,128)(2,1)S(1)}, u32[]{:S(2)}, u32[]{:S(2)}) collective-permute-start(bf16[192,128]{1,0:T(8,128)(2,1)S(1)} %get-tuple-element.18), channel_id=1, source_target_pairs={{0,1},{1,0},{2,3},{3,2},{4,5},{5,4},{6,7},{7,6},{8,9},{9,8},{10,11... | collective-permute-start | bytes 147464 | tf_op jit(solution)/shard_map/ppermute | solution.py:70
  5.9 4.8 %collective-permute-start.1 = (bf16[192,128]{1,0:T(8,128)(2,1)S(1)}, bf16[192,128]{1,0:T(8,128)(2,1)S(1)}, u32[]{:S(2)}, u32[]{:S(2)}) collective-permute-start(bf16[192,128]{1,0:T(8,128)(2,1)S(1)} %get-tuple-element.19), channel_id=1, source_target_pairs={{0,16},{1,2},{2,1},{3,4},{4,3},{5,6},{6,5},{7,8},{8,7},{9,10},{10,... | collective-permute-start | bytes 147464 | tf_op jit(solution)/shard_map/ppermute | solution.py:81
  7.5 5.6 %collective-permute-start.5 = (bf16[64,128]{1,0:T(8,128)(2,1)S(1)}, bf16[64,128]{1,0:T(8,128)(2,1)S(1)}, u32[]{:S(2)}, u32[]{:S(2)}) collective-permute-start(bf16[64,128]{1,0:T(8,128)(2,1)S(1)} %constant_dynamic-update-slice_fusion), channel_id=1, source_target_pairs={{0,6},{1,7},{2,4},{3,5},{4,2},{5,3},{6,0},{7,1},{8,14},{9,15},{10,... | collective-permute-start | bytes 49160 | tf_op jit(solution)/shard_map/ppermute | solution.py:70
  9.7 3.3 %collective-permute-start.4 = (bf16[64,128]{1,0:T(8,128)(2,1)S(1)}, bf16[64,128]{1,0:T(8,128)(2,1)S(1)}, u32[]{:S(2)}, u32[]{:S(2)}) collective-permute-start(bf16[64,128]{1,0:T(8,128)(2,1)S(1)} %constant_dynamic-update-slice_fusion), channel_id=1, source_target_pairs={{0,5},{1,4},{2,7},{3,6},{4,1},{5,0},{6,3},{7,2},{8,13},{9,12},{10,... | collective-permute-start | bytes 49160 | tf_op jit(solution)/shard_map/ppermute | solution.py:70
  10.0 3.2 %collective-permute-start.3 = (bf16[64,128]{1,0:T(8,128)(2,1)S(1)}, bf16[64,128]{1,0:T(8,128)(2,1)S(1)}, u32[]{:S(2)}, u32[]{:S(2)}) collective-permute-start(bf16[64,128]{1,0:T(8,128)(2,1)S(1)} %constant_dynamic-update-slice_fusion), channel_id=1, source_target_pairs={{0,3},{1,2},{2,1},{3,0},{4,7},{5,6},{6,5},{7,4},{8,11},{9,10},{10,... | collective-permute-start | bytes 49160 | tf_op jit(solution)/shard_map/ppermute | solution.py:70
  13.4 1.2 %collective-permute-start.6 = (bf16[32,256]{1,0:T(8,128)(2,1)S(1)}, bf16[32,256]{1,0:T(8,128)(2,1)S(1)}, u32[]{:S(2)}, u32[]{:S(2)}) collective-permute-start(bf16[32,256]{1,0:T(8,128)(2,1)S(1)} %get-tuple-element.27), channel_id=1, source_target_pairs={{0,1},{1,0},{2,3},{3,2},{4,5},{5,4},{6,7},{7,6},{8,9},{9,8},{10,11... | collective-permute-start | bytes 49160 | tf_op jit(solution)/shard_map/ppermute | solution.py:70

commit v7 on v6

--- a/solution.py
+++ b/solution.py
@@ -271,7 +271,7 @@
 
 
 def dense_plan_kernel(
-    levels, slots, facing, away, own0, own1, codes, transfer, couple, state, spread, masks, weights, chosen
+    levels, slots, away, facing, own0, own1, codes, transfer, couple, state, spread, masks, weights, chosen
 ):
     rank = transfer.shape[-1]
     leaves = spread.shape[1] // rank
@@ -472,7 +472,7 @@
                 pltpu.VMEM((16, 4 * rank), F32),
                 pltpu.VMEM((2 * rank * len(slots), 4 * rank), BF),
             ],
-            (facing, away, own0, own1, codes, transfer, couple),
+            (away, facing, own0, own1, codes, transfer, couple),
             "plan",
             1 << 30,
             scratch_shapes=[pltpu.VMEM((2 * levels, 5, rank, rank), BF)],

time: 15.9 us -> 15.9 us (level)
  starting transfers between devices: 9.38 us -> 8.87 us
  waiting for transfers between devices: 0.16 us -> 0.67 us
    ppermute x6, starting transfers between devices: 7.86 us -> 7.34 us  [exchanged(): return lax.ppermute(x, AXES, [(i, i ^ apart) for i in range(devices)])]
    ppermute x6, waiting for transfers between devices: 0.16 us -> 0.67 us  [exchanged(): return lax.ppermute(x, AXES, [(i, i ^ apart) for i in range(devices)])]
where the time goes in v7:
time: 15.9 us; the launch traced here: 15.8 us
  starting transfers between devices  8.87 us (56%)
  Pallas kernels  6.11 us (38%)
  waiting for transfers between devices  0.67 us (4%)
    ppermute x6, starting transfers between devices, exchanged(): return lax.ppermute(x, AXES, [(i, i ^ apart) for i in range(devices)])  7.34 us
    pallas_call x6, Pallas kernels, call(): pl.pallas_call(kernel, out_shape=shapes if single else list(shapes), comp...  6.11 us
    ppermute x1, starting transfers between devices, across_pairs(): return lax.ppermute(x, ('groups', *AXES), pairs)  1.52 us
    ppermute x6, waiting for transfers between devices, exchanged(): return lax.ppermute(x, AXES, [(i, i ^ apart) for i in range(devices)])  0.67 us
  transfers between devices with their start and end apart: 7, of which 2 were waited for; matrix products, arithmetic and copies ran while one was open for 0% of the time, Pallas kernels for 19%

profile of v7, /device:TPU:0, one launch (start us, length us, event | category | flops | bytes accessed | tf_op | source)
XLA Modules:
  0.0 15.8 jit_solution(10042019873460183752)
XLA Ops:
  0.0 0.0 copy-start.1
  0.0 0.0 copy-start.3
  0.0 0.0 copy-start.2
  0.0 1.7 %first.1 = (bf16[32,2048]{1,0:T(8,128)(2,1)S(1)}, bf16[8,64,256]{2,1,0:T(8,128)(2,1)S(1)}, bf16[192,128]{1,0:T(8,128)(2,1)S(1)}, bf16[192,128]{1,0:T(8,128)(2,1)...) custom-call(bf16[32,2048]{1,0:T(8,128)(2,1)} %rhs_hbm.1, ...), custom_call_target="tpu_custom_call" | custom-call | flops 4294967296 | bytes 1048576 | tf_op jit(solution)/shard_map/first/pallas_call | solution.py:433
  1.7 0.0 copy-start
  1.7 3.5 %collective-permute-start.2 = (bf16[32,128]{1,0:T(8,128)(2,1)S(1)}, bf16[32,128]{1,0:T(8,128)(2,1)S(1)}, u32[]{:S(2)}, u32[]{:S(2)}) collective-permute-start(bf16[32,128]{1,0:T(8,128)(2,1)S(1)} %get-tuple-element.24.refs_0_.refs_2_), channel_id=1, source_target_pairs={{0,9},{1,8},{2,11},{3,10},{4,13},{5,12},{6,15},{7,14},{8,1},{9,0},... | collective-permute-start | bytes 24584 | tf_op jit(solution)/shard_map/ppermute | solution.py:70
  5.3 1.5 %collective-permute-start = (bf16[192,128]{1,0:T(8,128)(2,1)S(1)}, bf16[192,128]{1,0:T(8,128)(2,1)S(1)}, u32[]{:S(2)}, u32[]{:S(2)}) collective-permute-start(bf16[192,128]{1,0:T(8,128)(2,1)S(1)} %get-tuple-element.18), channel_id=1, source_target_pairs={{0,16},{1,2},{2,1},{3,4},{4,3},{5,6},{6,5},{7,8},{8,7},{9,10},{10,... | collective-permute-start | bytes 147464 | tf_op jit(solution)/shard_map/ppermute | solution.py:81
  6.8 0.1 collective-permute-start.1
  6.9 0.0 collective-permute-done.2.refs_1_.refs_3_
  6.9 2.8 %collective-permute-start.5 = (bf16[64,128]{1,0:T(8,128)(2,1)S(1)}, bf16[64,128]{1,0:T(8,128)(2,1)S(1)}, u32[]{:S(2)}, u32[]{:S(2)}) collective-permute-start(bf16[64,128]{1,0:T(8,128)(2,1)S(1)} %constant_dynamic-update-slice_fusion), channel_id=1, source_target_pairs={{0,6},{1,7},{2,4},{3,5},{4,2},{5,3},{6,0},{7,1},{8,14},{9,15},{10,... | collective-permute-start | bytes 49160 | tf_op jit(solution)/shard_map/ppermute | solution.py:70
  9.7 0.0 collective-permute-start.4
  9.7 0.4 %collective-permute-start.3 = (bf16[64,128]{1,0:T(8,128)(2,1)S(1)}, bf16[64,128]{1,0:T(8,128)(2,1)S(1)}, u32[]{:S(2)}, u32[]{:S(2)}) collective-permute-start(bf16[64,128]{1,0:T(8,128)(2,1)S(1)} %constant_dynamic-update-slice_fusion), channel_id=1, source_target_pairs={{0,3},{1,2},{2,1},{3,0},{4,7},{5,6},{6,5},{7,4},{8,11},{9,10},{10,... | collective-permute-start | bytes 49160 | tf_op jit(solution)/shard_map/ppermute | solution.py:70
  10.2 0.0 collective-permute-done.away
  10.2 0.0 collective-permute-done.1.facing
  10.2 0.0 copy-done.1
  10.2 0.0 copy-done.3
  10.2 0.0 copy-done.2
  10.2 1.9 %plan.1 = (f32[32,512]{1,0:T(8,128)S(1)}, bf16[320,512]{1,0:T(8,128)(2,1)S(1)}, f32[16,256]{1,0:T(8,128)S(1)}, bf16[1024,256]{1,0:T(8,128)(2,1)S(1)}) custom-call(bf16[192,128]{1,0:T(8,128)(2,1)S(1)} %collective-permute-done.away, bf16[192,128]{1,0:T(8,128)(2,1)S(1)} %collective-permute-done.1.facing, bf16[128,128]{1,0:T(8,128)(2,1)S(1)} %get-tuple-element.20.own0, ...), custom_call_target="tpu_custom_call" | custom-call | flops 1073741824 | bytes 1048576 | tf_op jit(solution)/shard_map/plan/pallas_call | solution.py:433
  12.1 0.0 copy-done
  12.1 0.3 %near_field.2.refs_5_.refs_0_ = f32[32,512]{1,0:T(8,128)S(1)} custom-call(bf16[192,128]{1,0:T(8,128)(2,1)S(1)} %collective-permute-done.1.facing, bf16[192,128]{1,0:T(8,128)(2,1)S(1)} %collective-permute-done.away, bf16[32,2048]{1,0:T(8,128)(2,1)S(1)} %get-tuple-element.25.x, bf16[8,3,256,256]{3,2,1,0:T(8,128)(2,1)S(1)} %copy-done), custom_call_target="tpu_custom_call" | custom-call | flops 25165824 | bytes 1048576 | tf_op jit(solution)/shard_map/near_field/pallas_call | solution.py:433
  12.4 0.0 collective-permute-done.5.refs_4_.refs_6_
  12.5 0.6 %collective-permute-done.4.refs_3_.refs_5_ = bf16[64,128]{1,0:T(8,128)(2,1)S(1)} collective-permute-done((bf16[64,128]{1,0:T(8,128)(2,1)S(1)}, bf16[64,128]{1,0:T(8,128)(2,1)S(1)}, u32[]{:S(2)}, u32[]{:S(2)}) %collective-permute-start.4) | collective-permute-done | bytes 16416 | tf_op jit(solution)/shard_map/ppermute | solution.py:70
  13.0 0.0 collective-permute-done.3.refs_2_.refs_4_
  13.1 0.3 %half.1 = (bf16[32,256]{1,0:T(8,128)(2,1)S(1)}, bf16[32,256]{1,0:T(8,128)(2,1)S(1)}) custom-call(f32[16,256]{1,0:T(8,128)S(1)} %get-tuple-element.22.masks.refs_7_, bf16[1024,256]{1,0:T(8,128)(2,1)S(1)} %get-tuple-element.23.weights.refs_8_, bf16[32,128]{1,0:T(8,128)(2,1)S(1)} %get-tuple-element.24.refs_0_.refs_2_, ...), custom_call_target="tpu_custom_call" | custom-call | bytes 1048576 | tf_op jit(solution)/shard_map/half/pallas_call | solution.py:433
  13.3 0.4 %collective-permute-start.6 = (bf16[32,256]{1,0:T(8,128)(2,1)S(1)}, bf16[32,256]{1,0:T(8,128)(2,1)S(1)}, u32[]{:S(2)}, u32[]{:S(2)}) collective-permute-start(bf16[32,256]{1,0:T(8,128)(2,1)S(1)} %get-tuple-element.27), channel_id=1, source_target_pairs={{0,1},{1,0},{2,3},{3,2},{4,5},{5,4},{6,7},{7,6},{8,9},{9,8},{10,11... | collective-permute-start | bytes 49160 | tf_op jit(solution)/shard_map/ppermute | solution.py:70
  13.8 0.8 %near_field.3.refs_1_ = f32[32,1536]{1,0:T(8,128)S(1)} custom-call(bf16[192,128]{1,0:T(8,128)(2,1)S(1)} %collective-permute-done.1.facing, bf16[192,128]{1,0:T(8,128)(2,1)S(1)} %collective-permute-done.away, bf16[32,2048]{1,0:T(8,128)(2,1)S(1)} %get-tuple-element.25.x, bf16[8,3,256,256]{3,2,1,0:T(8,128)(2,1)S(1)} %copy-done), custom_call_target="tpu_custom_call" | custom-call | flops 75497472 | bytes 1048576 | tf_op jit(solution)/shard_map/near_field/pallas_call | solution.py:433
  14.5 0.1 collective-permute-done.6.theirs
  14.6 1.2 %leaves.1 = bf16[32,2048]{1,0:T(8,128)(2,1)} custom-call(bf16[32,256]{1,0:T(8,128)(2,1)S(1)} %get-tuple-element.26.mine, bf16[32,256]{1,0:T(8,128)(2,1)S(1)} %collective-permute-done.6.theirs, f32[32,512]{1,0:T(8,128)S(1)} %get-tuple-element.28.state, bf16[320,512]{1,0:T(8,128)(2,1)S(1)} %get-tuple-element.29.spread, ...), custom_call_target="tpu_custom_call" | custom-call | bytes 1048576 | tf_op jit(solution)/shard_map/leaves/pallas_call | solution.py:433
  (2 shorter events, 0.0 us)
Async XLA Ops:
  0.0 10.2 %copy-start.1 = (bf16[12,2,64,64]{3,2,1,0:T(8,128)(2,1)S(1)}, bf16[12,2,64,64]{3,2,1,0:T(8,128)(2,1)}, u32[]{:S(2)}) copy-start(bf16[12,2,64,64]{3,2,1,0:T(8,128)(2,1)} %refs_9_.1) | copy-start | bytes 589828
  0.0 10.2 %copy-start.3 = (s32[12,3,128]{2,1,0:T(4,128)S(1)}, s32[12,3,128]{2,1,0:T(4,128)}, u32[]{:S(2)}) copy-start(s32[12,3,128]{2,1,0:T(4,128)} %codes.1) | copy-start | bytes 55300
  0.0 10.2 %copy-start.2 = (bf16[12,4,64,64]{3,2,1,0:T(8,128)(2,1)S(1)}, bf16[12,4,64,64]{3,2,1,0:T(8,128)(2,1)}, u32[]{:S(2)}) copy-start(bf16[12,4,64,64]{3,2,1,0:T(8,128)(2,1)} %couple.1) | copy-start | bytes 1179652
  1.7 10.4 %copy-start = (bf16[8,3,256,256]{3,2,1,0:T(8,128)(2,1)S(1)}, bf16[8,3,256,256]{3,2,1,0:T(8,128)(2,1)}, u32[]{:S(2)}) copy-start(bf16[8,3,256,256]{3,2,1,0:T(8,128)(2,1)} %blocks.3) | copy-start | bytes 9437188
  1.7 5.2 %collective-permute-start.2 = (bf16[32,128]{1,0:T(8,128)(2,1)S(1)}, bf16[32,128]{1,0:T(8,128)(2,1)S(1)}, u32[]{:S(2)}, u32[]{:S(2)}) collective-permute-start(bf16[32,128]{1,0:T(8,128)(2,1)S(1)} %get-tuple-element.24.refs_0_.refs_2_), channel_id=1, source_target_pairs={{0,9},{1,8},{2,11},{3,10},{4,13},{5,12},{6,15},{7,14},{8,1},{9,0},... | collective-permute-start | bytes 24584 | tf_op jit(solution)/shard_map/ppermute | solution.py:70
  5.3 4.9 %collective-permute-start = (bf16[192,128]{1,0:T(8,128)(2,1)S(1)}, bf16[192,128]{1,0:T(8,128)(2,1)S(1)}, u32[]{:S(2)}, u32[]{:S(2)}) collective-permute-start(bf16[192,128]{1,0:T(8,128)(2,1)S(1)} %get-tuple-element.18), channel_id=1, source_target_pairs={{0,16},{1,2},{2,1},{3,4},{4,3},{5,6},{6,5},{7,8},{8,7},{9,10},{10,... | collective-permute-start | bytes 147464 | tf_op jit(solution)/shard_map/ppermute | solution.py:81
  6.8 3.4 %collective-permute-start.1 = (bf16[192,128]{1,0:T(8,128)(2,1)S(1)}, bf16[192,128]{1,0:T(8,128)(2,1)S(1)}, u32[]{:S(2)}, u32[]{:S(2)}) collective-permute-start(bf16[192,128]{1,0:T(8,128)(2,1)S(1)} %get-tuple-element.19), channel_id=1, source_target_pairs={{0,1},{1,0},{2,3},{3,2},{4,5},{5,4},{6,7},{7,6},{8,9},{9,8},{10,11... | collective-permute-start | bytes 147464 | tf_op jit(solution)/shard_map/ppermute | solution.py:70
  6.9 5.6 %collective-permute-start.5 = (bf16[64,128]{1,0:T(8,128)(2,1)S(1)}, bf16[64,128]{1,0:T(8,128)(2,1)S(1)}, u32[]{:S(2)}, u32[]{:S(2)}) collective-permute-start(bf16[64,128]{1,0:T(8,128)(2,1)S(1)} %constant_dynamic-update-slice_fusion), channel_id=1, source_target_pairs={{0,6},{1,7},{2,4},{3,5},{4,2},{5,3},{6,0},{7,1},{8,14},{9,15},{10,... | collective-permute-start | bytes 49160 | tf_op jit(solution)/shard_map/ppermute | solution.py:70
  9.7 3.3 %collective-permute-start.4 = (bf16[64,128]{1,0:T(8,128)(2,1)S(1)}, bf16[64,128]{1,0:T(8,128)(2,1)S(1)}, u32[]{:S(2)}, u32[]{:S(2)}) collective-permute-start(bf16[64,128]{1,0:T(8,128)(2,1)S(1)} %constant_dynamic-update-slice_fusion), channel_id=1, source_target_pairs={{0,5},{1,4},{2,7},{3,6},{4,1},{5,0},{6,3},{7,2},{8,13},{9,12},{10,... | collective-permute-start | bytes 49160 | tf_op jit(solution)/shard_map/ppermute | solution.py:70
  9.7 3.3 %collective-permute-start.3 = (bf16[64,128]{1,0:T(8,128)(2,1)S(1)}, bf16[64,128]{1,0:T(8,128)(2,1)S(1)}, u32[]{:S(2)}, u32[]{:S(2)}) collective-permute-start(bf16[64,128]{1,0:T(8,128)(2,1)S(1)} %constant_dynamic-update-slice_fusion), channel_id=1, source_target_pairs={{0,3},{1,2},{2,1},{3,0},{4,7},{5,6},{6,5},{7,4},{8,11},{9,10},{10,... | collective-permute-start | bytes 49160 | tf_op jit(solution)/shard_map/ppermute | solution.py:70
  13.3 1.3 %collective-permute-start.6 = (bf16[32,256]{1,0:T(8,128)(2,1)S(1)}, bf16[32,256]{1,0:T(8,128)(2,1)S(1)}, u32[]{:S(2)}, u32[]{:S(2)}) collective-permute-start(bf16[32,256]{1,0:T(8,128)(2,1)S(1)} %get-tuple-element.27), channel_id=1, source_target_pairs={{0,1},{1,0},{2,3},{3,2},{4,5},{5,4},{6,7},{7,6},{8,9},{9,8},{10,11... | collective-permute-start | bytes 49160 | tf_op jit(solution)/shard_map/ppermute | solution.py:70

commit v8 on v7

--- a/solution.py
+++ b/solution.py
@@ -13,7 +13,7 @@
 BF = jnp.bfloat16
 F32 = jnp.float32
 LANES = 64
-SHARE = 2
+SHARE = 3
 
 
 def mm(a, b):

time: 15.9 us -> 15.9 us (level)
  no operation moved by 1% of the time
where the time goes in v8:
time: 15.9 us; the launch traced here: 15.8 us
  starting transfers between devices  8.87 us (56%)
  Pallas kernels  6.18 us (39%)
  waiting for transfers between devices  0.62 us (4%)
    ppermute x6, starting transfers between devices, exchanged(): return lax.ppermute(x, AXES, [(i, i ^ apart) for i in range(devices)])  7.34 us
    pallas_call x6, Pallas kernels, call(): pl.pallas_call(kernel, out_shape=shapes if single else list(shapes), comp...  6.18 us
    ppermute x1, starting transfers between devices, across_pairs(): return lax.ppermute(x, ('groups', *AXES), pairs)  1.52 us
    ppermute x6, waiting for transfers between devices, exchanged(): return lax.ppermute(x, AXES, [(i, i ^ apart) for i in range(devices)])  0.62 us
  transfers between devices with their start and end apart: 7, of which 2 were waited for; matrix products, arithmetic and copies ran while one was open for 0% of the time, Pallas kernels for 19%

profile of v8, /device:TPU:0, one launch (start us, length us, event | category | flops | bytes accessed | tf_op | source)
XLA Modules:
  0.0 15.8 jit_solution(537099602682581632)
XLA Ops:
  0.0 0.0 copy-start.1
  0.0 0.0 copy-start.3
  0.0 0.0 copy-start.2
  0.0 1.7 %first.1 = (bf16[32,2048]{1,0:T(8,128)(2,1)S(1)}, bf16[8,64,256]{2,1,0:T(8,128)(2,1)S(1)}, bf16[192,128]{1,0:T(8,128)(2,1)S(1)}, bf16[192,128]{1,0:T(8,128)(2,1)...) custom-call(bf16[32,2048]{1,0:T(8,128)(2,1)} %rhs_hbm.1, ...), custom_call_target="tpu_custom_call" | custom-call | flops 4294967296 | bytes 1048576 | tf_op jit(solution)/shard_map/first/pallas_call | solution.py:433
  1.7 0.0 copy-start
  1.7 3.5 %collective-permute-start.2 = (bf16[32,128]{1,0:T(8,128)(2,1)S(1)}, bf16[32,128]{1,0:T(8,128)(2,1)S(1)}, u32[]{:S(2)}, u32[]{:S(2)}) collective-permute-start(bf16[32,128]{1,0:T(8,128)(2,1)S(1)} %get-tuple-element.24.refs_0_.refs_2_), channel_id=1, source_target_pairs={{0,9},{1,8},{2,11},{3,10},{4,13},{5,12},{6,15},{7,14},{8,1},{9,0},... | collective-permute-start | bytes 24584 | tf_op jit(solution)/shard_map/ppermute | solution.py:70
  5.3 1.5 %collective-permute-start = (bf16[192,128]{1,0:T(8,128)(2,1)S(1)}, bf16[192,128]{1,0:T(8,128)(2,1)S(1)}, u32[]{:S(2)}, u32[]{:S(2)}) collective-permute-start(bf16[192,128]{1,0:T(8,128)(2,1)S(1)} %get-tuple-element.18), channel_id=1, source_target_pairs={{0,16},{1,2},{2,1},{3,4},{4,3},{5,6},{6,5},{7,8},{8,7},{9,10},{10,... | collective-permute-start | bytes 147464 | tf_op jit(solution)/shard_map/ppermute | solution.py:81
  6.8 0.1 collective-permute-start.1
  6.9 0.0 collective-permute-done.2.refs_1_.refs_3_
  6.9 2.8 %collective-permute-start.5 = (bf16[64,128]{1,0:T(8,128)(2,1)S(1)}, bf16[64,128]{1,0:T(8,128)(2,1)S(1)}, u32[]{:S(2)}, u32[]{:S(2)}) collective-permute-start(bf16[64,128]{1,0:T(8,128)(2,1)S(1)} %constant_dynamic-update-slice_fusion), channel_id=1, source_target_pairs={{0,6},{1,7},{2,4},{3,5},{4,2},{5,3},{6,0},{7,1},{8,14},{9,15},{10,... | collective-permute-start | bytes 49160 | tf_op jit(solution)/shard_map/ppermute | solution.py:70
  9.7 0.0 collective-permute-start.4
  9.7 0.4 %collective-permute-start.3 = (bf16[64,128]{1,0:T(8,128)(2,1)S(1)}, bf16[64,128]{1,0:T(8,128)(2,1)S(1)}, u32[]{:S(2)}, u32[]{:S(2)}) collective-permute-start(bf16[64,128]{1,0:T(8,128)(2,1)S(1)} %constant_dynamic-update-slice_fusion), channel_id=1, source_target_pairs={{0,3},{1,2},{2,1},{3,0},{4,7},{5,6},{6,5},{7,4},{8,11},{9,10},{10,... | collective-permute-start | bytes 49160 | tf_op jit(solution)/shard_map/ppermute | solution.py:70
  10.2 0.0 collective-permute-done.away
  10.2 0.0 collective-permute-done.1.facing
  10.2 0.0 copy-done.1
  10.2 0.0 copy-done.3
  10.2 0.0 copy-done.2
  10.2 1.9 %plan.1 = (f32[32,512]{1,0:T(8,128)S(1)}, bf16[320,512]{1,0:T(8,128)(2,1)S(1)}, f32[16,256]{1,0:T(8,128)S(1)}, bf16[1024,256]{1,0:T(8,128)(2,1)S(1)}) custom-call(bf16[192,128]{1,0:T(8,128)(2,1)S(1)} %collective-permute-done.away, bf16[192,128]{1,0:T(8,128)(2,1)S(1)} %collective-permute-done.1.facing, bf16[128,128]{1,0:T(8,128)(2,1)S(1)} %get-tuple-element.20.own0, ...), custom_call_target="tpu_custom_call" | custom-call | flops 1073741824 | bytes 1048576 | tf_op jit(solution)/shard_map/plan/pallas_call | solution.py:433
  12.1 0.0 copy-done
  12.1 0.5 %near_field.2.refs_5_.refs_0_ = f32[32,768]{1,0:T(8,128)S(1)} custom-call(bf16[192,128]{1,0:T(8,128)(2,1)S(1)} %collective-permute-done.1.facing, bf16[192,128]{1,0:T(8,128)(2,1)S(1)} %collective-permute-done.away, bf16[32,2048]{1,0:T(8,128)(2,1)S(1)} %get-tuple-element.25.x, bf16[8,3,256,256]{3,2,1,0:T(8,128)(2,1)S(1)} %copy-done), custom_call_target="tpu_custom_call" | custom-call | flops 37748736 | bytes 1048576 | tf_op jit(solution)/shard_map/near_field/pallas_call | solution.py:433
  12.6 0.0 collective-permute-done.5.refs_4_.refs_6_
  12.6 0.5 %collective-permute-done.4.refs_3_.refs_5_ = bf16[64,128]{1,0:T(8,128)(2,1)S(1)} collective-permute-done((bf16[64,128]{1,0:T(8,128)(2,1)S(1)}, bf16[64,128]{1,0:T(8,128)(2,1)S(1)}, u32[]{:S(2)}, u32[]{:S(2)}) %collective-permute-start.4) | collective-permute-done | bytes 16416 | tf_op jit(solution)/shard_map/ppermute | solution.py:70
  13.1 0.0 collective-permute-done.3.refs_2_.refs_4_
  13.1 0.3 %half.1 = (bf16[32,256]{1,0:T(8,128)(2,1)S(1)}, bf16[32,256]{1,0:T(8,128)(2,1)S(1)}) custom-call(f32[16,256]{1,0:T(8,128)S(1)} %get-tuple-element.22.masks.refs_7_, bf16[1024,256]{1,0:T(8,128)(2,1)S(1)} %get-tuple-element.23.weights.refs_8_, bf16[32,128]{1,0:T(8,128)(2,1)S(1)} %get-tuple-element.24.refs_0_.refs_2_, ...), custom_call_target="tpu_custom_call" | custom-call | bytes 1048576 | tf_op jit(solution)/shard_map/half/pallas_call | solution.py:433
  13.3 0.4 %collective-permute-start.6 = (bf16[32,256]{1,0:T(8,128)(2,1)S(1)}, bf16[32,256]{1,0:T(8,128)(2,1)S(1)}, u32[]{:S(2)}, u32[]{:S(2)}) collective-permute-start(bf16[32,256]{1,0:T(8,128)(2,1)S(1)} %get-tuple-element.27), channel_id=1, source_target_pairs={{0,1},{1,0},{2,3},{3,2},{4,5},{5,4},{6,7},{7,6},{8,9},{9,8},{10,11... | collective-permute-start | bytes 49160 | tf_op jit(solution)/shard_map/ppermute | solution.py:70
  13.8 0.7 %near_field.3.refs_1_ = f32[32,1280]{1,0:T(8,128)S(1)} custom-call(bf16[192,128]{1,0:T(8,128)(2,1)S(1)} %collective-permute-done.1.facing, bf16[192,128]{1,0:T(8,128)(2,1)S(1)} %collective-permute-done.away, bf16[32,2048]{1,0:T(8,128)(2,1)S(1)} %get-tuple-element.25.x, bf16[8,3,256,256]{3,2,1,0:T(8,128)(2,1)S(1)} %copy-done), custom_call_target="tpu_custom_call" | custom-call | flops 62914560 | bytes 1048576 | tf_op jit(solution)/shard_map/near_field/pallas_call | solution.py:433
  14.5 0.1 collective-permute-done.6.theirs
  14.6 1.1 %leaves.1 = bf16[32,2048]{1,0:T(8,128)(2,1)} custom-call(bf16[32,256]{1,0:T(8,128)(2,1)S(1)} %get-tuple-element.26.mine, bf16[32,256]{1,0:T(8,128)(2,1)S(1)} %collective-permute-done.6.theirs, f32[32,512]{1,0:T(8,128)S(1)} %get-tuple-element.28.state, bf16[320,512]{1,0:T(8,128)(2,1)S(1)} %get-tuple-element.29.spread, ...), custom_call_target="tpu_custom_call" | custom-call | bytes 1048576 | tf_op jit(solution)/shard_map/leaves/pallas_call | solution.py:433
  (2 shorter events, 0.0 us)
Async XLA Ops:
  0.0 10.2 %copy-start.1 = (bf16[12,2,64,64]{3,2,1,0:T(8,128)(2,1)S(1)}, bf16[12,2,64,64]{3,2,1,0:T(8,128)(2,1)}, u32[]{:S(2)}) copy-start(bf16[12,2,64,64]{3,2,1,0:T(8,128)(2,1)} %refs_9_.1) | copy-start | bytes 589828
  0.0 10.2 %copy-start.3 = (s32[12,3,128]{2,1,0:T(4,128)S(1)}, s32[12,3,128]{2,1,0:T(4,128)}, u32[]{:S(2)}) copy-start(s32[12,3,128]{2,1,0:T(4,128)} %codes.1) | copy-start | bytes 55300
  0.0 10.2 %copy-start.2 = (bf16[12,4,64,64]{3,2,1,0:T(8,128)(2,1)S(1)}, bf16[12,4,64,64]{3,2,1,0:T(8,128)(2,1)}, u32[]{:S(2)}) copy-start(bf16[12,4,64,64]{3,2,1,0:T(8,128)(2,1)} %couple.1) | copy-start | bytes 1179652
  1.7 10.4 %copy-start = (bf16[8,3,256,256]{3,2,1,0:T(8,128)(2,1)S(1)}, bf16[8,3,256,256]{3,2,1,0:T(8,128)(2,1)}, u32[]{:S(2)}) copy-start(bf16[8,3,256,256]{3,2,1,0:T(8,128)(2,1)} %blocks.3) | copy-start | bytes 9437188
  1.7 5.2 %collective-permute-start.2 = (bf16[32,128]{1,0:T(8,128)(2,1)S(1)}, bf16[32,128]{1,0:T(8,128)(2,1)S(1)}, u32[]{:S(2)}, u32[]{:S(2)}) collective-permute-start(bf16[32,128]{1,0:T(8,128)(2,1)S(1)} %get-tuple-element.24.refs_0_.refs_2_), channel_id=1, source_target_pairs={{0,9},{1,8},{2,11},{3,10},{4,13},{5,12},{6,15},{7,14},{8,1},{9,0},... | collective-permute-start | bytes 24584 | tf_op jit(solution)/shard_map/ppermute | solution.py:70
  5.3 4.9 %collective-permute-start = (bf16[192,128]{1,0:T(8,128)(2,1)S(1)}, bf16[192,128]{1,0:T(8,128)(2,1)S(1)}, u32[]{:S(2)}, u32[]{:S(2)}) collective-permute-start(bf16[192,128]{1,0:T(8,128)(2,1)S(1)} %get-tuple-element.18), channel_id=1, source_target_pairs={{0,16},{1,2},{2,1},{3,4},{4,3},{5,6},{6,5},{7,8},{8,7},{9,10},{10,... | collective-permute-start | bytes 147464 | tf_op jit(solution)/shard_map/ppermute | solution.py:81
  6.8 3.4 %collective-permute-start.1 = (bf16[192,128]{1,0:T(8,128)(2,1)S(1)}, bf16[192,128]{1,0:T(8,128)(2,1)S(1)}, u32[]{:S(2)}, u32[]{:S(2)}) collective-permute-start(bf16[192,128]{1,0:T(8,128)(2,1)S(1)} %get-tuple-element.19), channel_id=1, source_target_pairs={{0,1},{1,0},{2,3},{3,2},{4,5},{5,4},{6,7},{7,6},{8,9},{9,8},{10,11... | collective-permute-start | bytes 147464 | tf_op jit(solution)/shard_map/ppermute | solution.py:70
  6.9 5.7 %collective-permute-start.5 = (bf16[64,128]{1,0:T(8,128)(2,1)S(1)}, bf16[64,128]{1,0:T(8,128)(2,1)S(1)}, u32[]{:S(2)}, u32[]{:S(2)}) collective-permute-start(bf16[64,128]{1,0:T(8,128)(2,1)S(1)} %constant_dynamic-update-slice_fusion), channel_id=1, source_target_pairs={{0,6},{1,7},{2,4},{3,5},{4,2},{5,3},{6,0},{7,1},{8,14},{9,15},{10,... | collective-permute-start | bytes 49160 | tf_op jit(solution)/shard_map/ppermute | solution.py:70
  9.7 3.3 %collective-permute-start.4 = (bf16[64,128]{1,0:T(8,128)(2,1)S(1)}, bf16[64,128]{1,0:T(8,128)(2,1)S(1)}, u32[]{:S(2)}, u32[]{:S(2)}) collective-permute-start(bf16[64,128]{1,0:T(8,128)(2,1)S(1)} %constant_dynamic-update-slice_fusion), channel_id=1, source_target_pairs={{0,5},{1,4},{2,7},{3,6},{4,1},{5,0},{6,3},{7,2},{8,13},{9,12},{10,... | collective-permute-start | bytes 49160 | tf_op jit(solution)/shard_map/ppermute | solution.py:70
  9.7 3.3 %collective-permute-start.3 = (bf16[64,128]{1,0:T(8,128)(2,1)S(1)}, bf16[64,128]{1,0:T(8,128)(2,1)S(1)}, u32[]{:S(2)}, u32[]{:S(2)}) collective-permute-start(bf16[64,128]{1,0:T(8,128)(2,1)S(1)} %constant_dynamic-update-slice_fusion), channel_id=1, source_target_pairs={{0,3},{1,2},{2,1},{3,0},{4,7},{5,6},{6,5},{7,4},{8,11},{9,10},{10,... | collective-permute-start | bytes 49160 | tf_op jit(solution)/shard_map/ppermute | solution.py:70
  13.3 1.3 %collective-permute-start.6 = (bf16[32,256]{1,0:T(8,128)(2,1)S(1)}, bf16[32,256]{1,0:T(8,128)(2,1)S(1)}, u32[]{:S(2)}, u32[]{:S(2)}) collective-permute-start(bf16[32,256]{1,0:T(8,128)(2,1)S(1)} %get-tuple-element.27), channel_id=1, source_target_pairs={{0,1},{1,0},{2,3},{3,2},{4,5},{5,4},{6,7},{7,6},{8,9},{9,8},{10,11... | collective-permute-start | bytes 49160 | tf_op jit(solution)/shard_map/ppermute | solution.py:70

commit v9 on v8

--- a/solution.py
+++ b/solution.py
@@ -13,7 +13,7 @@
 BF = jnp.bfloat16
 F32 = jnp.float32
 LANES = 64
-SHARE = 3
+SHARE = 4
 
 
 def mm(a, b):

time: 15.9 us -> 15.9 us (level)
  no operation moved by 1% of the time
where the time goes in v9:
time: 15.9 us; the launch traced here: 15.8 us
  starting transfers between devices  8.87 us (56%)
  Pallas kernels  6.1 us (38%)
  waiting for transfers between devices  0.69 us (4%)
    ppermute x6, starting transfers between devices, exchanged(): return lax.ppermute(x, AXES, [(i, i ^ apart) for i in range(devices)])  7.34 us
    pallas_call x6, Pallas kernels, call(): pl.pallas_call(kernel, out_shape=shapes if single else list(shapes), comp...  6.1 us
    ppermute x1, starting transfers between devices, across_pairs(): return lax.ppermute(x, ('groups', *AXES), pairs)  1.52 us
    ppermute x6, waiting for transfers between devices, exchanged(): return lax.ppermute(x, AXES, [(i, i ^ apart) for i in range(devices)])  0.68 us
  transfers between devices with their start and end apart: 7, of which 2 were waited for; matrix products, arithmetic and copies ran while one was open for 0% of the time, Pallas kernels for 19%

profile of v9, /device:TPU:0, one launch (start us, length us, event | category | flops | bytes accessed | tf_op | source)
XLA Modules:
  0.0 15.8 jit_solution(10601193709655861033)
XLA Ops:
  0.0 0.0 copy-start.1
  0.0 0.0 copy-start.3
  0.0 0.0 copy-start.2
  0.0 1.7 %first.1 = (bf16[32,2048]{1,0:T(8,128)(2,1)S(1)}, bf16[8,64,256]{2,1,0:T(8,128)(2,1)S(1)}, bf16[192,128]{1,0:T(8,128)(2,1)S(1)}, bf16[192,128]{1,0:T(8,128)(2,1)...) custom-call(bf16[32,2048]{1,0:T(8,128)(2,1)} %rhs_hbm.1, ...), custom_call_target="tpu_custom_call" | custom-call | flops 4294967296 | bytes 1048576 | tf_op jit(solution)/shard_map/first/pallas_call | solution.py:433
  1.7 0.0 copy-start
  1.7 3.5 %collective-permute-start.2 = (bf16[32,128]{1,0:T(8,128)(2,1)S(1)}, bf16[32,128]{1,0:T(8,128)(2,1)S(1)}, u32[]{:S(2)}, u32[]{:S(2)}) collective-permute-start(bf16[32,128]{1,0:T(8,128)(2,1)S(1)} %get-tuple-element.24.refs_0_.refs_2_), channel_id=1, source_target_pairs={{0,9},{1,8},{2,11},{3,10},{4,13},{5,12},{6,15},{7,14},{8,1},{9,0},... | collective-permute-start | bytes 24584 | tf_op jit(solution)/shard_map/ppermute | solution.py:70
  5.3 1.5 %collective-permute-start = (bf16[192,128]{1,0:T(8,128)(2,1)S(1)}, bf16[192,128]{1,0:T(8,128)(2,1)S(1)}, u32[]{:S(2)}, u32[]{:S(2)}) collective-permute-start(bf16[192,128]{1,0:T(8,128)(2,1)S(1)} %get-tuple-element.18), channel_id=1, source_target_pairs={{0,16},{1,2},{2,1},{3,4},{4,3},{5,6},{6,5},{7,8},{8,7},{9,10},{10,... | collective-permute-start | bytes 147464 | tf_op jit(solution)/shard_map/ppermute | solution.py:81
  6.8 0.1 collective-permute-start.1
  6.9 0.0 collective-permute-done.2.refs_1_.refs_3_
  6.9 2.8 %collective-permute-start.5 = (bf16[64,128]{1,0:T(8,128)(2,1)S(1)}, bf16[64,128]{1,0:T(8,128)(2,1)S(1)}, u32[]{:S(2)}, u32[]{:S(2)}) collective-permute-start(bf16[64,128]{1,0:T(8,128)(2,1)S(1)} %constant_dynamic-update-slice_fusion), channel_id=1, source_target_pairs={{0,6},{1,7},{2,4},{3,5},{4,2},{5,3},{6,0},{7,1},{8,14},{9,15},{10,... | collective-permute-start | bytes 49160 | tf_op jit(solution)/shard_map/ppermute | solution.py:70
  9.7 0.0 collective-permute-start.4
  9.7 0.4 %collective-permute-start.3 = (bf16[64,128]{1,0:T(8,128)(2,1)S(1)}, bf16[64,128]{1,0:T(8,128)(2,1)S(1)}, u32[]{:S(2)}, u32[]{:S(2)}) collective-permute-start(bf16[64,128]{1,0:T(8,128)(2,1)S(1)} %constant_dynamic-update-slice_fusion), channel_id=1, source_target_pairs={{0,3},{1,2},{2,1},{3,0},{4,7},{5,6},{6,5},{7,4},{8,11},{9,10},{10,... | collective-permute-start | bytes 49160 | tf_op jit(solution)/shard_map/ppermute | solution.py:70
  10.2 0.0 collective-permute-done.away
  10.2 0.0 collective-permute-done.1.facing
  10.2 0.0 copy-done.1
  10.2 0.0 copy-done.3
  10.2 0.0 copy-done.2
  10.2 1.9 %plan.1 = (f32[32,512]{1,0:T(8,128)S(1)}, bf16[320,512]{1,0:T(8,128)(2,1)S(1)}, f32[16,256]{1,0:T(8,128)S(1)}, bf16[1024,256]{1,0:T(8,128)(2,1)S(1)}) custom-call(bf16[192,128]{1,0:T(8,128)(2,1)S(1)} %collective-permute-done.away, bf16[192,128]{1,0:T(8,128)(2,1)S(1)} %collective-permute-done.1.facing, bf16[128,128]{1,0:T(8,128)(2,1)S(1)} %get-tuple-element.20.own0, ...), custom_call_target="tpu_custom_call" | custom-call | flops 1073741824 | bytes 1048576 | tf_op jit(solution)/shard_map/plan/pallas_call | solution.py:433
  12.1 0.0 copy-done
  12.1 0.5 %near_field.2.refs_5_.refs_0_ = f32[32,1024]{1,0:T(8,128)S(1)} custom-call(bf16[192,128]{1,0:T(8,128)(2,1)S(1)} %collective-permute-done.1.facing, bf16[192,128]{1,0:T(8,128)(2,1)S(1)} %collective-permute-done.away, bf16[32,2048]{1,0:T(8,128)(2,1)S(1)} %get-tuple-element.25.x, bf16[8,3,256,256]{3,2,1,0:T(8,128)(2,1)S(1)} %copy-done), custom_call_target="tpu_custom_call" | custom-call | flops 50331648 | bytes 1048576 | tf_op jit(solution)/shard_map/near_field/pallas_call | solution.py:433
  12.7 0.0 collective-permute-done.5.refs_4_.refs_6_
  12.7 0.4 %collective-permute-done.4.refs_3_.refs_5_ = bf16[64,128]{1,0:T(8,128)(2,1)S(1)} collective-permute-done((bf16[64,128]{1,0:T(8,128)(2,1)S(1)}, bf16[64,128]{1,0:T(8,128)(2,1)S(1)}, u32[]{:S(2)}, u32[]{:S(2)}) %collective-permute-start.4) | collective-permute-done | bytes 16416 | tf_op jit(solution)/shard_map/ppermute | solution.py:70
  13.1 0.0 collective-permute-done.3.refs_2_.refs_4_
  13.1 0.3 %half.1 = (bf16[32,256]{1,0:T(8,128)(2,1)S(1)}, bf16[32,256]{1,0:T(8,128)(2,1)S(1)}) custom-call(f32[16,256]{1,0:T(8,128)S(1)} %get-tuple-element.22.masks.refs_7_, bf16[1024,256]{1,0:T(8,128)(2,1)S(1)} %get-tuple-element.23.weights.refs_8_, bf16[32,128]{1,0:T(8,128)(2,1)S(1)} %get-tuple-element.24.refs_0_.refs_2_, ...), custom_call_target="tpu_custom_call" | custom-call | bytes 1048576 | tf_op jit(solution)/shard_map/half/pallas_call | solution.py:433
  13.3 0.4 %collective-permute-start.6 = (bf16[32,256]{1,0:T(8,128)(2,1)S(1)}, bf16[32,256]{1,0:T(8,128)(2,1)S(1)}, u32[]{:S(2)}, u32[]{:S(2)}) collective-permute-start(bf16[32,256]{1,0:T(8,128)(2,1)S(1)} %get-tuple-element.27), channel_id=1, source_target_pairs={{0,1},{1,0},{2,3},{3,2},{4,5},{5,4},{6,7},{7,6},{8,9},{9,8},{10,11... | collective-permute-start | bytes 49160 | tf_op jit(solution)/shard_map/ppermute | solution.py:70
  13.8 0.5 %near_field.3.refs_1_ = f32[32,1024]{1,0:T(8,128)S(1)} custom-call(bf16[192,128]{1,0:T(8,128)(2,1)S(1)} %collective-permute-done.1.facing, bf16[192,128]{1,0:T(8,128)(2,1)S(1)} %collective-permute-done.away, bf16[32,2048]{1,0:T(8,128)(2,1)S(1)} %get-tuple-element.25.x, bf16[8,3,256,256]{3,2,1,0:T(8,128)(2,1)S(1)} %copy-done), custom_call_target="tpu_custom_call" | custom-call | flops 50331648 | bytes 1048576 | tf_op jit(solution)/shard_map/near_field/pallas_call | solution.py:433
  14.3 0.3 %collective-permute-done.6.theirs = bf16[32,256]{1,0:T(8,128)(2,1)S(1)} collective-permute-done((bf16[32,256]{1,0:T(8,128)(2,1)S(1)}, bf16[32,256]{1,0:T(8,128)(2,1)S(1)}, u32[]{:S(2)}, u32[]{:S(2)}) %collective-permute-start.6) | collective-permute-done | bytes 16416 | tf_op jit(solution)/shard_map/ppermute | solution.py:70
  14.6 1.1 %leaves.1 = bf16[32,2048]{1,0:T(8,128)(2,1)} custom-call(bf16[32,256]{1,0:T(8,128)(2,1)S(1)} %get-tuple-element.26.mine, bf16[32,256]{1,0:T(8,128)(2,1)S(1)} %collective-permute-done.6.theirs, f32[32,512]{1,0:T(8,128)S(1)} %get-tuple-element.28.state, bf16[320,512]{1,0:T(8,128)(2,1)S(1)} %get-tuple-element.29.spread, ...), custom_call_target="tpu_custom_call" | custom-call | bytes 1048576 | tf_op jit(solution)/shard_map/leaves/pallas_call | solution.py:433
  (2 shorter events, 0.0 us)
Async XLA Ops:
  0.0 10.2 %copy-start.1 = (bf16[12,2,64,64]{3,2,1,0:T(8,128)(2,1)S(1)}, bf16[12,2,64,64]{3,2,1,0:T(8,128)(2,1)}, u32[]{:S(2)}) copy-start(bf16[12,2,64,64]{3,2,1,0:T(8,128)(2,1)} %refs_9_.1) | copy-start | bytes 589828
  0.0 10.2 %copy-start.3 = (s32[12,3,128]{2,1,0:T(4,128)S(1)}, s32[12,3,128]{2,1,0:T(4,128)}, u32[]{:S(2)}) copy-start(s32[12,3,128]{2,1,0:T(4,128)} %codes.1) | copy-start | bytes 55300
  0.0 10.2 %copy-start.2 = (bf16[12,4,64,64]{3,2,1,0:T(8,128)(2,1)S(1)}, bf16[12,4,64,64]{3,2,1,0:T(8,128)(2,1)}, u32[]{:S(2)}) copy-start(bf16[12,4,64,64]{3,2,1,0:T(8,128)(2,1)} %couple.1) | copy-start | bytes 1179652
  1.7 10.4 %copy-start = (bf16[8,3,256,256]{3,2,1,0:T(8,128)(2,1)S(1)}, bf16[8,3,256,256]{3,2,1,0:T(8,128)(2,1)}, u32[]{:S(2)}) copy-start(bf16[8,3,256,256]{3,2,1,0:T(8,128)(2,1)} %blocks.3) | copy-start | bytes 9437188
  1.7 5.2 %collective-permute-start.2 = (bf16[32,128]{1,0:T(8,128)(2,1)S(1)}, bf16[32,128]{1,0:T(8,128)(2,1)S(1)}, u32[]{:S(2)}, u32[]{:S(2)}) collective-permute-start(bf16[32,128]{1,0:T(8,128)(2,1)S(1)} %get-tuple-element.24.refs_0_.refs_2_), channel_id=1, source_target_pairs={{0,9},{1,8},{2,11},{3,10},{4,13},{5,12},{6,15},{7,14},{8,1},{9,0},... | collective-permute-start | bytes 24584 | tf_op jit(solution)/shard_map/ppermute | solution.py:70
  5.3 4.9 %collective-permute-start = (bf16[192,128]{1,0:T(8,128)(2,1)S(1)}, bf16[192,128]{1,0:T(8,128)(2,1)S(1)}, u32[]{:S(2)}, u32[]{:S(2)}) collective-permute-start(bf16[192,128]{1,0:T(8,128)(2,1)S(1)} %get-tuple-element.18), channel_id=1, source_target_pairs={{0,16},{1,2},{2,1},{3,4},{4,3},{5,6},{6,5},{7,8},{8,7},{9,10},{10,... | collective-permute-start | bytes 147464 | tf_op jit(solution)/shard_map/ppermute | solution.py:81
  6.8 3.4 %collective-permute-start.1 = (bf16[192,128]{1,0:T(8,128)(2,1)S(1)}, bf16[192,128]{1,0:T(8,128)(2,1)S(1)}, u32[]{:S(2)}, u32[]{:S(2)}) collective-permute-start(bf16[192,128]{1,0:T(8,128)(2,1)S(1)} %get-tuple-element.19), channel_id=1, source_target_pairs={{0,1},{1,0},{2,3},{3,2},{4,5},{5,4},{6,7},{7,6},{8,9},{9,8},{10,11... | collective-permute-start | bytes 147464 | tf_op jit(solution)/shard_map/ppermute | solution.py:70
  6.9 5.8 %collective-permute-start.5 = (bf16[64,128]{1,0:T(8,128)(2,1)S(1)}, bf16[64,128]{1,0:T(8,128)(2,1)S(1)}, u32[]{:S(2)}, u32[]{:S(2)}) collective-permute-start(bf16[64,128]{1,0:T(8,128)(2,1)S(1)} %constant_dynamic-update-slice_fusion), channel_id=1, source_target_pairs={{0,6},{1,7},{2,4},{3,5},{4,2},{5,3},{6,0},{7,1},{8,14},{9,15},{10,... | collective-permute-start | bytes 49160 | tf_op jit(solution)/shard_map/ppermute | solution.py:70
  9.7 3.3 %collective-permute-start.4 = (bf16[64,128]{1,0:T(8,128)(2,1)S(1)}, bf16[64,128]{1,0:T(8,128)(2,1)S(1)}, u32[]{:S(2)}, u32[]{:S(2)}) collective-permute-start(bf16[64,128]{1,0:T(8,128)(2,1)S(1)} %constant_dynamic-update-slice_fusion), channel_id=1, source_target_pairs={{0,5},{1,4},{2,7},{3,6},{4,1},{5,0},{6,3},{7,2},{8,13},{9,12},{10,... | collective-permute-start | bytes 49160 | tf_op jit(solution)/shard_map/ppermute | solution.py:70
  9.7 3.3 %collective-permute-start.3 = (bf16[64,128]{1,0:T(8,128)(2,1)S(1)}, bf16[64,128]{1,0:T(8,128)(2,1)S(1)}, u32[]{:S(2)}, u32[]{:S(2)}) collective-permute-start(bf16[64,128]{1,0:T(8,128)(2,1)S(1)} %constant_dynamic-update-slice_fusion), channel_id=1, source_target_pairs={{0,3},{1,2},{2,1},{3,0},{4,7},{5,6},{6,5},{7,4},{8,11},{9,10},{10,... | collective-permute-start | bytes 49160 | tf_op jit(solution)/shard_map/ppermute | solution.py:70
  13.3 1.3 %collective-permute-start.6 = (bf16[32,256]{1,0:T(8,128)(2,1)S(1)}, bf16[32,256]{1,0:T(8,128)(2,1)S(1)}, u32[]{:S(2)}, u32[]{:S(2)}) collective-permute-start(bf16[32,256]{1,0:T(8,128)(2,1)S(1)} %get-tuple-element.27), channel_id=1, source_target_pairs={{0,1},{1,0},{2,3},{3,2},{4,5},{5,4},{6,7},{7,6},{8,9},{9,8},{10,11... | collective-permute-start | bytes 49160 | tf_op jit(solution)/shard_map/ppermute | solution.py:70
